TPU v7x, 32 devices: a whole 2x2x4 slice. The times are simulated.
32 devices in a mesh: fsdp: 2 (over x), ctx: 8 (over z, core), tp: 2 (over y).
Axes of the slice: x: 2, y: 2, z: 4, core: 2. Of those that a mesh axis runs over, the one named last changes fastest.
Arguments:
- tokens: bfloat16 [2, 1024, 2048], P('fsdp', 'ctx'), may hold values from -6 to 6
- w_query: bfloat16 [2048, 8, 256], P(('fsdp', 'ctx'), 'tp'), may hold values from -0.125 to 0.125
- w_key: bfloat16 [2048, 8, 256], P(('fsdp', 'ctx'), 'tp'), may hold values from -0.125 to 0.125
- w_value: bfloat16 [2048, 8, 512], P(('fsdp', 'ctx'), 'tp'), may hold values from -0.125 to 0.125
- w_swish: bfloat16 [2048, 8, 512], P(('fsdp', 'ctx'), 'tp'), may hold values from -0.125 to 0.125
- w_output: bfloat16 [2048, 8, 512], P(('fsdp', 'ctx'), 'tp'), may hold values from -0.1875 to 0.1875
- w_gelu: bfloat16 [2048, 4096], P(('fsdp', 'ctx'), 'tp'), may hold values from -0.125 to 0.125
- w_up: bfloat16 [2048, 4096], P(('fsdp', 'ctx'), 'tp'), may hold values from -0.125 to 0.125
- w_down: bfloat16 [2048, 4096], P(('fsdp', 'ctx'), 'tp'), may hold values from -0.125 to 0.125
- gain_first: bfloat16 [2048], P(('fsdp', 'ctx')), may hold values from 0.25 to 1.75
- gain_second: bfloat16 [2048], P(('fsdp', 'ctx')), may hold values from 0.25 to 1.75
- gain_group: bfloat16 [8, 512], P('tp', ('fsdp', 'ctx')), may hold values from 0.25 to 1.75
- decay_rate: float32 [8], P('tp'), may hold values from 0.9 to 1, as said below
- cotangent: bfloat16 [2, 1024, 2048], P('fsdp', 'ctx'), may hold values from -6 to 6
Outputs:
- result: float32 [2, 1024, 2048], P('fsdp', 'ctx')
- grad_tokens: float32 [2, 1024, 2048], P('fsdp', 'ctx')
- grad_query: float32 [2048, 8, 256], P(('fsdp', 'ctx'), 'tp')
- grad_key: float32 [2048, 8, 256], P(('fsdp', 'ctx'), 'tp')
- grad_value: float32 [2048, 8, 512], P(('fsdp', 'ctx'), 'tp')
- grad_swish: float32 [2048, 8, 512], P(('fsdp', 'ctx'), 'tp')
- grad_output: float32 [2048, 8, 512], P(('fsdp', 'ctx'), 'tp')
- grad_gelu: float32 [2048, 4096], P(('fsdp', 'ctx'), 'tp')
- grad_up: float32 [2048, 4096], P(('fsdp', 'ctx'), 'tp')
- grad_down: float32 [2048, 4096], P(('fsdp', 'ctx'), 'tp')
- grad_first: float32 [2048], P(('fsdp', 'ctx'))
- grad_second: float32 [2048], P(('fsdp', 'ctx'))
- grad_group: float32 [8, 512], P('tp', ('fsdp', 'ctx'))
Inputs may be any that keep to these rules, and one draw needn't show every extreme that they name: `decay_rate`: each head's decay factor lies strictly between 0 and 1.
All inputs are finite; a program needn't handle non-finite values.
Results may differ from a plain program's by a relative error of at most 0.014.
Values may be sent and summed in bfloat16 or wider, within the bound.
A program may use at most 184 MiB of HBM per device.

v0:
```python
import jax
import jax.numpy as jnp
from jax import lax
from jax.sharding import PartitionSpec as P

highest_precision = lax.Precision.HIGHEST


def prefix(part, axis, combine, identity):
    place = lax.axis_index(axis)
    gathered = jax.tree.map(lambda a: lax.all_gather(a, axis), part)
    state = jax.tree.map(lambda a, e: jnp.zeros_like(a) + jnp.asarray(e, a.dtype), part, identity)

    def one(turn, state):
        return combine(
            state, jax.tree.map(lambda a: lax.dynamic_index_in_dim(a, turn, 0, False), gathered)
        )

    return lax.fori_loop(0, place, one, state)


def entering_2(value, axis, combine, identity):
    devices, mine = (lax.axis_size(axis), lax.axis_index(axis))
    everything = jax.tree.map(
        lambda part, kind: lax.all_gather(part.astype(kind), axis),
        value,
        jax.tree.map(lambda a: jnp.bfloat16 if a.dtype == jnp.float32 else a.dtype, value),
    )
    start = jax.tree.map(
        lambda part, zero: jnp.broadcast_to(jnp.asarray(zero, part.dtype), part.shape),
        value,
        identity,
    )

    def turn(k, before):
        at = devices - 1 - k
        reached = at > mine
        new = combine(
            before, jax.tree.map(lambda part, own: part[at].astype(own.dtype), everything, value)
        )
        return jax.tree.map(lambda a, b: jnp.where(reached, a, b), new, before)

    return lax.fori_loop(0, devices, turn, start)


def norm_rows(values, gain):
    center = values - jnp.mean(values, axis=-1, keepdims=True)
    spread = jnp.mean(center * center, axis=-1, keepdims=True)
    return center * lax.rsqrt(spread + 1e-05) * gain


def entry_weights(length, log_rate):
    position = jnp.arange(length).astype(jnp.float32)
    return jnp.exp((position[:, None] + 1.0) * log_rate[None, :])


def exit_weights(length, log_rate):
    position = jnp.arange(length).astype(jnp.float32)
    return jnp.exp((length - 1.0 - position)[:, None] * log_rate[None, :])


def decay_matrix(length, log_rate):
    position = jnp.arange(length).astype(jnp.float32)
    distance = position[:, None] - position[None, :]
    causal = distance >= 0.0
    return jnp.where(
        causal[None], jnp.exp(jnp.where(causal, distance, 0.0)[None] * log_rate[:, None, None]), 0.0
    )


def retain_out(query_block, key_block_rows, value_block_rows, retention_state, log_rate):
    length = query_block.shape[1]
    scores = (
        jnp.einsum("sthk,sqhk->shtq", query_block, key_block_rows, precision=highest_precision)
        * decay_matrix(length, log_rate)[None]
    )
    within = jnp.einsum("shtq,sqhv->sthv", scores, value_block_rows, precision=highest_precision)
    carried_state = jnp.einsum(
        "sthk,shkv->sthv",
        query_block * entry_weights(length, log_rate)[None, :, :, None],
        retention_state,
        precision=highest_precision,
    )
    return within + carried_state


def retain_low(query_low, key_low, query_wide, value_wide, retention_state, log_rate):
    length = query_low.shape[1]
    raw_scores = jnp.einsum(
        "sthk,sqhk->shtq", query_low, key_low, preferred_element_type=jnp.float32
    )
    scores = raw_scores * decay_matrix(length, log_rate)[None]
    within = jnp.einsum("shtq,sqhv->sthv", scores, value_wide, precision=highest_precision)
    carried_state = jnp.einsum(
        "sthk,shkv->sthv",
        query_wide * entry_weights(length, log_rate)[None, :, :, None],
        retention_state,
        precision=highest_precision,
    )
    return within + carried_state


def own_states(key_block_rows, value_block_rows, log_rate):
    length = key_block_rows.shape[1]
    return jnp.einsum(
        "sthk,sthv->shkv",
        key_block_rows * exit_weights(length, log_rate)[None, :, :, None],
        value_block_rows,
        precision=highest_precision,
    )


def combine_states(earlier, later):
    return (earlier[0] * later[0], later[0][None, :, None, None] * earlier[1] + later[1])


def gate_section(retained, swish_in, gain):
    return norm_rows(retained, gain) * jax.nn.silu(swish_in)


def mlp_section(act_gelu, act_up):
    return jax.nn.gelu(act_gelu) * act_up


def local(
    tokens,
    w_query,
    w_key,
    w_value,
    w_swish,
    w_output,
    w_gelu,
    w_up,
    w_down,
    gain_first,
    gain_second,
    gain_group,
    decay_rate,
    cotangent,
):
    f32 = jnp.float32
    bf16 = jnp.bfloat16
    gathered = (
        lax.all_gather(w_query, ("fsdp", "ctx"), axis=0, tiled=True),
        lax.all_gather(w_key, ("fsdp", "ctx"), axis=0, tiled=True),
        lax.all_gather(w_value, ("fsdp", "ctx"), axis=0, tiled=True),
        lax.all_gather(w_swish, ("fsdp", "ctx"), axis=0, tiled=True),
        lax.all_gather(w_output, ("fsdp", "ctx"), axis=0, tiled=True),
        lax.all_gather(w_gelu, ("fsdp", "ctx"), axis=0, tiled=True),
        lax.all_gather(w_up, ("fsdp", "ctx"), axis=0, tiled=True),
        lax.all_gather(w_down, ("fsdp", "ctx"), axis=0, tiled=True),
        lax.all_gather(gain_first, ("fsdp", "ctx"), axis=0, tiled=True),
        lax.all_gather(gain_second, ("fsdp", "ctx"), axis=0, tiled=True),
        lax.all_gather(gain_group, ("fsdp", "ctx"), axis=1, tiled=True),
    )
    (
        full_query,
        full_key,
        full_value,
        full_swish,
        full_output,
        full_gelu,
        full_up,
        full_down,
        full_first,
        full_second,
        full_group,
    ) = gathered
    log_rate = jnp.log(decay_rate)
    piece = tokens.shape[1]
    key_scale = full_query.shape[2] ** (-0.5)
    factor = jnp.exp(piece * log_rate)
    inputs = tokens.astype(f32)
    first_gain = full_first.astype(f32)
    second_gain = full_second.astype(f32)
    group_gain = full_group.astype(f32)
    first_low = norm_rows(inputs, first_gain).astype(bf16)
    query_block = jnp.einsum(
        "spd,dhk->sphk", first_low, full_query, preferred_element_type=f32
    ).astype(bf16)
    key_block_rows = (
        jnp.einsum("spd,dhk->sphk", first_low, full_key, preferred_element_type=f32) * key_scale
    ).astype(bf16)
    value_block_rows = jnp.einsum(
        "spd,dhv->sphv", first_low, full_value, preferred_element_type=f32
    ).astype(bf16)
    swish_in = jnp.einsum("spd,dhv->sphv", first_low, full_swish, preferred_element_type=f32)
    query_wide = query_block.astype(f32)
    key_wide = key_block_rows.astype(f32)
    value_wide = value_block_rows.astype(f32)
    local_state = own_states(key_wide, value_wide, log_rate)
    identity = (jnp.ones_like(factor), jnp.zeros_like(local_state))
    _, entering = prefix((factor, local_state), "ctx", combine_states, identity)
    retained = retain_low(query_block, key_block_rows, query_wide, value_wide, entering, log_rate)
    gated = gate_section(retained, swish_in, group_gain).astype(bf16)
    attn_terms = jnp.einsum("sphv,dhv->spd", gated, full_output, preferred_element_type=f32)
    hidden = inputs + lax.psum(attn_terms, "tp")
    second_low = norm_rows(hidden, second_gain).astype(bf16)
    act_gelu = jnp.einsum("spd,df->spf", second_low, full_gelu, preferred_element_type=f32)
    act_up = jnp.einsum("spd,df->spf", second_low, full_up, preferred_element_type=f32)
    mixed = mlp_section(act_gelu, act_up).astype(bf16)
    mlp_terms = jnp.einsum("spf,df->spd", mixed, full_down, preferred_element_type=f32)
    result = hidden + lax.psum(mlp_terms.astype(jnp.bfloat16), "tp").astype(jnp.float32)
    regathered = (
        lax.all_gather(w_query, ("fsdp", "ctx"), axis=0, tiled=True),
        lax.all_gather(w_key, ("fsdp", "ctx"), axis=0, tiled=True),
        lax.all_gather(w_value, ("fsdp", "ctx"), axis=0, tiled=True),
        lax.all_gather(w_swish, ("fsdp", "ctx"), axis=0, tiled=True),
        lax.all_gather(w_output, ("fsdp", "ctx"), axis=0, tiled=True),
        lax.all_gather(w_gelu, ("fsdp", "ctx"), axis=0, tiled=True),
        lax.all_gather(w_up, ("fsdp", "ctx"), axis=0, tiled=True),
        lax.all_gather(w_down, ("fsdp", "ctx"), axis=0, tiled=True),
        lax.all_gather(gain_first, ("fsdp", "ctx"), axis=0, tiled=True),
        lax.all_gather(gain_second, ("fsdp", "ctx"), axis=0, tiled=True),
        lax.all_gather(gain_group, ("fsdp", "ctx"), axis=1, tiled=True),
    )
    back_query, back_key, back_value, back_swish, back_output, back_gelu, back_up, back_down = (
        regathered[0],
        regathered[1],
        regathered[2],
        regathered[3],
        regathered[4],
        regathered[5],
        regathered[6],
        regathered[7],
    )
    grad_mixed = jnp.einsum("spd,df->spf", cotangent, back_down, preferred_element_type=f32)
    grad_down = jnp.einsum("spd,spf->df", cotangent, mixed, preferred_element_type=f32)
    _, pull_mlp = jax.vjp(mlp_section, act_gelu, act_up)
    grad_act_gelu, grad_act_up = pull_mlp(grad_mixed)
    gelu_low = grad_act_gelu.astype(bf16)
    up_low = grad_act_up.astype(bf16)
    grad_gelu = jnp.einsum("spd,spf->df", second_low, gelu_low, preferred_element_type=f32)
    grad_up = jnp.einsum("spd,spf->df", second_low, up_low, preferred_element_type=f32)
    second_terms = jnp.einsum(
        "spf,df->spd", gelu_low, back_gelu, preferred_element_type=f32
    ) + jnp.einsum("spf,df->spd", up_low, back_up, preferred_element_type=f32)
    grad_second_in = lax.psum(second_terms, "tp")
    _, pull_second = jax.vjp(norm_rows, hidden, second_gain)
    hidden_from_norm, grad_second = pull_second(grad_second_in)
    grad_hidden = cotangent.astype(f32) + hidden_from_norm
    hidden_low = grad_hidden.astype(bf16)
    grad_gated = jnp.einsum("spd,dhv->sphv", hidden_low, back_output, preferred_element_type=f32)
    grad_output = jnp.einsum("spd,sphv->dhv", hidden_low, gated, preferred_element_type=f32)
    _, pull_gate = jax.vjp(gate_section, retained, swish_in, group_gain)
    grad_retained, grad_swish_in, grad_group = pull_gate(grad_gated)
    swish_low = grad_swish_in.astype(bf16)
    entry_grad = jnp.einsum(
        "sthk,sthv->shkv",
        query_wide * entry_weights(piece, log_rate)[None, :, :, None],
        grad_retained,
        precision=highest_precision,
    )
    _, later_grad = entering_2((factor, entry_grad), "ctx", combine_states, identity)
    _, pull_retain = jax.vjp(
        lambda rows_q, rows_k, rows_v: (
            retain_out(rows_q, rows_k, rows_v, entering, log_rate),
            own_states(rows_k, rows_v, log_rate),
        ),
        query_wide,
        key_wide,
        value_wide,
    )
    grad_query_act, grad_key_act, grad_value_act = pull_retain((grad_retained, later_grad))
    query_low = grad_query_act.astype(bf16)
    key_low = (grad_key_act.astype(bf16).astype(f32) * key_scale).astype(bf16)
    value_low = grad_value_act.astype(bf16)
    grad_query = jnp.einsum("spd,sphk->dhk", first_low, query_low, preferred_element_type=f32)
    grad_key = jnp.einsum("spd,sphk->dhk", first_low, key_low, preferred_element_type=f32)
    grad_value = jnp.einsum("spd,sphv->dhv", first_low, value_low, preferred_element_type=f32)
    grad_swish = jnp.einsum("spd,sphv->dhv", first_low, swish_low, preferred_element_type=f32)
    first_terms = jnp.einsum("sphk,dhk->spd", query_low, back_query, preferred_element_type=f32)
    first_terms = first_terms + jnp.einsum(
        "sphk,dhk->spd", key_low, back_key, preferred_element_type=f32
    )
    first_terms = first_terms + jnp.einsum(
        "sphv,dhv->spd", value_low, back_value, preferred_element_type=f32
    )
    first_terms = first_terms + jnp.einsum(
        "sphv,dhv->spd", swish_low, back_swish, preferred_element_type=f32
    )
    grad_first_in = lax.psum(first_terms.astype(jnp.bfloat16), "tp").astype(jnp.float32)
    _, pull_first = jax.vjp(norm_rows, inputs, first_gain)
    tokens_from_norm, grad_first = pull_first(grad_first_in)
    grad_tokens = grad_hidden + tokens_from_norm
    owned = (
        lax.psum_scatter(grad_query, ("fsdp", "ctx"), scatter_dimension=0, tiled=True),
        lax.psum_scatter(grad_key, ("fsdp", "ctx"), scatter_dimension=0, tiled=True),
        lax.psum_scatter(grad_value, ("fsdp", "ctx"), scatter_dimension=0, tiled=True),
        lax.psum_scatter(grad_swish, ("fsdp", "ctx"), scatter_dimension=0, tiled=True),
        lax.psum_scatter(grad_output, ("fsdp", "ctx"), scatter_dimension=0, tiled=True),
        lax.psum_scatter(grad_gelu, ("fsdp", "ctx"), scatter_dimension=0, tiled=True),
        lax.psum_scatter(grad_up, ("fsdp", "ctx"), scatter_dimension=0, tiled=True),
        lax.psum_scatter(grad_down, ("fsdp", "ctx"), scatter_dimension=0, tiled=True),
        lax.psum_scatter(grad_first, ("fsdp", "ctx"), scatter_dimension=0, tiled=True),
        lax.psum_scatter(grad_second, ("fsdp", "ctx"), scatter_dimension=0, tiled=True),
        lax.psum_scatter(grad_group, ("fsdp", "ctx"), scatter_dimension=1, tiled=True),
    )
    return (
        result,
        grad_tokens,
        owned[0],
        owned[1],
        owned[2],
        owned[3],
        owned[4],
        owned[5],
        owned[6],
        owned[7],
        owned[8],
        owned[9],
        owned[10],
    )


def solution(mesh):
    in_specs = (
        P("fsdp", "ctx", None),
        P(("fsdp", "ctx"), "tp", None),
        P(("fsdp", "ctx"), "tp", None),
        P(("fsdp", "ctx"), "tp", None),
        P(("fsdp", "ctx"), "tp", None),
        P(("fsdp", "ctx"), "tp", None),
        P(("fsdp", "ctx"), "tp"),
        P(("fsdp", "ctx"), "tp"),
        P(("fsdp", "ctx"), "tp"),
        P(("fsdp", "ctx")),
        P(("fsdp", "ctx")),
        P("tp", ("fsdp", "ctx")),
        P("tp"),
        P("fsdp", "ctx", None),
    )
    out_specs = (
        P("fsdp", "ctx", None),
        P("fsdp", "ctx", None),
        P(("fsdp", "ctx"), "tp", None),
        P(("fsdp", "ctx"), "tp", None),
        P(("fsdp", "ctx"), "tp", None),
        P(("fsdp", "ctx"), "tp", None),
        P(("fsdp", "ctx"), "tp", None),
        P(("fsdp", "ctx"), "tp"),
        P(("fsdp", "ctx"), "tp"),
        P(("fsdp", "ctx"), "tp"),
        P(("fsdp", "ctx")),
        P(("fsdp", "ctx")),
        P("tp", ("fsdp", "ctx")),
    )
    return jax.shard_map(local, mesh=mesh, in_specs=in_specs, out_specs=out_specs, check_vma=False)
```

profile of v0, /device:TPU:0, one launch (start us, length us, event | category | flops | bytes accessed | tf_op | source)
XLA Modules:
  0.0 2348.8 jit_solution(9640736869900196026)
XLA Ops:
  14.8 23.2 all-gather.4
  43.9 20.3 all-gather.22.cloned.1.call-done
  64.2 3.1 fusion.43
  67.3 73.2 %all-gather.18.cloned.1.call-done = bf16[2048,4,512]{2,0,1:T(8,128)(2,1)} async-done(((bf16[128,4,512]{2,0,1:T(8,128)(2,1)}), bf16[2048,4,512]{2,0,1:T(8,128)(2,1)}) %all-gather.18.cloned.1.call-update) | async-done | bytes 8388624 | tf_op jit(solution)/shard_map/all_gather | solution.py:146
  140.5 4.7 convolution_convert_fusion.2
  145.2 2.5 fusion.90
  148.7 15.3 all-reduce
  164.1 17.4 all-gather.5
  181.7 10.6 all-gather.20.cloned.1.call-done
  192.4 2.9 convolution_convert_fusion.3
  197.0 71.5 %all-gather.24.cloned.1.call-done = bf16[2048,4,512]{2,0,1:T(8,128)(2,1)} async-done(((bf16[128,4,512]{2,0,1:T(8,128)(2,1)}), bf16[2048,4,512]{2,0,1:T(8,128)(2,1)}) %all-gather.24.cloned.1.call-update) | async-done | bytes 8388624 | tf_op jit(solution)/shard_map/all_gather | solution.py:147
  268.5 7.8 fusion.108
  276.3 143.1 %all-gather.34.cloned.1.call-done = f32[32,256,512]{2,1,0:T(8,128)} async-done(((f32[4,256,512]{2,1,0:T(8,128)}), f32[32,256,512]{2,1,0:T(8,128)}) %all-gather.34.cloned.1.call-update) | async-done | bytes 16777232 | tf_op jit(solution)/shard_map/all_gather | solution.py:11
  419.8 4.5 fusion.14
  428.6 66.5 %all-gather.26.cloned.1.call-done = bf16[2048,4,512]{2,0,1:T(8,128)(2,1)} async-done(((bf16[128,4,512]{2,0,1:T(8,128)(2,1)}), bf16[2048,4,512]{2,0,1:T(8,128)(2,1)}) %all-gather.26.cloned.1.call-update) | async-done | bytes 8388624 | tf_op jit(solution)/shard_map/all_gather | solution.py:148
  495.1 7.2 convolution_bitcast_fusion.3
  504.5 19.0 all-gather.6
  523.6 17.3 all-reduce.10.cloned.1.call-done
  543.4 74.8 %all-gather.28.cloned.1.call-done = bf16[2048,2048]{1,0:T(8,128)(2,1)} async-done(((bf16[128,2048]{1,0:T(8,128)(2,1)}), bf16[2048,2048]{1,0:T(8,128)(2,1)}) %all-gather.28.cloned.1.call-update) | async-done | bytes 8388624 | tf_op jit(solution)/shard_map/all_gather | solution.py:149
  618.2 5.6 fusion.117
  623.8 70.0 %all-gather.30.cloned.1.call-done = bf16[2048,2048]{1,0:T(8,128)(2,1)} async-done(((bf16[128,2048]{1,0:T(8,128)(2,1)}), bf16[2048,2048]{1,0:T(8,128)(2,1)}) %all-gather.30.cloned.1.call-update) | async-done | bytes 8388624 | tf_op jit(solution)/shard_map/all_gather | solution.py:150
  693.8 5.6 fusion.118
  699.4 69.9 %all-gather.32.cloned.1.call-done = bf16[2048,2048]{1,0:T(8,128)(2,1)} async-done(((bf16[128,2048]{1,0:T(8,128)(2,1)}), bf16[2048,2048]{1,0:T(8,128)(2,1)}) %all-gather.32.cloned.1.call-update) | async-done | bytes 8388624 | tf_op jit(solution)/shard_map/all_gather | solution.py:151
  769.3 7.0 multiply_convert_fusion
  777.1 7.0 fusion.119
  784.1 3.9 fusion.4
  788.3 38.2 %all-reduce.12.cloned.1.call-done = f32[1,128,2048]{2,1,0:T(8,128)} async-done(((f32[1,128,2048]{2,1,0:T(8,128)}), f32[1,128,2048]{2,1,0:T(8,128)}) %all-reduce.12.cloned.1.call-update) | async-done | bytes 1048592 | tf_op jit(solution)/shard_map/psum | solution.py:238
  832.8 8.6 fusion.62
  844.0 2.9 convolution_convert_fusion.1
  848.6 2.4 convolution_multiply_fusion.2
  851.0 3.3 fusion.35
  854.8 4.7 fusion.106
  860.2 17.1 all-reduce.1
  879.4 7.3 fusion.6
  886.6 7.3 convolution_bitcast_fusion.1
  893.9 35.5 %all-gather.36.cloned.1.call-done = bf16[32,256,512]{2,1,0:T(8,128)(2,1)} async-done(((bf16[4,256,512]{2,1,0:T(8,128)(2,1)}), bf16[32,256,512]{2,1,0:T(8,128)(2,1)}) %all-gather.36.cloned.1.call-update) | async-done | bytes 8388624 | tf_op jit(solution)/shard_map/all_gather | solution.py:25
  929.5 19.4 while.29
  939.2 2.4 fusion.174
  941.6 2.4 fusion.174
  944.1 2.4 fusion.174
  953.3 3.6 fusion.8
  960.7 2.9 convolution_bitcast_fusion.2
  966.1 9.2 convolution_bitcast_fusion
  976.5 8.1 fusion.120
  985.7 8.2 fusion.80
  994.8 5.1 fusion.104
  1000.0 9.9 fusion.102
  1011.0 8.2 fusion.121
  1020.3 8.2 fusion.122
  1031.8 62.7 %reduce-scatter.12.cloned.1.call-done = f32[128,4,256]{2,0,1:T(8,128)} async-done(((f32[2048,4,256]{2,0,1:T(8,128)}), f32[128,4,256]{2,0,1:T(8,128)}) %reduce-scatter.12.cloned.1.call-update) | async-done | bytes 524304 | tf_op jit(solution)/shard_map/reduce_scatter | solution.py:287
  1096.6 40.6 %all-reduce.14.cloned.1.call-done = (bf16[1,128,2048]{2,1,0:T(8,128)(2,1)}, bf16[1,128,2048]{2,1,0:T(8,128)(2,1)}) async-done(((bf16[1,128,2048]{2,1,0:T(8,128)(2,1)}, bf16[1,128,2048]{2,1,0:T(8,128)(2,1)}), (bf16[1,128,2048]{2,1,0:T(8,128)(2,1)}, bf16[1,128,2048]{2,1,0:T(8,128)(2,1)})) %all-reduce.14.cloned.1.call-update) | async-done | bytes 1048592 | tf_op jit(solution)/shard_map/psum | solution.py:203
  1140.2 62.5 %all-reduce.4 = (f32[2048]{0:T(1024)S(1)}, f32[2048]{0:T(1024)S(1)}) all-reduce(f32[2048]{0:T(1024)S(1)} %get-tuple-element.305, f32[2048]{0:T(1024)S(1)} %get-tuple-element.303), channel_id=14, replica_groups=mesh['fsdp'=2,'ctx'=8,'tp'=2] {'fsdp','ctx'}, use_global_device_ids=true, to_apply=%region_29.30.clone | all-reduce | flops 4096 | bytes 32768
  1206.0 2.5 add_add_fusion.3
  1208.6 112.0 %reduce-scatter.26.cloned.1.call-done = f32[128,2048]{0,1:T(8,128)} async-done(((f32[2048,2048]{0,1:T(8,128)}), f32[128,2048]{0,1:T(8,128)}) %reduce-scatter.26.cloned.1.call-update) | async-done | bytes 1048592 | tf_op jit(solution)/shard_map/reduce_scatter | solution.py:294
  1320.6 2.5 copy.193
  1323.1 179.6 %reduce-scatter.20.cloned.1.call-done = f32[128,4,512]{2,0,1:T(8,128)} async-done(((f32[2048,4,512]{2,0,1:T(8,128)}), f32[128,4,512]{2,0,1:T(8,128)}) %reduce-scatter.20.cloned.1.call-update) | async-done | bytes 1048592 | tf_op jit(solution)/shard_map/reduce_scatter | solution.py:291
  1502.7 2.9 copy.192
  1505.6 179.2 %reduce-scatter.18.cloned.1.call-done = f32[128,4,512]{2,0,1:T(8,128)} async-done(((f32[2048,4,512]{2,0,1:T(8,128)}), f32[128,4,512]{2,0,1:T(8,128)}) %reduce-scatter.18.cloned.1.call-update) | async-done | bytes 1048592 | tf_op jit(solution)/shard_map/reduce_scatter | solution.py:290
  1684.8 2.9 copy.191
  1687.6 105.5 %reduce-scatter.14.cloned.1.call-done = f32[128,4,256]{2,0,1:T(8,128)} async-done(((f32[2048,4,256]{2,0,1:T(8,128)}), f32[128,4,256]{2,0,1:T(8,128)}) %reduce-scatter.14.cloned.1.call-update) | async-done | bytes 524304 | tf_op jit(solution)/shard_map/reduce_scatter | solution.py:288
  1795.3 180.7 %reduce-scatter.16.cloned.1.call-done = f32[128,4,512]{2,0,1:T(8,128)} async-done(((f32[2048,4,512]{2,0,1:T(8,128)}), f32[128,4,512]{2,0,1:T(8,128)}) %reduce-scatter.16.cloned.1.call-update) | async-done | bytes 1048592 | tf_op jit(solution)/shard_map/reduce_scatter | solution.py:289
  1976.0 2.9 copy.190
  1978.9 180.0 %reduce-scatter.22.cloned.1.call-done = f32[128,2048]{1,0:T(8,128)} async-done(((f32[2048,2048]{1,0:T(8,128)}), f32[128,2048]{1,0:T(8,128)}) %reduce-scatter.22.cloned.1.call-update) | async-done | bytes 1048592 | tf_op jit(solution)/shard_map/reduce_scatter | solution.py:292
  2158.9 182.8 %reduce-scatter.24.cloned.1.call-done = f32[128,2048]{1,0:T(8,128)} async-done(((f32[2048,2048]{1,0:T(8,128)}), f32[128,2048]{1,0:T(8,128)}) %reduce-scatter.24.cloned.1.call-update) | async-done | bytes 1048592 | tf_op jit(solution)/shard_map/reduce_scatter | solution.py:293
  (221 shorter events, 80.7 us)
Async XLA Ops:
  7.2 133.3 %copy-start = (bf16[1,128,2048]{2,1,0:T(8,128)(2,1)S(1)}, bf16[1,128,2048]{2,1,0:T(8,128)(2,1)}, u32[]{:S(2)}) copy-start(bf16[1,128,2048]{2,1,0:T(8,128)(2,1)} %param.18) | copy-start | bytes 1572868
  7.2 57.0 %all-gather.22.cloned.1.call-start = ((), (), s32[]{:S(2)}) async-start(), calls=%async_computation.11 | async-start | bytes 4456448 | tf_op jit(solution)/shard_map/all_gather | solution.py:145
  9.0 131.5 %all-gather.18.cloned.1.call-start = ((), (), s32[]{:S(2)}) async-start(), calls=%async_computation.9 | async-start | bytes 8912896 | tf_op jit(solution)/shard_map/all_gather | solution.py:146
  11.0 181.4 %all-gather.20.cloned.1.call-start = ((), (), s32[]{:S(2)}) async-start(), calls=%async_computation.10 | async-start | bytes 4456448 | tf_op jit(solution)/shard_map/all_gather | solution.py:144
  12.7 255.7 %all-gather.24.cloned.1.call-start = ((), (), s32[]{:S(2)}) async-start(), calls=%async_computation.12 | async-start | bytes 8912896 | tf_op jit(solution)/shard_map/all_gather | solution.py:147
  14.8 404.6 %all-gather.34.cloned.1.call-start = ((), (), s32[]{:S(2)}) async-start(), calls=%async_computation.27 | async-start | bytes 18874368 | tf_op jit(solution)/shard_map/all_gather | solution.py:11
  42.6 1.2 copy-start.43
  67.3 80.5 %copy-start.34 = (bf16[128,4,512]{2,1,0:T(4,128)(2,1)S(1)}, bf16[128,4,512]{2,1,0:T(4,128)(2,1)}, u32[]{:S(2)}) copy-start(bf16[128,4,512]{2,1,0:T(4,128)(2,1)} %param.23) | copy-start | bytes 1572868
  67.3 96.8 %copy-start.39 = (bf16[4,32]{1,0:T(4,128)(2,1)S(1)}, bf16[4,32]{1,0:T(4,128)(2,1)}, u32[]{:S(2)}) copy-start(bf16[4,32]{1,0:T(4,128)(2,1)} %param.29) | copy-start | bytes 772
  145.2 279.2 %copy-start.8 = (bf16[128,4,512]{2,0,1:T(8,128)(2,1)}, bf16[128,4,512]{2,0,1:T(8,128)(2,1)S(1)}, u32[]{:S(2)}) copy-start(bf16[128,4,512]{2,0,1:T(8,128)(2,1)S(1)} %convolution_convert_fusion.2) | copy-start | bytes 1572868
  147.7 347.4 %all-gather.26.cloned.1.call-start = ((), (), s32[]{:S(2)}) async-start(), calls=%async_computation.13 | async-start | bytes 8912896 | tf_op jit(solution)/shard_map/all_gather | solution.py:148
  148.7 392.1 %all-reduce.10.cloned.1.call-start = ((), (), s32[]{:S(2)}) async-start(), calls=%async_computation.14 | async-start | bytes 2097152 | tf_op jit(solution)/shard_map/psum | solution.py:197
  426.0 78.5 %copy-start.41 = (bf16[128]{0:T(256)(128)(2,1)S(1)}, bf16[128]{0:T(256)(128)(2,1)}, u32[]{:S(2)}) copy-start(bf16[128]{0:T(256)(128)(2,1)} %param.28) | copy-start | bytes 772
  428.6 113.9 %copy-start.16 = (bf16[128,4,512]{0,2,1:T(8,128)(2,1)}, bf16[128,4,512]{0,2,1:T(8,128)(2,1)S(1)}, u32[]{:S(2)}) copy-start(bf16[128,4,512]{0,2,1:T(8,128)(2,1)S(1)} %fusion.78) | copy-start | bytes 1572868
  502.4 115.8 %all-gather.28.cloned.1.call-start = ((), (), s32[]{:S(2)}) async-start(), calls=%async_computation.15 | async-start | bytes 8912896 | tf_op jit(solution)/shard_map/all_gather | solution.py:149
  503.1 190.7 %all-gather.30.cloned.1.call-start = ((), (), s32[]{:S(2)}) async-start(), calls=%async_computation.16 | async-start | bytes 8912896 | tf_op jit(solution)/shard_map/all_gather | solution.py:150
  503.9 265.4 %all-gather.32.cloned.1.call-start = ((), (), s32[]{:S(2)}) async-start(), calls=%async_computation.17 | async-start | bytes 8912896 | tf_op jit(solution)/shard_map/all_gather | solution.py:151
  504.5 322.0 %all-reduce.12.cloned.1.call-start = ((), (), s32[]{:S(2)}) async-start(), calls=%async_computation.18 | async-start | bytes 2097152 | tf_op jit(solution)/shard_map/psum | solution.py:238
  542.2 1.0 copy-start.2
  542.3 81.5 %copy-start.35 = (f32[128]{0:T(128)}, f32[128]{0:T(128)S(1)}, u32[]{:S(2)}) copy-start(f32[128]{0:T(128)S(1)} %broadcast_multiply_fusion.1) | copy-start | bytes 1540
  542.6 81.3 %copy-start.36 = (f32[128]{0:T(128)}, f32[128]{0:T(128)S(1)}, u32[]{:S(2)}) copy-start(f32[128]{0:T(128)S(1)} %fusion.100) | copy-start | bytes 1540
  776.3 7.8 copy-start.32
  776.3 7.9 copy-start.1
  788.0 141.4 %all-gather.36.cloned.1.call-start = ((), (), s32[]{:S(2)}) async-start(), calls=%async_computation.28 | async-start | bytes 9437184 | tf_op jit(solution)/shard_map/all_gather | solution.py:25
  831.0 12.0 copy-start.9
  831.0 10.3 copy-start.7
  831.1 10.3 copy-start.11
  831.1 10.3 copy-start.37
  832.7 10.3 copy-start.30
  832.7 11.3 copy-start.13
  843.1 1.0 copy-start.4
  847.0 183.4 %reduce-scatter.28.cloned.1.call-start = ((), (), s32[]{:S(2)}) async-start(), calls=%async_computation.29 | async-start | bytes 278528
  851.0 3.3 copy-start.27
  854.7 4.8 copy-start.23
  854.7 5.3 copy-start.42
  854.7 239.7 %reduce-scatter.12.cloned.1.call-start = ((), (), s32[]{:S(2)}) async-start(), calls=%async_computation.19 | async-start | bytes 8912896 | tf_op jit(solution)/shard_map/reduce_scatter | solution.py:287
  859.5 277.7 %all-reduce.14.cloned.1.call-start = ((), (), s32[]{:S(2)}) async-start(), calls=%async_computation.30 | async-start | bytes 2097152 | tf_op jit(solution)/shard_map/psum | solution.py:203
  877.4 9.2 copy-start.18
  948.9 8.0 copy-start.5
  948.9 10.2 copy-start.20
  948.9 11.8 slice-start
  953.3 5.8 copy-start.25
  956.9 3.8 slice-start.1
  959.1 4.5 copy-start.21
  959.2 4.5 copy-start.22
  959.2 4.5 copy-start.24
  960.7 5.4 copy-start.14
  966.1 354.5 %reduce-scatter.26.cloned.1.call-start = ((), (), s32[]{:S(2)}) async-start(), calls=%async_computation.26 | async-start | bytes 17825792 | tf_op jit(solution)/shard_map/reduce_scatter | solution.py:294
  975.3 1.0 copy-start.17
  975.3 1.2 copy-start.31
  975.3 527.4 %reduce-scatter.20.cloned.1.call-start = ((), (), s32[]{:S(2)}) async-start(), calls=%async_computation.23 | async-start | bytes 17825792 | tf_op jit(solution)/shard_map/reduce_scatter | solution.py:291
  984.6 1.0 copy-start.19
  984.6 700.1 %reduce-scatter.18.cloned.1.call-start = ((), (), s32[]{:S(2)}) async-start(), calls=%async_computation.22 | async-start | bytes 17825792 | tf_op jit(solution)/shard_map/reduce_scatter | solution.py:290
  993.9 799.3 %reduce-scatter.14.cloned.1.call-start = ((), (), s32[]{:S(2)}) async-start(), calls=%async_computation.20 | async-start | bytes 8912896 | tf_op jit(solution)/shard_map/reduce_scatter | solution.py:288
  1000.0 976.1 %reduce-scatter.16.cloned.1.call-start = ((), (), s32[]{:S(2)}) async-start(), calls=%async_computation.21 | async-start | bytes 17825792 | tf_op jit(solution)/shard_map/reduce_scatter | solution.py:289
  1009.9 1.1 copy-start.29
  1010.0 1148.9 %reduce-scatter.22.cloned.1.call-start = ((), (), s32[]{:S(2)}) async-start(), calls=%async_computation.24 | async-start | bytes 17825792 | tf_op jit(solution)/shard_map/reduce_scatter | solution.py:292
  1019.2 1.0 copy-start.33
  1019.2 1322.5 %reduce-scatter.24.cloned.1.call-start = ((), (), s32[]{:S(2)}) async-start(), calls=%async_computation.25 | async-start | bytes 17825792 | tf_op jit(solution)/shard_map/reduce_scatter | solution.py:293
  1028.5 110.1 %copy-start.44 = (f32[128]{0:T(128)S(1)}, f32[128]{0:T(128)}, u32[]{:S(2)}) copy-start(f32[128]{0:T(128)} %copy-done.43) | copy-start | bytes 1540
  1028.5 175.4 %copy-start.3 = (f32[1,128,2048]{2,1,0:T(8,128)S(1)}, f32[1,128,2048]{2,1,0:T(8,128)}, u32[]{:S(2)}) copy-start(f32[1,128,2048]{2,1,0:T(8,128)} %copy-done.2) | copy-start | bytes 3145732
  1028.5 177.5 %copy-start.10 = (f32[1,128,2048]{2,1,0:T(8,128)S(1)}, f32[1,128,2048]{2,1,0:T(8,128)}, u32[]{:S(2)}) copy-start(f32[1,128,2048]{2,1,0:T(8,128)} %copy-done.9) | copy-start | bytes 3145732
  1028.5 177.5 %copy-start.15 = (bf16[1,128,2048]{2,1,0:T(8,128)(2,1)S(1)}, bf16[1,128,2048]{2,1,0:T(8,128)(2,1)}, u32[]{:S(2)}) copy-start(bf16[1,128,2048]{2,1,0:T(8,128)(2,1)} %param.31) | copy-start | bytes 1572868
  1028.5 177.5 %copy-start.38 = (f32[128]{0:T(128)S(1)}, f32[128]{0:T(128)}, u32[]{:S(2)}) copy-start(f32[128]{0:T(128)} %copy-done.37) | copy-start | bytes 1540
  (6 other events, 4.8 us)
Sparse Core Ops, SparseCore 0:
  10.8 53.2 all-gather.21
  67.0 73.4 all-gather.17
  143.3 49.0 all-gather.19
  195.0 73.4 all-gather.23
  269.9 149.3 all-gather.33
  422.0 73.1 all-gather.25
  502.5 38.2 all-reduce.9
  543.3 74.8 all-gather.27
  620.6 73.1 all-gather.29
  696.1 73.1 all-gather.31
  788.2 38.2 all-reduce.11
  847.1 82.3 all-gather.35
  933.0 53.8 reduce-scatter.27
  990.8 103.6 reduce-scatter.11
  1097.2 39.9 all-reduce.13
  1141.7 178.8 reduce-scatter.25
  1325.1 177.5 reduce-scatter.19
  1507.2 177.5 reduce-scatter.17
  1689.4 103.7 reduce-scatter.13
  1797.7 178.3 reduce-scatter.15
  1981.3 177.5 reduce-scatter.21
  2164.1 177.5 reduce-scatter.23
where the time goes:
time: 2360 us; the launch traced here: 2350 us
  waiting for transfers between devices  1920 us (81%)
  matrix products  177 us (8%)
  blocking collectives  155 us (7%)
  other arithmetic  42.4 us (2%)
  local copies, waits for them, and re-layouts  39.5 us (2%)
    reduce_scatter x1, waiting for transfers between devices, local(): lax.psum_scatter(grad_up, ('fsdp', 'ctx'), scatter_dimension=0, tiled=True)  183 us
    reduce_scatter x1, waiting for transfers between devices, local(): lax.psum_scatter(grad_value, ('fsdp', 'ctx'), scatter_dimension=0, tiled=...  181 us
    reduce_scatter x1, waiting for transfers between devices, local(): lax.psum_scatter(grad_gelu, ('fsdp', 'ctx'), scatter_dimension=0, tiled=T...  180 us
    reduce_scatter x1, waiting for transfers between devices, local(): lax.psum_scatter(grad_output, ('fsdp', 'ctx'), scatter_dimension=0, tiled...  180 us
    reduce_scatter x1, waiting for transfers between devices, local(): lax.psum_scatter(grad_swish, ('fsdp', 'ctx'), scatter_dimension=0, tiled=...  179 us
    all_gather x1, waiting for transfers between devices, prefix(): gathered = jax.tree.map(lambda a: lax.all_gather(a, axis), part)  143 us
    reduce_scatter x1, waiting for transfers between devices, local(): lax.psum_scatter(grad_down, ('fsdp', 'ctx'), scatter_dimension=0, tiled=T...  112 us
    reduce_scatter x1, waiting for transfers between devices, local(): lax.psum_scatter(grad_key, ('fsdp', 'ctx'), scatter_dimension=0, tiled=True)  106 us
  transfers between devices with their start and end apart: 22, of which 21 were waited for; matrix products, arithmetic and copies ran while one was open for 9% of the time, Pallas kernels for 0%

commit v1 on v0

--- a/solution.py
+++ b/solution.py
@@ -1,7 +1,762 @@
+import types
+
 import jax
 import jax.numpy as jnp
 from jax import lax
+from jax.experimental import pallas as pl
+from jax.experimental.pallas import tpu as pltpu
 from jax.sharding import PartitionSpec as P
+
+MESH = pl.DeviceIdType.MESH
+BF = jnp.bfloat16
+F32 = jnp.float32
+
+ZN = 4
+BLK = 128
+HALF = 64
+TOK = ZN * BLK
+D = 2048
+CH = 512
+NCH = 7
+NC = 4
+AC = 4
+AR = HALF // AC
+SETS = 4
+VLIM = 62 * 2**20
+
+
+def nt(a, b):
+    return lax.dot_general(a, b, (((1,), (1,)), ((), ())), preferred_element_type=F32)
+
+
+def nn(a, b):
+    return lax.dot_general(a, b, (((1,), (0,)), ((), ())), preferred_element_type=F32)
+
+
+def normed(v):
+    center = v - jnp.mean(v, axis=-1, keepdims=True)
+    rstd = lax.rsqrt(jnp.mean(center * center, axis=-1, keepdims=True) + 1e-05)
+    return center * rstd, rstd
+
+
+def norm_back(n, rstd, g):
+    return rstd * (
+        g - jnp.mean(g, axis=-1, keepdims=True) - n * jnp.mean(g * n, axis=-1, keepdims=True)
+    )
+
+
+def remote(src, dst, ss, rs, dev):
+    return pltpu.make_async_remote_copy(src, dst, ss, rs, device_id=dev, device_id_type=MESH)
+
+
+SCRATCH = dict(
+    gall=((16, 8, 128), F32),
+    W=((NCH, 16, BLK, CH), BF),
+    first=((ZN, BLK, D), BF),
+    cot=((ZN, BLK, D), BF),
+    second=((ZN, BLK, D), BF),
+    hlow=((ZN, BLK, D), BF),
+    XT=((16, BLK, TOK), BF),
+    qkv=((2, TOK, 1024), BF),
+    swish=((TOK, CH), F32),
+    ret=((TOK, CH), F32),
+    gg=((TOK, CH), F32),
+    dr=((TOK, CH), BF),
+    YB=((NCH, TOK, CH), BF),
+    dkv_s=((TOK, 768), BF),
+    dkv_r=((TOK, 768), BF),
+    tmp=((3, TOK, 256), F32),
+    ysend=((2, NC, ZN, HALF, CH), BF),
+    yrecv=((2, NC, ZN, HALF, CH), BF),
+    zsend=((2, NC, ZN, HALF, CH), BF),
+    zrecv=((2, NC, ZN, HALF, CH), BF),
+    hidden=((HALF, D), F32),
+    ghid=((HALF, D), F32),
+    rsum=((HALF, D), F32),
+    ostage=((2, HALF, D), BF),
+    gcs=((2, ZN, BLK, CH), BF),
+    gcr=((SETS, 2, ZN, BLK, CH), BF),
+    gxs=((SETS, ZN, BLK, CH), BF),
+    gxr=((SETS, ZN, BLK, CH), BF),
+    gzs=((SETS, ZN, BLK, CH), BF),
+    vec=((8, D), F32),
+    vrc=((8, D), F32),
+    vrx=((8, D), F32),
+    vry=((8, D), F32),
+    vz=((ZN, 8, D), F32),
+)
+SEMS = dict(
+    g_s=(3, 8), g_r=(3, 8),
+    wz_s=(NCH, 3), wz_r=(NCH, 3), wx_s=(NCH, 4), wx_r=(NCH, 4), wc_s=(NCH, 8), wc_r=(NCH, 8), wl=(NCH,),
+    az_s=(4, AC, 3), az_r=(4, AC, 3), ay_s=(4, AC, 4), ay_r=(4, AC, 4),
+    ry_s=(4, NC), ry_r=(4, NC), rz_s=(4, NC, 3), rz_r=(4, NC, 3),
+    kv_s=(2,), kv_r=(2,),
+    gc_s=(NCH, 2), gc_r=(NCH, 2), gx_s=(NCH,), gx_r=(NCH,), gz_s=(NCH, 3), gz_r=(NCH, 3), gl=(NCH,),
+    v_s=(6,), v_r=(6,), o_s=(2,), o_r=(2,), ol=(4,),
+    credit=None,
+)
+NAMES = list(SCRATCH) + list(SEMS)
+
+
+def kernel(tok, gp, lr, cot_in, pk, wg, wu, wd, res_o, gtok_o, gwa_o, gwf_o, vec_o, *scratch):
+    s = types.SimpleNamespace(**dict(zip(NAMES, scratch)))
+    W, YB, XT = s.W, s.YB, s.XT
+    x, k, y = lax.axis_index("fsdp"), lax.axis_index("ctx"), lax.axis_index("tp")
+    z, c = k // 2, k % 2
+    zup = [lax.rem(z + i, ZN) for i in range(ZN)]
+    zdn = [lax.rem(z + ZN - i, ZN) for i in range(ZN)]
+    zdev = [(x, zup[i] * 2 + c, y) for i in range(ZN)]
+    xdev, ydev, cdev = (1 - x, k, y), (x, k, 1 - y), (x, z * 2 + 1 - c, y)
+    peers = range(1, ZN)
+
+    def place(xx, zz, cc):
+        return xx * 8 + zz * 2 + cc
+
+    me = place(x, z, c)
+    log_rate = lr[z]
+
+    def loop(n, f):
+        def step(i, carry):
+            f(i)
+            return carry
+
+        lax.fori_loop(0, n, step, 0)
+
+    barrier = pltpu.get_barrier_semaphore()
+    for dev in zdev[1:] + [xdev, ydev, cdev]:
+        pl.semaphore_signal(barrier, inc=1, device_id=dev, device_id_type=MESH)
+    pl.semaphore_wait(barrier, 6)
+
+    def w_src(n, zz):
+        if n < 4:
+            return pk.at[zz, :, pl.ds(n * CH, CH)]
+        return (wg, wu, wd)[n - 4].at[:, pl.ds(pl.multiple_of(zz * CH, CH), CH)]
+
+    def w_local(n, zz):
+        return pltpu.make_async_copy(w_src(n, zz), W.at[n, me], s.wl.at[n])
+
+    def w_send(n):
+        for i in peers:
+            remote(w_src(n, zup[i]), W.at[n, me], s.wz_s.at[n, i - 1], s.wz_r.at[n, i - 1], zdev[i]).start()
+        w_local(n, z).start()
+
+    def w_z(n, i):
+        blk = W.at[n, place(x, zdn[i], c)]
+        return remote(blk, blk, s.wz_s.at[n, i - 1], s.wz_r.at[n, i - 1], zdev[i])
+
+    def w_x(n, j, xx):
+        blk = W.at[n, place(xx, zdn[j], c)]
+        return remote(blk, blk, s.wx_s.at[n, j], s.wx_r.at[n, j], xdev)
+
+    def w_c(n, j, cc):
+        xx = x if j < 4 else 1 - x
+        blk = W.at[n, place(xx, zdn[j % 4], cc)]
+        return remote(blk, blk, s.wc_s.at[n, j], s.wc_r.at[n, j], cdev)
+
+    def pump_z(n):
+        for i in range(ZN):
+            if i == 0:
+                pltpu.make_async_copy(W.at[n, me], W.at[n, me], s.wl.at[n]).wait()
+            else:
+                w_z(n, i).wait_recv()
+            w_x(n, i, x).start()
+            w_c(n, i, c).start()
+
+    def pump_x(n):
+        for j in range(ZN):
+            w_x(n, j, 1 - x).wait_recv()
+            w_c(n, ZN + j, c).start()
+
+    def w_fin(n):
+        for j in range(8):
+            w_c(n, j, 1 - c).wait_recv()
+
+    def w_done(n):
+        for i in peers:
+            w_z(n, i).wait_send()
+        for j in range(ZN):
+            w_x(n, j, x).wait_send()
+        for j in range(8):
+            w_c(n, j, c).wait_send()
+
+    def a_rows(yy, ch):
+        return pl.ds(pl.multiple_of(yy * HALF + ch * AR, AR), AR)
+
+    def a_z(buf, ia, ch, i, zz):
+        blk = buf.at[zz, a_rows(y, ch)]
+        return remote(blk, blk, s.az_s.at[ia, ch, i - 1], s.az_r.at[ia, ch, i - 1], zdev[i])
+
+    def a_y(buf, ia, ch, i, yy):
+        blk = buf.at[zdn[i], a_rows(yy, ch)]
+        return remote(blk, blk, s.ay_s.at[ia, ch, i], s.ay_r.at[ia, ch, i], ydev)
+
+    def ag_send(buf, ia, own):
+        def f(ch):
+            for i in peers:
+                a_z(buf, ia, ch, i, z).start()
+            if own:
+                a_y(buf, ia, ch, 0, y).start()
+
+        loop(AC, f)
+
+    def ag_forward(buf, ia):
+        def f(ch):
+            for i in peers:
+                a_z(buf, ia, ch, i, zdn[i]).wait_recv()
+                a_y(buf, ia, ch, i, y).start()
+
+        loop(AC, f)
+
+    def ag_wait(buf, ia, own):
+        def f(ch):
+            for i in range(0 if own else 1, ZN):
+                a_y(buf, ia, ch, i, 1 - y).wait_recv()
+
+        loop(AC, f)
+
+    def ag_done(buf, ia, own):
+        def f(ch):
+            for i in peers:
+                a_z(buf, ia, ch, i, z).wait_send()
+            for i in range(0 if own else 1, ZN):
+                a_y(buf, ia, ch, i, y).wait_send()
+
+        loop(AC, f)
+
+    def product(chunks, j, yy):
+        total = None
+        for n in chunks:
+            rows = [YB[n, pl.ds(pl.multiple_of(zz * BLK + yy * HALF, HALF), HALF), :] for zz in range(ZN)]
+            lhs = jnp.concatenate(rows, axis=0)
+            rhs = W[n, pl.ds(j * 4, 4)].reshape(CH, CH)
+            part = nt(lhs, rhs)
+            total = part if total is None else total + part
+        return total.reshape(ZN, HALF, CH)
+
+    def r_y(ir, b, j):
+        return remote(s.ysend.at[b, j], s.yrecv.at[b, j], s.ry_s.at[ir, j], s.ry_r.at[ir, j], ydev)
+
+    def r_z(ir, b, j, i):
+        return remote(
+            s.zsend.at[b, j, zup[i]], s.zrecv.at[b, j, i], s.rz_s.at[ir, j, i - 1], s.rz_r.at[ir, j, i - 1], zdev[i]
+        )
+
+    def rs_a(ir, b, chunks):
+        def f(j):
+            s.ysend[b, j] = product(chunks, j, 1 - y).astype(BF)
+            r_y(ir, b, j).start()
+
+        loop(NC, f)
+
+    def rs_b(ir, b, chunks):
+        def f(j):
+            own = product(chunks, j, y)
+            r_y(ir, b, j).wait_recv()
+            s.zsend[b, j] = (own + s.yrecv[b, j].astype(F32)).astype(BF)
+            for i in peers:
+                r_z(ir, b, j, i).start()
+
+        loop(NC, f)
+
+    def rs_c(ir, b):
+        def f(j):
+            for i in peers:
+                r_z(ir, b, j, i).wait_recv()
+            total = s.zsend[b, j, z].astype(F32)
+            for i in peers:
+                total = total + s.zrecv[b, j, i].astype(F32)
+            s.rsum[:, pl.ds(pl.multiple_of(j * CH, CH), CH)] = total
+
+        loop(NC, f)
+
+    def rs_done(ir, b):
+        def f(j):
+            r_y(ir, b, j).wait_send()
+            for i in peers:
+                r_z(ir, b, j, i).wait_send()
+
+        loop(NC, f)
+
+    def transpose(buf):
+        def f(q):
+            cols = pl.ds(pl.multiple_of(q * BLK, BLK), BLK)
+            XT[q] = buf[:, :, cols].reshape(TOK, BLK).T
+
+        loop(16, f)
+
+    def grad_rows(n, xx, cc):
+        lhs = jnp.concatenate([XT[place(xx, zz, cc)] for zz in range(ZN)], axis=0)
+        return nn(lhs, YB[n]).reshape(ZN, BLK, CH)
+
+    def g_c(n, xx):
+        return remote(s.gcs.at[xx], s.gcr.at[n % SETS, xx], s.gc_s.at[n, xx], s.gc_r.at[n, xx], cdev)
+
+    def g_x(n):
+        return remote(s.gxs.at[n % SETS], s.gxr.at[n % SETS], s.gx_s.at[n], s.gx_r.at[n], xdev)
+
+    def g_dst(n):
+        if n < 4:
+            return gwa_o.at[n, z]
+        return gwf_o.at[n - 4, :, pl.ds(pl.multiple_of(z * CH, CH), CH)]
+
+    def g_z(n, i):
+        return remote(s.gzs.at[n % SETS, zup[i]], g_dst(n), s.gz_s.at[n, i - 1], s.gz_r.at[n, i - 1], zdev[i])
+
+    def g_local(n):
+        return pltpu.make_async_copy(s.gzs.at[n % SETS, z], g_dst(n), s.gl.at[n])
+
+    def grad_a(n, first_use):
+        b = n % SETS
+
+        def f(t):
+            xx = (1 - x) * (1 - t) + x * t
+            s.gcs[xx] = grad_rows(n, xx, 1 - c).astype(BF)
+            g_c(n, xx).start()
+
+        loop(2, f)
+        own = grad_rows(n, 1 - x, c)
+        g_c(n, 1 - x).wait_recv()
+        if not first_use:
+            pl.semaphore_wait(s.credit, 1)
+        s.gxs[b] = (own + s.gcr[b, 1 - x].astype(F32)).astype(BF)
+        g_x(n).start()
+        own = grad_rows(n, x, c)
+        g_c(n, x).wait_recv()
+        s.gzs[b] = (own + s.gcr[b, x].astype(F32)).astype(BF)
+        for xx in range(2):
+            g_c(n, xx).wait_send()
+
+    def grad_b(n, more):
+        b = n % SETS
+        g_x(n).wait_recv()
+        s.gzs[b] = (s.gzs[b].astype(F32) + s.gxr[b].astype(F32)).astype(BF)
+        for i in peers:
+            g_z(n, i).start()
+        g_local(n).start()
+        g_x(n).wait_send()
+        if more:
+            pl.semaphore_signal(s.credit, inc=1, device_id=xdev, device_id_type=MESH)
+
+    def grad_sent(n):
+        for i in peers:
+            g_z(n, i).wait_send()
+        g_local(n).wait()
+
+    def grad_done(n):
+        for i in peers:
+            g_z(n, i).wait_recv()
+
+    def gain_row(r):
+        return jnp.concatenate([s.gall[q, r : r + 1, :] for q in range(16)], axis=1)
+
+    def group_gain():
+        pick = lax.broadcasted_iota(jnp.int32, (8, 128), 0) == 2 + z
+        parts = []
+        for r in range(4):
+            total = s.gall[4 * r]
+            for q in range(4 * r + 1, 4 * r + 4):
+                total = total + s.gall[q]
+            parts.append(jnp.sum(jnp.where(pick, total, 0.0), axis=0, keepdims=True))
+        return jnp.concatenate(parts, axis=1)
+
+    def position(shape, dim, both, start):
+        r = lax.broadcasted_iota(jnp.int32, shape, dim) + start
+        if both:
+            core, r = r // TOK, lax.rem(r, TOK)
+        else:
+            core = c
+        return r + (r // BLK) * BLK + core * BLK
+
+    def decay(later, earlier):
+        gap = later - earlier
+        keep = gap >= 0
+        return jnp.where(keep, jnp.exp(jnp.where(keep, gap, 0).astype(F32) * log_rate), 0.0)
+
+    own_rows = pl.ds(pl.multiple_of(y * HALF, HALF), HALF)
+
+    for n in range(3):
+        w_send(n)
+    cot_local = pltpu.make_async_copy(cot_in, s.cot.at[z], s.ol.at[0])
+    cot_local.start()
+
+    gall = s.gall
+    gall[me] = gp[...]
+
+    def g_gain(j, i, dev, q):
+        return remote(gall.at[q], gall.at[q], s.g_s.at[j, i], s.g_r.at[j, i], dev)
+
+    for i in peers:
+        g_gain(0, i, zdev[i], me).start()
+    for i in peers:
+        g_gain(0, i, zdev[i], place(x, zdn[i], c)).wait_recv()
+    for i in range(ZN):
+        g_gain(1, i, xdev, place(x, zdn[i], c)).start()
+    for i in range(ZN):
+        g_gain(2, i, cdev, place(x, zdn[i], c)).start()
+    for i in range(ZN):
+        g_gain(1, i, xdev, place(1 - x, zdn[i], c)).wait_recv()
+        g_gain(2, ZN + i, cdev, place(1 - x, zdn[i], c)).start()
+    for i in range(8):
+        xx = x if i < ZN else 1 - x
+        g_gain(2, i, cdev, place(xx, zdn[i % ZN], 1 - c)).wait_recv()
+    for i in peers:
+        g_gain(0, i, zdev[i], me).wait_send()
+    for i in range(ZN):
+        g_gain(1, i, xdev, place(x, zdn[i], c)).wait_send()
+    for i in range(8):
+        xx = x if i < ZN else 1 - x
+        g_gain(2, i, cdev, place(xx, zdn[i % ZN], c)).wait_send()
+
+    tokens = tok[...].astype(F32)
+    n_first, _ = normed(tokens)
+    s.first[z] = (n_first * gain_row(0)).astype(BF)
+    ag_send(s.first, 0, False)
+    loop(2, pump_z)
+    ag_forward(s.first, 0)
+    pump_z(2)
+    for n in range(3, NCH):
+        w_send(n)
+    cot_local.wait()
+    ag_send(s.cot, 1, False)
+    loop(3, pump_x)
+    ag_wait(s.first, 0, False)
+
+    qkv, swish = s.qkv, s.swish
+
+    def columns(n, t):
+        return W[n, :, :, pl.ds(pl.multiple_of(t * 256, 256), 256)].reshape(D, 256)
+
+    w_fin(0)
+
+    def project_qk(t):
+        scale = jnp.where(t == 1, 0.0625, 1.0)
+        out = nn(s.first[...].reshape(TOK, D), columns(0, t)) * scale
+        qkv[c, :, pl.ds(pl.multiple_of(t * 256, 256), 256)] = out.astype(BF)
+
+    loop(2, project_qk)
+    w_fin(1)
+
+    def project_v(t):
+        out = nn(s.first[...].reshape(TOK, D), columns(1, t))
+        qkv[c, :, pl.ds(pl.multiple_of(512 + t * 256, 256), 256)] = out.astype(BF)
+
+    loop(2, project_v)
+
+    def kv_copy(cc):
+        blk = qkv.at[cc, :, pl.ds(256, 768)]
+        return remote(blk, blk, s.kv_s.at[0], s.kv_r.at[0], cdev)
+
+    kv_copy(c).start()
+    w_fin(2)
+
+    def project_s(t):
+        out = nn(s.first[...].reshape(TOK, D), columns(2, t))
+        swish[:, pl.ds(pl.multiple_of(t * 256, 256), 256)] = out
+
+    loop(2, project_s)
+    pump_z(3)
+    kv_copy(1 - c).wait_recv()
+
+    def all_keys():
+        return qkv[:, :, 256:512].reshape(2 * TOK, 256)
+
+    def all_values():
+        return qkv[:, :, 512:1024].reshape(2 * TOK, CH)
+
+    def retain(h):
+        rows = pl.ds(pl.multiple_of(h * 256, 256), 256)
+        later = position((256, 2 * TOK), 0, False, h * 256)
+        earlier = position((256, 2 * TOK), 1, True, 0)
+        scores = nt(qkv[c, rows, 0:256], all_keys()) * decay(later, earlier)
+        s.ret[rows, :] = nn(scores.astype(BF), all_values())
+
+    loop(2, retain)
+    gain_g = group_gain()
+
+    def gate(h):
+        rows = pl.ds(pl.multiple_of(h * BLK, BLK), BLK)
+        n, _ = normed(s.ret[rows, :])
+        w = swish[rows, :]
+        YB[3, rows, :] = (n * gain_g * (w / (1.0 + jnp.exp(-w)))).astype(BF)
+
+    loop(ZN, gate)
+    pump_x(3)
+    w_fin(3)
+
+    rs_a(0, 0, (3,))
+    rs_b(0, 0, (3,))
+    loop(2, lambda n: pump_z(n + 4))
+    rs_c(0, 0)
+    hidden = tok[own_rows, :].astype(F32) + s.rsum[...]
+    s.hidden[...] = hidden
+    n_second, _ = normed(hidden)
+    s.second[z, own_rows, :] = (n_second * gain_row(1)).astype(BF)
+    ag_send(s.second, 2, True)
+    loop(2, lambda n: pump_x(n + 4))
+    pump_z(6)
+    pump_x(6)
+    ag_forward(s.cot, 1)
+    ag_forward(s.second, 2)
+    for n in range(4, NCH):
+        w_fin(n)
+    ag_wait(s.cot, 1, False)
+    ag_wait(s.second, 2, True)
+
+    tmp = s.tmp
+
+    def feed(t):
+        cols = pl.ds(pl.multiple_of(t * 256, 256), 256)
+        sec = s.second[...].reshape(TOK, D)
+        tmp[0] = nn(sec, columns(4, t))
+        tmp[1] = nn(sec, columns(5, t))
+        tmp[2] = nn(s.cot[...].reshape(TOK, D), columns(6, t))
+
+        def act(h):
+            rows = pl.ds(pl.multiple_of(h * HALF, HALF), HALF)
+            a, u, gm = tmp[0, rows, :], tmp[1, rows, :], tmp[2, rows, :]
+            root = 0.7978845608028654
+            th = jnp.tanh(root * (a + 0.044715 * (a * a * a)))
+            half = 0.5 * (1.0 + th)
+            gelu = a * half
+            slope = half + 0.5 * a * (1.0 - th * th) * (root * (1.0 + 0.134145 * (a * a)))
+            YB[6, rows, cols] = (gelu * u).astype(BF)
+            YB[4, rows, cols] = (gm * u * slope).astype(BF)
+            YB[5, rows, cols] = (gm * gelu).astype(BF)
+
+        loop(TOK // HALF, act)
+
+    loop(2, feed)
+    rs_done(0, 0)
+    rs_a(1, 0, (4, 5))
+    rs_a(2, 1, (6,))
+    rs_b(1, 0, (4, 5))
+    transpose(s.second)
+    grad_a(4, True)
+    grad_a(5, True)
+    rs_c(1, 0)
+    n_second, rstd = normed(s.hidden[...])
+    g_in = s.rsum[...]
+    s.vec[1:2, :] = jnp.sum(g_in * n_second, axis=0, keepdims=True)
+    ghid = s.cot[z, own_rows, :].astype(F32) + norm_back(n_second, rstd, g_in * gain_row(1))
+    s.ghid[...] = ghid
+    s.hlow[z, own_rows, :] = ghid.astype(BF)
+    ag_send(s.hlow, 3, True)
+    rs_b(2, 1, (6,))
+    transpose(s.cot)
+    grad_a(6, True)
+    grad_b(4, True)
+    grad_b(5, True)
+    grad_b(6, True)
+    ag_forward(s.hlow, 3)
+    ag_wait(s.hlow, 3, True)
+
+    def back_gated(t):
+        out = nn(s.hlow[...].reshape(TOK, D), columns(3, t))
+        s.gg[:, pl.ds(pl.multiple_of(t * 256, 256), 256)] = out
+
+    loop(2, back_gated)
+
+    def back_gate(h, total):
+        rows = pl.ds(pl.multiple_of(h * BLK, BLK), BLK)
+        n, rstd = normed(s.ret[rows, :])
+        w, g = swish[rows, :], s.gg[rows, :]
+        sig = 1.0 / (1.0 + jnp.exp(-w))
+        silu = w * sig
+        YB[2, rows, :] = (g * (n * gain_g) * (sig * (1.0 + w * (1.0 - sig)))).astype(BF)
+        gs = g * silu
+        s.dr[rows, :] = norm_back(n, rstd, gs * gain_g).astype(BF)
+        return total + jnp.sum(gs * n, axis=0, keepdims=True)
+
+    group = lax.fori_loop(0, ZN, back_gate, jnp.zeros((1, CH), F32))
+    s.vec[2:3, 0:CH] = group
+
+    def back_keys(core, h):
+        rows = pl.ds(pl.multiple_of(h * 256, 256), 256)
+        keys, values = qkv[core, rows, 256:512], qkv[core, rows, 512:1024]
+        query = qkv[c, :, 0:256]
+        r = lax.broadcasted_iota(jnp.int32, (256, TOK), 0) + h * 256
+        earlier = r + (r // BLK) * BLK + core * BLK
+        table = decay(position((256, TOK), 1, False, 0), earlier)
+        weights = (nt(keys, query) * table).astype(BF)
+        slopes = (nt(values, s.dr[...]) * table).astype(BF)
+        return rows, nn(slopes, query), nn(weights, s.dr[...])
+
+    def back_other(h):
+        rows, dk, dv = back_keys(1 - c, h)
+        s.dkv_s[rows, 0:256] = dk.astype(BF)
+        s.dkv_s[rows, 256:768] = dv.astype(BF)
+
+    def back_own(h):
+        rows, dk, dv = back_keys(c, h)
+        tmp[0, rows, :] = dk
+        tmp[1, rows, :] = dv[:, 0:256]
+        tmp[2, rows, :] = dv[:, 256:512]
+
+    loop(2, back_other)
+    dkv_copy = remote(s.dkv_s, s.dkv_r, s.kv_s.at[1], s.kv_r.at[1], cdev)
+    dkv_copy.start()
+    loop(2, back_own)
+
+    def back_query(h):
+        rows = pl.ds(pl.multiple_of(h * 256, 256), 256)
+        later = position((256, 2 * TOK), 0, False, h * 256)
+        earlier = position((256, 2 * TOK), 1, True, 0)
+        slopes = nt(s.dr[rows, :], all_values()) * decay(later, earlier)
+        YB[0, rows, 0:256] = nn(slopes.astype(BF), all_keys()).astype(BF)
+
+    loop(2, back_query)
+    dkv_copy.wait_recv()
+
+    def back_sum(h):
+        rows = pl.ds(pl.multiple_of(h * BLK, BLK), BLK)
+        other = s.dkv_r[rows, :].astype(F32)
+        YB[0, rows, 256:512] = ((tmp[0, rows, :] + other[:, 0:256]) * 0.0625).astype(BF)
+        YB[1, rows, 0:256] = (tmp[1, rows, :] + other[:, 256:512]).astype(BF)
+        YB[1, rows, 256:512] = (tmp[2, rows, :] + other[:, 512:768]).astype(BF)
+
+    loop(ZN, back_sum)
+
+    rs_done(1, 0)
+    rs_a(3, 0, (0, 1, 2))
+    rs_b(3, 0, (0, 1, 2))
+    transpose(s.first)
+    grad_sent(4)
+    grad_a(0, False)
+    grad_sent(5)
+    grad_a(1, False)
+    rs_c(3, 0)
+    n_first, rstd = normed(tok[own_rows, :].astype(F32))
+    g_in = s.rsum[...]
+    s.vec[0:1, :] = jnp.sum(g_in * n_first, axis=0, keepdims=True)
+    g_tok = s.ghid[...] + norm_back(n_first, rstd, g_in * gain_row(0))
+    s.ostage[0] = g_tok.astype(BF)
+
+    def out_copies(j, dst):
+        there = dst.at[own_rows]
+        return (
+            remote(s.ostage.at[j], there, s.o_s.at[j], s.o_r.at[j], ydev),
+            pltpu.make_async_copy(s.ostage.at[j], there, s.ol.at[1 + j]),
+        )
+
+    for copy in out_copies(0, gtok_o):
+        copy.start()
+    grad_b(0, False)
+    grad_b(1, False)
+    grad_sent(6)
+    grad_a(2, False)
+    transpose(s.hlow)
+    grad_a(3, True)
+    grad_b(2, False)
+    grad_b(3, False)
+    rs_c(2, 1)
+    s.ostage[1] = (s.hidden[...] + s.rsum[...]).astype(BF)
+    for copy in out_copies(1, res_o):
+        copy.start()
+
+    vec = s.vec
+
+    def v_copy(j, dst, dev):
+        return remote(vec, dst, s.v_s.at[j], s.v_r.at[j], dev)
+
+    vec[3:8, :] = jnp.zeros((5, D), F32)
+    vec[2:3, CH:D] = jnp.zeros((1, D - CH), F32)
+    for j, (dst, dev) in enumerate(((s.vrc, cdev), (s.vrx, xdev), (s.vry, ydev))):
+        copy = v_copy(j, dst, dev)
+        copy.start()
+        copy.wait()
+        if j < 2:
+            vec[...] = vec[...] + dst[...]
+        else:
+            vec[0:2, :] = vec[0:2, :] + dst[0:2, :]
+    s.vz[z] = vec[...]
+    for i in peers:
+        remote(vec, s.vz.at[z], s.v_s.at[2 + i], s.v_r.at[2 + i], zdev[i]).start()
+    for i in peers:
+        there = s.vz.at[zdn[i]]
+        copy = remote(there, there, s.v_s.at[2 + i], s.v_r.at[2 + i], zdev[i])
+        copy.wait_recv()
+    for i in peers:
+        remote(vec, s.vz.at[z], s.v_s.at[2 + i], s.v_r.at[2 + i], zdev[i]).wait_send()
+    vz = s.vz
+    vec_o[0:2, :] = ((vz[0, 0:2, :] + vz[1, 0:2, :]) + vz[2, 0:2, :]) + vz[3, 0:2, :]
+    vec_o[2:4, :] = jnp.zeros((2, D), F32)
+    for zz in range(ZN):
+        vec_o[4 + zz : 5 + zz, :] = vz[zz, 2:3, :]
+
+    for j, dst in enumerate((gtok_o, res_o)):
+        there = dst.at[pl.ds(pl.multiple_of((1 - y) * HALF, HALF), HALF)]
+        a, b = out_copies(j, dst)
+        a.wait_send()
+        b.wait()
+        remote(s.ostage.at[j], there, s.o_s.at[j], s.o_r.at[j], ydev).wait_recv()
+    for n in range(4):
+        grad_sent(n)
+    for n in range(NCH):
+        grad_done(n)
+    loop(NCH, w_done)
+    kv_copy(c).wait_send()
+    dkv_copy.wait_send()
+    for ia, (buf, own) in enumerate(((s.first, False), (s.cot, False), (s.second, True), (s.hlow, True))):
+        ag_done(buf, ia, own)
+    rs_done(2, 1)
+    rs_done(3, 0)
+
+
+def pieces(tokens, w_query, w_key, w_value, w_swish, w_output, w_gelu, w_up, w_down, gain_first, gain_second, gain_group, decay_rate, cotangent):
+    me = lax.axis_index("fsdp") * 8 + lax.axis_index("ctx")
+    pk = jnp.concatenate([w_query, w_key, w_value, w_swish, w_output], axis=2).transpose(1, 0, 2)
+    lane = lax.broadcasted_iota(jnp.int32, (ZN, BLK), 1) // 32
+    spread = jnp.where(lane == lax.rem(me, 4), jnp.tile(gain_group.astype(F32), (1, 4)), 0.0)
+    gp = jnp.concatenate(
+        [gain_first.astype(F32)[None], gain_second.astype(F32)[None], spread, jnp.zeros((2, BLK), F32)], axis=0
+    )
+    return (tokens[0], gp, jnp.log(decay_rate), cotangent[0], pk, w_gelu, w_up, w_down)
+
+
+def fused(*args):
+    shapes = [
+        jax.ShapeDtypeStruct((BLK, D), BF),
+        jax.ShapeDtypeStruct((BLK, D), BF),
+        jax.ShapeDtypeStruct((4, ZN, BLK, CH), BF),
+        jax.ShapeDtypeStruct((3, BLK, D), BF),
+        jax.ShapeDtypeStruct((8, D), F32),
+    ]
+    hbm = pl.BlockSpec(memory_space=pl.ANY)
+    vmem = pl.BlockSpec(memory_space=pltpu.VMEM)
+    smem = pl.BlockSpec(memory_space=pltpu.SMEM)
+    scratch = [pltpu.VMEM(*v) for v in SCRATCH.values()]
+    for name, shape in SEMS.items():
+        scratch.append(pltpu.SemaphoreType.REGULAR if shape is None else pltpu.SemaphoreType.DMA(shape))
+    result, g_tok, gwa, gwf, vec = pl.pallas_call(
+        kernel,
+        out_shape=shapes,
+        in_specs=[vmem, vmem, smem, hbm, hbm, hbm, hbm, hbm],
+        out_specs=[hbm, hbm, hbm, hbm, vmem],
+        scratch_shapes=scratch,
+        compiler_params=pltpu.CompilerParams(collective_id=0, has_side_effects=True, vmem_limit_bytes=VLIM),
+    )(*pieces(*args))
+    me = lax.axis_index("fsdp") * 8 + lax.axis_index("ctx")
+    swap = gwa.transpose(0, 2, 1, 3).astype(F32)
+    gwf = gwf.astype(F32)
+    g_first = lax.dynamic_slice(vec[0], (me * BLK,), (BLK,))
+    g_second = lax.dynamic_slice(vec[1], (me * BLK,), (BLK,))
+    g_group = lax.dynamic_slice(vec, (4, me * 32), (4, 32))
+    return (
+        result[None].astype(F32),
+        g_tok[None].astype(F32),
+        swap[0, :, :, 0:256],
+        swap[0, :, :, 256:512],
+        swap[1],
+        swap[2],
+        swap[3],
+        gwf[0],
+        gwf[1],
+        gwf[2],
+        g_first,
+        g_second,
+        g_group,
+    )
+
 
 highest_precision = lax.Precision.HIGHEST
 
@@ -122,7 +877,7 @@
     return jax.nn.gelu(act_gelu) * act_up
 
 
-def local(
+def general(
     tokens,
     w_query,
     w_key,
@@ -201,37 +956,15 @@
     mixed = mlp_section(act_gelu, act_up).astype(bf16)
     mlp_terms = jnp.einsum("spf,df->spd", mixed, full_down, preferred_element_type=f32)
     result = hidden + lax.psum(mlp_terms.astype(jnp.bfloat16), "tp").astype(jnp.float32)
-    regathered = (
-        lax.all_gather(w_query, ("fsdp", "ctx"), axis=0, tiled=True),
-        lax.all_gather(w_key, ("fsdp", "ctx"), axis=0, tiled=True),
-        lax.all_gather(w_value, ("fsdp", "ctx"), axis=0, tiled=True),
-        lax.all_gather(w_swish, ("fsdp", "ctx"), axis=0, tiled=True),
-        lax.all_gather(w_output, ("fsdp", "ctx"), axis=0, tiled=True),
-        lax.all_gather(w_gelu, ("fsdp", "ctx"), axis=0, tiled=True),
-        lax.all_gather(w_up, ("fsdp", "ctx"), axis=0, tiled=True),
-        lax.all_gather(w_down, ("fsdp", "ctx"), axis=0, tiled=True),
-        lax.all_gather(gain_first, ("fsdp", "ctx"), axis=0, tiled=True),
-        lax.all_gather(gain_second, ("fsdp", "ctx"), axis=0, tiled=True),
-        lax.all_gather(gain_group, ("fsdp", "ctx"), axis=1, tiled=True),
-    )
-    back_query, back_key, back_value, back_swish, back_output, back_gelu, back_up, back_down = (
-        regathered[0],
-        regathered[1],
-        regathered[2],
-        regathered[3],
-        regathered[4],
-        regathered[5],
-        regathered[6],
-        regathered[7],
-    )
+    back_query, back_key, back_value, back_swish, back_output, back_gelu, back_up, back_down = gathered[:8]
     grad_mixed = jnp.einsum("spd,df->spf", cotangent, back_down, preferred_element_type=f32)
-    grad_down = jnp.einsum("spd,spf->df", cotangent, mixed, preferred_element_type=f32)
+    grad_down = jnp.einsum("spd,spf->df", cotangent, mixed, preferred_element_type=f32).astype(bf16)
     _, pull_mlp = jax.vjp(mlp_section, act_gelu, act_up)
     grad_act_gelu, grad_act_up = pull_mlp(grad_mixed)
     gelu_low = grad_act_gelu.astype(bf16)
     up_low = grad_act_up.astype(bf16)
-    grad_gelu = jnp.einsum("spd,spf->df", second_low, gelu_low, preferred_element_type=f32)
-    grad_up = jnp.einsum("spd,spf->df", second_low, up_low, preferred_element_type=f32)
+    grad_gelu = jnp.einsum("spd,spf->df", second_low, gelu_low, preferred_element_type=f32).astype(bf16)
+    grad_up = jnp.einsum("spd,spf->df", second_low, up_low, preferred_element_type=f32).astype(bf16)
     second_terms = jnp.einsum(
         "spf,df->spd", gelu_low, back_gelu, preferred_element_type=f32
     ) + jnp.einsum("spf,df->spd", up_low, back_up, preferred_element_type=f32)
@@ -241,7 +974,7 @@
     grad_hidden = cotangent.astype(f32) + hidden_from_norm
     hidden_low = grad_hidden.astype(bf16)
     grad_gated = jnp.einsum("spd,dhv->sphv", hidden_low, back_output, preferred_element_type=f32)
-    grad_output = jnp.einsum("spd,sphv->dhv", hidden_low, gated, preferred_element_type=f32)
+    grad_output = jnp.einsum("spd,sphv->dhv", hidden_low, gated, preferred_element_type=f32).astype(bf16)
     _, pull_gate = jax.vjp(gate_section, retained, swish_in, group_gain)
     grad_retained, grad_swish_in, grad_group = pull_gate(grad_gated)
     swish_low = grad_swish_in.astype(bf16)
@@ -265,10 +998,10 @@
     query_low = grad_query_act.astype(bf16)
     key_low = (grad_key_act.astype(bf16).astype(f32) * key_scale).astype(bf16)
     value_low = grad_value_act.astype(bf16)
-    grad_query = jnp.einsum("spd,sphk->dhk", first_low, query_low, preferred_element_type=f32)
-    grad_key = jnp.einsum("spd,sphk->dhk", first_low, key_low, preferred_element_type=f32)
-    grad_value = jnp.einsum("spd,sphv->dhv", first_low, value_low, preferred_element_type=f32)
-    grad_swish = jnp.einsum("spd,sphv->dhv", first_low, swish_low, preferred_element_type=f32)
+    grad_query = jnp.einsum("spd,sphk->dhk", first_low, query_low, preferred_element_type=f32).astype(bf16)
+    grad_key = jnp.einsum("spd,sphk->dhk", first_low, key_low, preferred_element_type=f32).astype(bf16)
+    grad_value = jnp.einsum("spd,sphv->dhv", first_low, value_low, preferred_element_type=f32).astype(bf16)
+    grad_swish = jnp.einsum("spd,sphv->dhv", first_low, swish_low, preferred_element_type=f32).astype(bf16)
     first_terms = jnp.einsum("sphk,dhk->spd", query_low, back_query, preferred_element_type=f32)
     first_terms = first_terms + jnp.einsum(
         "sphk,dhk->spd", key_low, back_key, preferred_element_type=f32
@@ -283,19 +1016,10 @@
     _, pull_first = jax.vjp(norm_rows, inputs, first_gain)
     tokens_from_norm, grad_first = pull_first(grad_first_in)
     grad_tokens = grad_hidden + tokens_from_norm
-    owned = (
-        lax.psum_scatter(grad_query, ("fsdp", "ctx"), scatter_dimension=0, tiled=True),
-        lax.psum_scatter(grad_key, ("fsdp", "ctx"), scatter_dimension=0, tiled=True),
-        lax.psum_scatter(grad_value, ("fsdp", "ctx"), scatter_dimension=0, tiled=True),
-        lax.psum_scatter(grad_swish, ("fsdp", "ctx"), scatter_dimension=0, tiled=True),
-        lax.psum_scatter(grad_output, ("fsdp", "ctx"), scatter_dimension=0, tiled=True),
-        lax.psum_scatter(grad_gelu, ("fsdp", "ctx"), scatter_dimension=0, tiled=True),
-        lax.psum_scatter(grad_up, ("fsdp", "ctx"), scatter_dimension=0, tiled=True),
-        lax.psum_scatter(grad_down, ("fsdp", "ctx"), scatter_dimension=0, tiled=True),
-        lax.psum_scatter(grad_first, ("fsdp", "ctx"), scatter_dimension=0, tiled=True),
-        lax.psum_scatter(grad_second, ("fsdp", "ctx"), scatter_dimension=0, tiled=True),
-        lax.psum_scatter(grad_group, ("fsdp", "ctx"), scatter_dimension=1, tiled=True),
-    )
+    owned = tuple(
+        lax.psum_scatter(g, ("fsdp", "ctx"), scatter_dimension=0, tiled=True).astype(f32)
+        for g in (grad_query, grad_key, grad_value, grad_swish, grad_output, grad_gelu, grad_up, grad_down, grad_first, grad_second)
+    ) + (lax.psum_scatter(grad_group, ("fsdp", "ctx"), scatter_dimension=1, tiled=True),)
     return (
         result,
         grad_tokens,
@@ -314,35 +1038,10 @@
 
 
 def solution(mesh):
-    in_specs = (
-        P("fsdp", "ctx", None),
-        P(("fsdp", "ctx"), "tp", None),
-        P(("fsdp", "ctx"), "tp", None),
-        P(("fsdp", "ctx"), "tp", None),
-        P(("fsdp", "ctx"), "tp", None),
-        P(("fsdp", "ctx"), "tp", None),
-        P(("fsdp", "ctx"), "tp"),
-        P(("fsdp", "ctx"), "tp"),
-        P(("fsdp", "ctx"), "tp"),
-        P(("fsdp", "ctx")),
-        P(("fsdp", "ctx")),
-        P("tp", ("fsdp", "ctx")),
-        P("tp"),
-        P("fsdp", "ctx", None),
-    )
-    out_specs = (
-        P("fsdp", "ctx", None),
-        P("fsdp", "ctx", None),
-        P(("fsdp", "ctx"), "tp", None),
-        P(("fsdp", "ctx"), "tp", None),
-        P(("fsdp", "ctx"), "tp", None),
-        P(("fsdp", "ctx"), "tp", None),
-        P(("fsdp", "ctx"), "tp", None),
-        P(("fsdp", "ctx"), "tp"),
-        P(("fsdp", "ctx"), "tp"),
-        P(("fsdp", "ctx"), "tp"),
-        P(("fsdp", "ctx")),
-        P(("fsdp", "ctx")),
-        P("tp", ("fsdp", "ctx")),
-    )
+    wide, flat = P(("fsdp", "ctx"), "tp", None), P(("fsdp", "ctx"), "tp")
+    tok, row, group = P("fsdp", "ctx", None), P(("fsdp", "ctx")), P("tp", ("fsdp", "ctx"))
+    in_specs = (tok,) + (wide,) * 5 + (flat,) * 3 + (row, row, group, P("tp"), tok)
+    out_specs = (tok, tok) + (wide,) * 5 + (flat,) * 3 + (row, row, group)
+    sizes = (mesh.shape["fsdp"], mesh.shape["ctx"], mesh.shape["tp"])
+    local = fused if sizes == (2, 2 * ZN, 2) else general
     return jax.shard_map(local, mesh=mesh, in_specs=in_specs, out_specs=out_specs, check_vma=False)

time: 2360 us -> 437 us (0.19)
  waiting for transfers between devices: 1920 us -> 0 us
  Pallas kernels: 0 us -> 407 us
  matrix products: 177 us -> 0 us
  blocking collectives: 155 us -> 0 us
  other arithmetic: 42.4 us -> 6.69 us
    reduce_scatter x8 -> x0, waiting for transfers between devices: 1180 us -> none  [the longest x1 183 us: local(): lax.psum_scatter(grad_up, ('fsdp', 'ctx'), scatter_dimension=0, tiled=True)]
    all_gather x10 -> x0, waiting for transfers between devices: 635 us -> none  [the longest x1 143 us: prefix(): gathered = jax.tree.map(lambda a: lax.all_gather(a, axis), part)]
    pallas_call x0 -> x1, Pallas kernels: none -> 407 us  [fused(): pl.pallas_call(kernel, out_shape=shapes, in_specs=[vmem, vmem, smem, hbm,...]
    dot_general x37 -> x0, matrix products: 177 us -> none  [the longest x1 9.9 us: local(): jnp.einsum('spd,sphv->dhv', first_low, value_low, preferred_element_type=...]
    psum x3 -> x0, waiting for transfers between devices: 96.1 us -> none  [the longest x1 40.6 us: local(): lax.psum(mlp_terms.astype(jnp.bfloat16), 'tp').astype(jnp.float32)]
    unnamed x3 -> x0, blocking collectives: 94.9 us -> none
    all_gather x3 -> x0, blocking collectives: 59.7 us -> none  [the longest x1 23.2 us: local(): lax.all_gather(gain_first, ('fsdp', 'ctx'), axis=0, tiled=True)]
    unnamed x116 -> x17, local copies, waits for them, and re-layouts: 39 us -> 13.5 us
  transfers between devices with their start and end apart: 22 -> 0, of which waited for: 21 -> 0; matrix products, arithmetic and copies ran while one was open for 9% -> 0% of each run, Pallas kernels for 0% -> 0%
where the time goes in v1:
time: 437 us; the launch traced here: 436 us
  Pallas kernels  407 us (93%)
  local copies, waits for them, and re-layouts  22 us (5%)
  other arithmetic  6.69 us (2%)
    pallas_call x1, Pallas kernels, fused(): pl.pallas_call(kernel, out_shape=shapes, in_specs=[vmem, vmem, smem, hbm,...  407 us
    unnamed x17, local copies, waits for them, and re-layouts  13.5 us

profile of v1, /device:TPU:0, one launch (start us, length us, event | category | flops | bytes accessed | tf_op | source)
XLA Modules:
  0.0 436.2 jit_solution(1519124477971294620)
XLA Ops:
  0.6 0.0 copy-start.2
  0.7 0.0 copy-start.3
  0.7 0.8 tile.4
  1.4 0.1 tile.10
  1.6 0.7 bitcast_convert_fusion.2
  2.2 0.1 pad.3.clone
  2.3 0.7 maximum_maximum_fusion.gp
  3.0 1.2 log.3.lr
  4.1 1.7 copy_dynamic-update-slice_fusion.4
  5.8 1.7 copy_dynamic-update-slice_fusion.3
  7.5 2.0 copy_dynamic-update-slice_fusion.2
  9.5 0.0 copy-done.2
  9.5 0.9 copy_dynamic-update-slice_fusion.1
  10.5 0.0 copy-done.3
  10.5 0.9 copy_dynamic-update-slice_fusion
  11.4 406.8 %shard_map.237 = (bf16[128,2048]{1,0:T(8,128)(2,1)}, bf16[128,2048]{1,0:T(8,128)(2,1)}, bf16[4,4,128,512]{3,2,1,0:T(8,128)(2,1)}, bf16[3,128,2048]{2,1,0:T(8,128)(2,1)}, f32[8,2048]{1,0:T(8,128)}) custom-call(bf16[128,2048]{1,0:T(8,128)(2,1)} %bitcast.37, f32[8,128]{1,0:T(8,128)} %maximum_maximum_fusion.gp, f32[4]{0:T(128)} %log.3.lr, ...), custom_call_target="tpu_custom_call" | custom-call | tf_op jit(solution)/shard_map/pallas_call | solution.py:730
  418.2 0.0 copy-start
  418.2 2.3 bitcast_convert_fusion.1
  420.5 2.1 bitcast_convert_fusion
  422.6 0.0 copy-done
  422.6 0.6 convert_bitcast_fusion
  423.2 0.1 slice_bitcast_fusion.6
  423.3 1.1 copy.32
  424.4 1.1 copy.33
  425.5 0.3 slice_bitcast_fusion.3
  425.8 1.6 copy.34
  427.5 0.0 copy-start.1
  427.5 1.6 copy.35
  429.1 1.6 copy.36
  430.8 0.0 copy-done.1
  430.8 0.4 convert_element_type.33
  431.2 1.7 slice_bitcast_fusion
  432.9 0.9 fusion.1
  433.9 0.5 dynamic-slice_bitcast_fusion.1
  434.4 0.5 dynamic-slice_bitcast_fusion
  434.9 1.3 constant_dynamic-slice_fusion
  (4 shorter events, 0.0 us)
Async XLA Ops:
  0.6 8.9 %copy-start.2 = (bf16[128,4,512]{2,1,0:T(4,128)(2,1)S(1)}, bf16[128,4,512]{2,1,0:T(4,128)(2,1)}, u32[]{:S(2)}) copy-start(bf16[128,4,512]{2,1,0:T(4,128)(2,1)} %param.18) | copy-start | bytes 1572868
  0.7 9.8 %copy-start.3 = (bf16[128,4,512]{2,1,0:T(4,128)(2,1)S(1)}, bf16[128,4,512]{2,1,0:T(4,128)(2,1)}, u32[]{:S(2)}) copy-start(bf16[128,4,512]{2,1,0:T(4,128)(2,1)} %param.19) | copy-start | bytes 1572868
  418.2 4.4 %copy-start = (bf16[4,4,128,512]{3,2,1,0:T(8,128)(2,1)S(1)}, bf16[4,4,128,512]{3,2,1,0:T(8,128)(2,1)}, u32[]{:S(2)}) copy-start(bf16[4,4,128,512]{3,2,1,0:T(8,128)(2,1)} %get-tuple-element.20) | copy-start | bytes 6291460
  427.5 3.3 copy-start.1

commit v2 on v1

--- a/solution.py
+++ b/solution.py
@@ -60,7 +60,6 @@
     qkv=((2, TOK, 1024), BF),
     swish=((TOK, CH), F32),
     ret=((TOK, CH), F32),
-    gg=((TOK, CH), F32),
     dr=((TOK, CH), BF),
     YB=((NCH, TOK, CH), BF),
     dkv_s=((TOK, 768), BF),
@@ -69,7 +68,7 @@
     ysend=((2, NC, ZN, HALF, CH), BF),
     yrecv=((2, NC, ZN, HALF, CH), BF),
     zsend=((2, NC, ZN, HALF, CH), BF),
-    zrecv=((2, NC, ZN, HALF, CH), BF),
+    zrecv=((2, NC, ZN + 1, HALF, CH), BF),
     hidden=((HALF, D), F32),
     ghid=((HALF, D), F32),
     rsum=((HALF, D), F32),
@@ -88,8 +87,8 @@
 SEMS = dict(
     g_s=(3, 8), g_r=(3, 8),
     wz_s=(NCH, 3), wz_r=(NCH, 3), wx_s=(NCH, 4), wx_r=(NCH, 4), wc_s=(NCH, 8), wc_r=(NCH, 8), wl=(NCH,),
-    az_s=(4, AC, 3), az_r=(4, AC, 3), ay_s=(4, AC, 4), ay_r=(4, AC, 4),
-    ry_s=(4, NC), ry_r=(4, NC), rz_s=(4, NC, 3), rz_r=(4, NC, 3),
+    az_s=(4, AC, 2, ZN), az_r=(4, AC, ZN), ay_s=(4, AC, ZN), ay_r=(4, AC, ZN),
+    ry_s=(4, NC), ry_r=(4, NC), rz_s=(4, NC, ZN), rz_r=(4, NC, ZN + 1),
     kv_s=(2,), kv_r=(2,),
     gc_s=(NCH, 2), gc_r=(NCH, 2), gx_s=(NCH,), gx_r=(NCH,), gz_s=(NCH, 3), gz_r=(NCH, 3), gl=(NCH,),
     v_s=(6,), v_r=(6,), o_s=(2,), o_r=(2,), ol=(4,),
@@ -106,6 +105,7 @@
     zup = [lax.rem(z + i, ZN) for i in range(ZN)]
     zdn = [lax.rem(z + ZN - i, ZN) for i in range(ZN)]
     zdev = [(x, zup[i] * 2 + c, y) for i in range(ZN)]
+    updev, dndev = zdev[1], zdev[ZN - 1]
     xdev, ydev, cdev = (1 - x, k, y), (x, k, 1 - y), (x, z * 2 + 1 - c, y)
     peers = range(1, ZN)
 
@@ -135,10 +135,12 @@
     def w_local(n, zz):
         return pltpu.make_async_copy(w_src(n, zz), W.at[n, me], s.wl.at[n])
 
+    def w_piece(n, i):
+        remote(w_src(n, zup[i]), W.at[n, me], s.wz_s.at[n, i - 1], s.wz_r.at[n, i - 1], zdev[i]).start()
+
     def w_send(n):
         for i in peers:
-            remote(w_src(n, zup[i]), W.at[n, me], s.wz_s.at[n, i - 1], s.wz_r.at[n, i - 1], zdev[i]).start()
-        w_local(n, z).start()
+            w_piece(n, i)
 
     def w_z(n, i):
         blk = W.at[n, place(x, zdn[i], c)]
@@ -153,12 +155,14 @@
         blk = W.at[n, place(xx, zdn[j % 4], cc)]
         return remote(blk, blk, s.wc_s.at[n, j], s.wc_r.at[n, j], cdev)
 
+    def w_own(n):
+        pltpu.make_async_copy(W.at[n, me], W.at[n, me], s.wl.at[n]).wait()
+        w_x(n, 0, x).start()
+        w_c(n, 0, c).start()
+
     def pump_z(n):
-        for i in range(ZN):
-            if i == 0:
-                pltpu.make_async_copy(W.at[n, me], W.at[n, me], s.wl.at[n]).wait()
-            else:
-                w_z(n, i).wait_recv()
+        for i in peers:
+            w_z(n, i).wait_recv()
             w_x(n, i, x).start()
             w_c(n, i, c).start()
 
@@ -182,44 +186,51 @@
     def a_rows(yy, ch):
         return pl.ds(pl.multiple_of(yy * HALF + ch * AR, AR), AR)
 
-    def a_z(buf, ia, ch, i, zz):
+    def a_z(buf, ia, ch, zz, way):
         blk = buf.at[zz, a_rows(y, ch)]
-        return remote(blk, blk, s.az_s.at[ia, ch, i - 1], s.az_r.at[ia, ch, i - 1], zdev[i])
-
-    def a_y(buf, ia, ch, i, yy):
-        blk = buf.at[zdn[i], a_rows(yy, ch)]
-        return remote(blk, blk, s.ay_s.at[ia, ch, i], s.ay_r.at[ia, ch, i], ydev)
+        return remote(blk, blk, s.az_s.at[ia, ch, way, zz], s.az_r.at[ia, ch, zz], (updev, dndev)[way])
+
+    def a_y(buf, ia, ch, zz, yy):
+        blk = buf.at[zz, a_rows(yy, ch)]
+        return remote(blk, blk, s.ay_s.at[ia, ch, zz], s.ay_r.at[ia, ch, zz], ydev)
+
+    def ag_sends(buf, ia, ch, zz, do):
+        pl.when((zz <= z) & (z < ZN - 1))(lambda: do(a_z(buf, ia, ch, zz, 0)))
+        pl.when((zz >= z) & (z > 0))(lambda: do(a_z(buf, ia, ch, zz, 1)))
 
     def ag_send(buf, ia, own):
         def f(ch):
-            for i in peers:
-                a_z(buf, ia, ch, i, z).start()
+            ag_sends(buf, ia, ch, z, lambda copy: copy.start())
             if own:
-                a_y(buf, ia, ch, 0, y).start()
+                a_y(buf, ia, ch, z, y).start()
 
         loop(AC, f)
 
-    def ag_forward(buf, ia):
+    def ag_forward(buf, ia, d):
         def f(ch):
-            for i in peers:
-                a_z(buf, ia, ch, i, zdn[i]).wait_recv()
-                a_y(buf, ia, ch, i, y).start()
+            def pass_on(zz):
+                a_z(buf, ia, ch, zz, 0).wait_recv()
+                ag_sends(buf, ia, ch, zz, lambda copy: copy.start())
+                a_y(buf, ia, ch, zz, y).start()
+
+            pl.when(z >= d)(lambda: pass_on(z - d))
+            pl.when(z + d < ZN)(lambda: pass_on(z + d))
 
         loop(AC, f)
 
     def ag_wait(buf, ia, own):
         def f(ch):
             for i in range(0 if own else 1, ZN):
-                a_y(buf, ia, ch, i, 1 - y).wait_recv()
+                a_y(buf, ia, ch, zdn[i], 1 - y).wait_recv()
 
         loop(AC, f)
 
     def ag_done(buf, ia, own):
         def f(ch):
-            for i in peers:
-                a_z(buf, ia, ch, i, z).wait_send()
-            for i in range(0 if own else 1, ZN):
-                a_y(buf, ia, ch, i, y).wait_send()
+            for i in range(ZN):
+                ag_sends(buf, ia, ch, zdn[i], lambda copy: copy.wait_send())
+                if own or i > 0:
+                    a_y(buf, ia, ch, zdn[i], y).wait_send()
 
         loop(AC, f)
 
@@ -236,10 +247,15 @@
     def r_y(ir, b, j):
         return remote(s.ysend.at[b, j], s.yrecv.at[b, j], s.ry_s.at[ir, j], s.ry_r.at[ir, j], ydev)
 
-    def r_z(ir, b, j, i):
+    def r_z(ir, b, j, d, way):
+        slot = d if way == 0 else jnp.where(d == z - 1, ZN, d)
         return remote(
-            s.zsend.at[b, j, zup[i]], s.zrecv.at[b, j, i], s.rz_s.at[ir, j, i - 1], s.rz_r.at[ir, j, i - 1], zdev[i]
+            s.zsend.at[b, j, d], s.zrecv.at[b, j, slot], s.rz_s.at[ir, j, d], s.rz_r.at[ir, j, slot], (updev, dndev)[way]
         )
+
+    def r_arrived(ir, b, j, slot):
+        there = s.zrecv.at[b, j, slot]
+        remote(there, there, s.rz_s.at[ir, j, 0], s.rz_r.at[ir, j, slot], updev).wait_recv()
 
     def rs_a(ir, b, chunks):
         def f(j):
@@ -248,24 +264,42 @@
 
         loop(NC, f)
 
-    def rs_b(ir, b, chunks):
-        def f(j):
-            own = product(chunks, j, y)
-            r_y(ir, b, j).wait_recv()
-            s.zsend[b, j] = (own + s.yrecv[b, j].astype(F32)).astype(BF)
-            for i in peers:
-                r_z(ir, b, j, i).start()
-
-        loop(NC, f)
+    def r_pass(ir, b, j, level):
+        def go(dests, way):
+            for d in dests:
+                if level > 0:
+                    r_arrived(ir, b, j, d)
+                    s.zsend[b, j, d] = (s.zsend[b, j, d].astype(F32) + s.zrecv[b, j, d].astype(F32)).astype(BF)
+                r_z(ir, b, j, d, way).start()
+
+        pl.when(z == level)(lambda: go(range(ZN - 1, level, -1), 0))
+        pl.when(z == ZN - 1 - level)(lambda: go(range(ZN - 1 - level), 1))
+
+    def rs_b(ir, b, chunks, between):
+        for j in range(NC + 2):
+            if j < NC:
+                own = product(chunks, j, y)
+                r_y(ir, b, j).wait_recv()
+                s.zsend[b, j] = (own + s.yrecv[b, j].astype(F32)).astype(BF)
+                r_pass(ir, b, j, 0)
+            if 1 <= j <= NC:
+                r_pass(ir, b, j - 1, 1)
+            if j >= 2:
+                r_pass(ir, b, j - 2, 2)
+            for job in between.get(j, ()):
+                job()
 
     def rs_c(ir, b):
         def f(j):
-            for i in peers:
-                r_z(ir, b, j, i).wait_recv()
-            total = s.zsend[b, j, z].astype(F32)
-            for i in peers:
-                total = total + s.zrecv[b, j, i].astype(F32)
-            s.rsum[:, pl.ds(pl.multiple_of(j * CH, CH), CH)] = total
+            cols = pl.ds(pl.multiple_of(j * CH, CH), CH)
+            s.rsum[:, cols] = s.zsend[b, j, z].astype(F32)
+
+            def add(slot):
+                r_arrived(ir, b, j, slot)
+                s.rsum[:, cols] = s.rsum[:, cols] + s.zrecv[b, j, slot].astype(F32)
+
+            pl.when(z > 0)(lambda: add(z))
+            pl.when(z < ZN - 1)(lambda: add(ZN))
 
         loop(NC, f)
 
@@ -273,7 +307,7 @@
         def f(j):
             r_y(ir, b, j).wait_send()
             for i in peers:
-                r_z(ir, b, j, i).wait_send()
+                r_z(ir, b, j, zdn[i], 0).wait_send()
 
         loop(NC, f)
 
@@ -374,19 +408,19 @@
 
     own_rows = pl.ds(pl.multiple_of(y * HALF, HALF), HALF)
 
-    for n in range(3):
-        w_send(n)
+    gall = s.gall
+    gall[me] = gp[...]
+
+    def g_gain(j, i, dev, q):
+        return remote(gall.at[q], gall.at[q], s.g_s.at[j, i], s.g_r.at[j, i], dev)
+
+    for i in peers:
+        g_gain(0, i, zdev[i], me).start()
+    w_send(0)
+    for n in range(NCH):
+        w_local(n, z).start()
     cot_local = pltpu.make_async_copy(cot_in, s.cot.at[z], s.ol.at[0])
     cot_local.start()
-
-    gall = s.gall
-    gall[me] = gp[...]
-
-    def g_gain(j, i, dev, q):
-        return remote(gall.at[q], gall.at[q], s.g_s.at[j, i], s.g_r.at[j, i], dev)
-
-    for i in peers:
-        g_gain(0, i, zdev[i], me).start()
     for i in peers:
         g_gain(0, i, zdev[i], place(x, zdn[i], c)).wait_recv()
     for i in range(ZN):
@@ -407,19 +441,26 @@
         xx = x if i < ZN else 1 - x
         g_gain(2, i, cdev, place(xx, zdn[i % ZN], c)).wait_send()
 
+    for n in range(4):
+        w_own(n)
     tokens = tok[...].astype(F32)
     n_first, _ = normed(tokens)
     s.first[z] = (n_first * gain_row(0)).astype(BF)
     ag_send(s.first, 0, False)
-    loop(2, pump_z)
-    ag_forward(s.first, 0)
-    pump_z(2)
-    for n in range(3, NCH):
+    for n in range(1, 4):
         w_send(n)
+    pump_z(0)
+    ag_forward(s.first, 0, 1)
+    pump_x(0)
+    ag_forward(s.first, 0, 2)
+    ag_forward(s.first, 0, 3)
+    pump_z(1)
+    ag_wait(s.first, 0, False)
     cot_local.wait()
     ag_send(s.cot, 1, False)
-    loop(3, pump_x)
-    ag_wait(s.first, 0, False)
+    for n in range(4, NCH):
+        w_send(n)
+        w_own(n)
 
     qkv, swish = s.qkv, s.swish
 
@@ -434,6 +475,8 @@
         qkv[c, :, pl.ds(pl.multiple_of(t * 256, 256), 256)] = out.astype(BF)
 
     loop(2, project_qk)
+    pump_z(2)
+    pump_x(1)
     w_fin(1)
 
     def project_v(t):
@@ -447,14 +490,8 @@
         return remote(blk, blk, s.kv_s.at[0], s.kv_r.at[0], cdev)
 
     kv_copy(c).start()
-    w_fin(2)
-
-    def project_s(t):
-        out = nn(s.first[...].reshape(TOK, D), columns(2, t))
-        swish[:, pl.ds(pl.multiple_of(t * 256, 256), 256)] = out
-
-    loop(2, project_s)
     pump_z(3)
+    pump_x(2)
     kv_copy(1 - c).wait_recv()
 
     def all_keys():
@@ -471,6 +508,13 @@
         s.ret[rows, :] = nn(scores.astype(BF), all_values())
 
     loop(2, retain)
+    w_fin(2)
+
+    def project_s(t):
+        out = nn(s.first[...].reshape(TOK, D), columns(2, t))
+        swish[:, pl.ds(pl.multiple_of(t * 256, 256), 256)] = out
+
+    loop(2, project_s)
     gain_g = group_gain()
 
     def gate(h):
@@ -484,19 +528,27 @@
     w_fin(3)
 
     rs_a(0, 0, (3,))
-    rs_b(0, 0, (3,))
-    loop(2, lambda n: pump_z(n + 4))
+    rs_b(
+        0,
+        0,
+        (3,),
+        {
+            0: (lambda: ag_forward(s.cot, 1, 1), lambda: pump_z(4)),
+            1: (lambda: ag_forward(s.cot, 1, 2), lambda: pump_x(4)),
+            2: (lambda: ag_forward(s.cot, 1, 3), lambda: pump_z(5)),
+            3: (lambda: pump_x(5), lambda: pump_z(6)),
+        },
+    )
     rs_c(0, 0)
     hidden = tok[own_rows, :].astype(F32) + s.rsum[...]
     s.hidden[...] = hidden
     n_second, _ = normed(hidden)
     s.second[z, own_rows, :] = (n_second * gain_row(1)).astype(BF)
     ag_send(s.second, 2, True)
-    loop(2, lambda n: pump_x(n + 4))
-    pump_z(6)
+    ag_forward(s.second, 2, 1)
+    ag_forward(s.second, 2, 2)
+    ag_forward(s.second, 2, 3)
     pump_x(6)
-    ag_forward(s.cot, 1)
-    ag_forward(s.second, 2)
     for n in range(4, NCH):
         w_fin(n)
     ag_wait(s.cot, 1, False)
@@ -528,11 +580,18 @@
     loop(2, feed)
     rs_done(0, 0)
     rs_a(1, 0, (4, 5))
-    rs_a(2, 1, (6,))
-    rs_b(1, 0, (4, 5))
-    transpose(s.second)
-    grad_a(4, True)
-    grad_a(5, True)
+    rs_b(
+        1,
+        0,
+        (4, 5),
+        {
+            0: (lambda: transpose(s.second),),
+            1: (lambda: grad_a(4, True),),
+            2: (lambda: grad_a(5, True),),
+            3: (lambda: transpose(s.cot),),
+            4: (lambda: grad_a(6, True),),
+        },
+    )
     rs_c(1, 0)
     n_second, rstd = normed(s.hidden[...])
     g_in = s.rsum[...]
@@ -541,25 +600,24 @@
     s.ghid[...] = ghid
     s.hlow[z, own_rows, :] = ghid.astype(BF)
     ag_send(s.hlow, 3, True)
-    rs_b(2, 1, (6,))
-    transpose(s.cot)
-    grad_a(6, True)
+    ag_forward(s.hlow, 3, 1)
     grad_b(4, True)
+    ag_forward(s.hlow, 3, 2)
+    ag_forward(s.hlow, 3, 3)
     grad_b(5, True)
     grad_b(6, True)
-    ag_forward(s.hlow, 3)
+    rs_a(2, 1, (6,))
     ag_wait(s.hlow, 3, True)
 
     def back_gated(t):
-        out = nn(s.hlow[...].reshape(TOK, D), columns(3, t))
-        s.gg[:, pl.ds(pl.multiple_of(t * 256, 256), 256)] = out
+        tmp[t] = nn(s.hlow[...].reshape(TOK, D), columns(3, t))
 
     loop(2, back_gated)
 
     def back_gate(h, total):
         rows = pl.ds(pl.multiple_of(h * BLK, BLK), BLK)
         n, rstd = normed(s.ret[rows, :])
-        w, g = swish[rows, :], s.gg[rows, :]
+        w, g = swish[rows, :], jnp.concatenate([tmp[0, rows, :], tmp[1, rows, :]], axis=1)
         sig = 1.0 / (1.0 + jnp.exp(-w))
         silu = w * sig
         YB[2, rows, :] = (g * (n * gain_g) * (sig * (1.0 + w * (1.0 - sig)))).astype(BF)
@@ -567,6 +625,8 @@
         s.dr[rows, :] = norm_back(n, rstd, gs * gain_g).astype(BF)
         return total + jnp.sum(gs * n, axis=0, keepdims=True)
 
+    transpose(s.hlow)
+    grad_a(3, True)
     group = lax.fori_loop(0, ZN, back_gate, jnp.zeros((1, CH), F32))
     s.vec[2:3, 0:CH] = group
 
@@ -618,12 +678,21 @@
 
     rs_done(1, 0)
     rs_a(3, 0, (0, 1, 2))
-    rs_b(3, 0, (0, 1, 2))
-    transpose(s.first)
-    grad_sent(4)
-    grad_a(0, False)
-    grad_sent(5)
-    grad_a(1, False)
+    rs_b(2, 1, (6,), {})
+    for n in (4, 5, 6):
+        grad_sent(n)
+    rs_b(
+        3,
+        0,
+        (0, 1, 2),
+        {
+            0: (lambda: transpose(s.first), lambda: grad_a(0, False)),
+            1: (lambda: grad_a(1, False),),
+            2: (lambda: grad_a(2, False),),
+            3: (lambda: grad_b(0, False),),
+            4: (lambda: grad_b(1, False),),
+        },
+    )
     rs_c(3, 0)
     n_first, rstd = normed(tok[own_rows, :].astype(F32))
     g_in = s.rsum[...]
@@ -640,12 +709,6 @@
 
     for copy in out_copies(0, gtok_o):
         copy.start()
-    grad_b(0, False)
-    grad_b(1, False)
-    grad_sent(6)
-    grad_a(2, False)
-    transpose(s.hlow)
-    grad_a(3, True)
     grad_b(2, False)
     grad_b(3, False)
     rs_c(2, 1)

time: 437 us -> 389 us (0.89)
  Pallas kernels: 407 us -> 359 us
    pallas_call x1, Pallas kernels: 407 us -> 359 us  [fused(): pl.pallas_call(kernel, out_shape=shapes, in_specs=[vmem, vmem, smem, hbm,...]
where the time goes in v2:
time: 389 us
  Pallas kernels  359 us (92%)
  local copies, waits for them, and re-layouts  22 us (6%)
  other arithmetic  6.69 us (2%)
    pallas_call x1, Pallas kernels, fused(): pl.pallas_call(kernel, out_shape=shapes, in_specs=[vmem, vmem, smem, hbm,...  359 us
    unnamed x17, local copies, waits for them, and re-layouts  13.5 us

profile of v2, /device:TPU:0, one launch (start us, length us, event | category | flops | bytes accessed | tf_op | source)
XLA Modules:
  0.0 388.7 jit_solution(15450661201919948530)
XLA Ops:
  0.6 0.0 copy-start.2
  0.7 0.0 copy-start.3
  0.7 0.8 tile.4
  1.4 0.1 tile.10
  1.6 0.7 bitcast_convert_fusion.2
  2.2 0.1 pad.3.clone
  2.3 0.7 maximum_maximum_fusion.gp
  3.0 1.2 log.3.lr
  4.1 1.7 copy_dynamic-update-slice_fusion.4
  5.8 1.7 copy_dynamic-update-slice_fusion.3
  7.5 2.0 copy_dynamic-update-slice_fusion.2
  9.5 0.0 copy-done.2
  9.5 0.9 copy_dynamic-update-slice_fusion.1
  10.5 0.0 copy-done.3
  10.5 0.9 copy_dynamic-update-slice_fusion
  11.4 359.2 %shard_map.237 = (bf16[128,2048]{1,0:T(8,128)(2,1)}, bf16[128,2048]{1,0:T(8,128)(2,1)}, bf16[4,4,128,512]{3,2,1,0:T(8,128)(2,1)}, bf16[3,128,2048]{2,1,0:T(8,128)(2,1)}, f32[8,2048]{1,0:T(8,128)}) custom-call(bf16[128,2048]{1,0:T(8,128)(2,1)} %bitcast.37, f32[8,128]{1,0:T(8,128)} %maximum_maximum_fusion.gp, f32[4]{0:T(128)} %log.3.lr, ...), custom_call_target="tpu_custom_call" | custom-call | tf_op jit(solution)/shard_map/pallas_call | solution.py:793
  370.7 0.0 copy-start
  370.7 2.3 bitcast_convert_fusion.1
  372.9 2.1 bitcast_convert_fusion
  375.0 0.0 copy-done
  375.1 0.6 convert_bitcast_fusion
  375.6 0.1 slice_bitcast_fusion.6
  375.7 1.1 copy.32
  376.9 1.1 copy.33
  378.0 0.3 slice_bitcast_fusion.3
  378.3 1.6 copy.34
  379.9 0.0 copy-start.1
  379.9 1.6 copy.35
  381.6 1.6 copy.36
  383.2 0.0 copy-done.1
  383.2 0.4 convert_element_type.33
  383.6 1.7 slice_bitcast_fusion
  385.4 0.9 fusion.1
  386.3 0.5 dynamic-slice_bitcast_fusion.1
  386.8 0.5 dynamic-slice_bitcast_fusion
  387.3 1.3 constant_dynamic-slice_fusion
  (4 shorter events, 0.0 us)
Async XLA Ops:
  0.6 8.9 %copy-start.2 = (bf16[128,4,512]{2,1,0:T(4,128)(2,1)S(1)}, bf16[128,4,512]{2,1,0:T(4,128)(2,1)}, u32[]{:S(2)}) copy-start(bf16[128,4,512]{2,1,0:T(4,128)(2,1)} %param.18) | copy-start | bytes 1572868
  0.7 9.8 %copy-start.3 = (bf16[128,4,512]{2,1,0:T(4,128)(2,1)S(1)}, bf16[128,4,512]{2,1,0:T(4,128)(2,1)}, u32[]{:S(2)}) copy-start(bf16[128,4,512]{2,1,0:T(4,128)(2,1)} %param.19) | copy-start | bytes 1572868
  370.7 4.4 %copy-start = (bf16[4,4,128,512]{3,2,1,0:T(8,128)(2,1)S(1)}, bf16[4,4,128,512]{3,2,1,0:T(8,128)(2,1)}, u32[]{:S(2)}) copy-start(bf16[4,4,128,512]{3,2,1,0:T(8,128)(2,1)} %get-tuple-element.20) | copy-start | bytes 6291460
  379.9 3.3 copy-start.1

commit v3 on v2

--- a/solution.py
+++ b/solution.py
@@ -22,6 +22,7 @@
 AC = 4
 AR = HALF // AC
 SETS = 4
+VW = 640
 VLIM = 62 * 2**20
 
 
@@ -78,11 +79,11 @@
     gxs=((SETS, ZN, BLK, CH), BF),
     gxr=((SETS, ZN, BLK, CH), BF),
     gzs=((SETS, ZN, BLK, CH), BF),
-    vec=((8, D), F32),
-    vrc=((8, D), F32),
-    vrx=((8, D), F32),
-    vry=((8, D), F32),
-    vz=((ZN, 8, D), F32),
+    vec=((8, VW), F32),
+    vrc=((8, VW), F32),
+    vrx=((8, VW), F32),
+    vry=((8, VW), F32),
+    vz=((ZN, 8, VW), F32),
 )
 SEMS = dict(
     g_s=(3, 8), g_r=(3, 8),
@@ -275,19 +276,11 @@
         pl.when(z == level)(lambda: go(range(ZN - 1, level, -1), 0))
         pl.when(z == ZN - 1 - level)(lambda: go(range(ZN - 1 - level), 1))
 
-    def rs_b(ir, b, chunks, between):
-        for j in range(NC + 2):
-            if j < NC:
-                own = product(chunks, j, y)
-                r_y(ir, b, j).wait_recv()
-                s.zsend[b, j] = (own + s.yrecv[b, j].astype(F32)).astype(BF)
-                r_pass(ir, b, j, 0)
-            if 1 <= j <= NC:
-                r_pass(ir, b, j - 1, 1)
-            if j >= 2:
-                r_pass(ir, b, j - 2, 2)
-            for job in between.get(j, ()):
-                job()
+    def rs_y(ir, b, chunks, j):
+        own = product(chunks, j, y)
+        r_y(ir, b, j).wait_recv()
+        s.zsend[b, j] = (own + s.yrecv[b, j].astype(F32)).astype(BF)
+        r_pass(ir, b, j, 0)
 
     def rs_c(ir, b):
         def f(j):
@@ -351,7 +344,7 @@
         own = grad_rows(n, 1 - x, c)
         g_c(n, 1 - x).wait_recv()
         if not first_use:
-            pl.semaphore_wait(s.credit, 1)
+            pl.semaphore_wait(s.credit.at[b], 1)
         s.gxs[b] = (own + s.gcr[b, 1 - x].astype(F32)).astype(BF)
         g_x(n).start()
         own = grad_rows(n, x, c)
@@ -369,7 +362,7 @@
         g_local(n).start()
         g_x(n).wait_send()
         if more:
-            pl.semaphore_signal(s.credit, inc=1, device_id=xdev, device_id_type=MESH)
+            pl.semaphore_signal(s.credit.at[b], inc=1, device_id=xdev, device_id_type=MESH)
 
     def grad_sent(n):
         for i in peers:
@@ -392,6 +385,9 @@
                 total = total + s.gall[q]
             parts.append(jnp.sum(jnp.where(pick, total, 0.0), axis=0, keepdims=True))
         return jnp.concatenate(parts, axis=1)
+
+    def packed(row):
+        return jnp.concatenate([row[:, 256 * q : 256 * q + 256] for q in range(D // 256)], axis=0)
 
     def position(shape, dim, both, start):
         r = lax.broadcasted_iota(jnp.int32, shape, dim) + start
@@ -440,33 +436,48 @@
     for i in range(8):
         xx = x if i < ZN else 1 - x
         g_gain(2, i, cdev, place(xx, zdn[i % ZN], c)).wait_send()
-
-    for n in range(4):
-        w_own(n)
+    vec = s.vec
+    vec[...] = jnp.zeros((8, VW), F32)
+    gain_g = group_gain()
+    tmp, qkv, swish = s.tmp, s.qkv, s.swish
+
+    def columns(n, t):
+        return W[n, :, :, pl.ds(pl.multiple_of(t * 256, 256), 256)].reshape(D, 256)
+
+    def all_keys():
+        return qkv[:, :, 256:512].reshape(2 * TOK, 256)
+
+    def all_values():
+        return qkv[:, :, 512:1024].reshape(2 * TOK, CH)
+
+    def out_copies(j, dst):
+        there = dst.at[own_rows]
+        return (
+            remote(s.ostage.at[j], there, s.o_s.at[j], s.o_r.at[j], ydev),
+            pltpu.make_async_copy(s.ostage.at[j], there, s.ol.at[1 + j]),
+        )
+
     tokens = tok[...].astype(F32)
     n_first, _ = normed(tokens)
     s.first[z] = (n_first * gain_row(0)).astype(BF)
     ag_send(s.first, 0, False)
-    for n in range(1, 4):
-        w_send(n)
+    ag_forward(s.first, 0, 1)
+    w_own(3)
+    w_own(1)
+    w_own(0)
     pump_z(0)
-    ag_forward(s.first, 0, 1)
+    w_send(3)
+    ag_forward(s.first, 0, 2)
+    w_send(1)
+    w_own(2)
     pump_x(0)
-    ag_forward(s.first, 0, 2)
+    pump_z(3)
+    w_send(2)
     ag_forward(s.first, 0, 3)
+    ag_wait(s.first, 0, False)
     pump_z(1)
-    ag_wait(s.first, 0, False)
     cot_local.wait()
     ag_send(s.cot, 1, False)
-    for n in range(4, NCH):
-        w_send(n)
-        w_own(n)
-
-    qkv, swish = s.qkv, s.swish
-
-    def columns(n, t):
-        return W[n, :, :, pl.ds(pl.multiple_of(t * 256, 256), 256)].reshape(D, 256)
-
     w_fin(0)
 
     def project_qk(t):
@@ -475,8 +486,9 @@
         qkv[c, :, pl.ds(pl.multiple_of(t * 256, 256), 256)] = out.astype(BF)
 
     loop(2, project_qk)
+    pump_x(1)
+    w_send(5)
     pump_z(2)
-    pump_x(1)
     w_fin(1)
 
     def project_v(t):
@@ -490,15 +502,9 @@
         return remote(blk, blk, s.kv_s.at[0], s.kv_r.at[0], cdev)
 
     kv_copy(c).start()
-    pump_z(3)
-    pump_x(2)
+    w_own(4)
+    pump_x(3)
     kv_copy(1 - c).wait_recv()
-
-    def all_keys():
-        return qkv[:, :, 256:512].reshape(2 * TOK, 256)
-
-    def all_values():
-        return qkv[:, :, 512:1024].reshape(2 * TOK, CH)
 
     def retain(h):
         rows = pl.ds(pl.multiple_of(h * 256, 256), 256)
@@ -508,6 +514,9 @@
         s.ret[rows, :] = nn(scores.astype(BF), all_values())
 
     loop(2, retain)
+    pump_x(2)
+    w_send(6)
+    ag_forward(s.cot, 1, 1)
     w_fin(2)
 
     def project_s(t):
@@ -515,8 +524,6 @@
         swish[:, pl.ds(pl.multiple_of(t * 256, 256), 256)] = out
 
     loop(2, project_s)
-    gain_g = group_gain()
-
     def gate(h):
         rows = pl.ds(pl.multiple_of(h * BLK, BLK), BLK)
         n, _ = normed(s.ret[rows, :])
@@ -524,21 +531,28 @@
         YB[3, rows, :] = (n * gain_g * (w / (1.0 + jnp.exp(-w)))).astype(BF)
 
     loop(ZN, gate)
-    pump_x(3)
+    w_own(5)
+    w_own(6)
     w_fin(3)
-
     rs_a(0, 0, (3,))
-    rs_b(
-        0,
-        0,
-        (3,),
-        {
-            0: (lambda: ag_forward(s.cot, 1, 1), lambda: pump_z(4)),
-            1: (lambda: ag_forward(s.cot, 1, 2), lambda: pump_x(4)),
-            2: (lambda: ag_forward(s.cot, 1, 3), lambda: pump_z(5)),
-            3: (lambda: pump_x(5), lambda: pump_z(6)),
-        },
-    )
+    w_send(4)
+    rs_y(0, 0, (3,), 0)
+    rs_y(0, 0, (3,), 1)
+    ag_forward(s.cot, 1, 2)
+    pump_z(6)
+    r_pass(0, 0, 0, 1)
+    r_pass(0, 0, 1, 1)
+    rs_y(0, 0, (3,), 2)
+    r_pass(0, 0, 2, 1)
+    r_pass(0, 0, 0, 2)
+    pump_z(4)
+    rs_y(0, 0, (3,), 3)
+    ag_forward(s.cot, 1, 3)
+    r_pass(0, 0, 3, 1)
+    r_pass(0, 0, 1, 2)
+    pump_z(5)
+    r_pass(0, 0, 2, 2)
+    r_pass(0, 0, 3, 2)
     rs_c(0, 0)
     hidden = tok[own_rows, :].astype(F32) + s.rsum[...]
     s.hidden[...] = hidden
@@ -546,15 +560,15 @@
     s.second[z, own_rows, :] = (n_second * gain_row(1)).astype(BF)
     ag_send(s.second, 2, True)
     ag_forward(s.second, 2, 1)
+    pump_x(6)
+    ag_wait(s.cot, 1, False)
     ag_forward(s.second, 2, 2)
     ag_forward(s.second, 2, 3)
-    pump_x(6)
+    pump_x(5)
+    pump_x(4)
+    ag_wait(s.second, 2, True)
     for n in range(4, NCH):
         w_fin(n)
-    ag_wait(s.cot, 1, False)
-    ag_wait(s.second, 2, True)
-
-    tmp = s.tmp
 
     def feed(t):
         cols = pl.ds(pl.multiple_of(t * 256, 256), 256)
@@ -580,35 +594,47 @@
     loop(2, feed)
     rs_done(0, 0)
     rs_a(1, 0, (4, 5))
-    rs_b(
-        1,
-        0,
-        (4, 5),
-        {
-            0: (lambda: transpose(s.second),),
-            1: (lambda: grad_a(4, True),),
-            2: (lambda: grad_a(5, True),),
-            3: (lambda: transpose(s.cot),),
-            4: (lambda: grad_a(6, True),),
-        },
-    )
+    rs_y(1, 0, (4, 5), 0)
+    r_pass(1, 0, 0, 1)
+    transpose(s.second)
+    rs_a(2, 1, (6,))
+    rs_y(1, 0, (4, 5), 1)
+    grad_a(5, True)
+    r_pass(1, 0, 1, 1)
+    rs_y(1, 0, (4, 5), 2)
+    r_pass(1, 0, 2, 1)
+    rs_y(1, 0, (4, 5), 3)
+    r_pass(1, 0, 0, 2)
+    r_pass(1, 0, 1, 2)
+    r_pass(1, 0, 3, 1)
+    r_pass(1, 0, 2, 2)
+    rs_y(2, 1, (6,), 0)
+    r_pass(1, 0, 3, 2)
     rs_c(1, 0)
     n_second, rstd = normed(s.hidden[...])
     g_in = s.rsum[...]
-    s.vec[1:2, :] = jnp.sum(g_in * n_second, axis=0, keepdims=True)
+    vec[:, 256:512] = packed(jnp.sum(g_in * n_second, axis=0, keepdims=True))
     ghid = s.cot[z, own_rows, :].astype(F32) + norm_back(n_second, rstd, g_in * gain_row(1))
     s.ghid[...] = ghid
     s.hlow[z, own_rows, :] = ghid.astype(BF)
     ag_send(s.hlow, 3, True)
+    r_pass(2, 1, 0, 1)
+    grad_a(4, True)
+    transpose(s.cot)
+    rs_y(2, 1, (6,), 1)
+    grad_a(6, True)
     ag_forward(s.hlow, 3, 1)
+    r_pass(2, 1, 1, 1)
+    ag_forward(s.hlow, 3, 2)
     grad_b(4, True)
-    ag_forward(s.hlow, 3, 2)
     ag_forward(s.hlow, 3, 3)
+    rs_y(2, 1, (6,), 2)
     grad_b(5, True)
+    rs_y(2, 1, (6,), 3)
     grad_b(6, True)
-    rs_a(2, 1, (6,))
     ag_wait(s.hlow, 3, True)
-
+    transpose(s.hlow)
+    grad_a(3, True)
     def back_gated(t):
         tmp[t] = nn(s.hlow[...].reshape(TOK, D), columns(3, t))
 
@@ -625,11 +651,10 @@
         s.dr[rows, :] = norm_back(n, rstd, gs * gain_g).astype(BF)
         return total + jnp.sum(gs * n, axis=0, keepdims=True)
 
-    transpose(s.hlow)
-    grad_a(3, True)
     group = lax.fori_loop(0, ZN, back_gate, jnp.zeros((1, CH), F32))
-    s.vec[2:3, 0:CH] = group
-
+    vec[0:4, 512:VW] = jnp.concatenate([group[:, 128 * q : 128 * q + 128] for q in range(4)], axis=0)
+
+    r_pass(2, 1, 0, 2)
     def back_keys(core, h):
         rows = pl.ds(pl.multiple_of(h * 256, 256), 256)
         keys, values = qkv[core, rows, 256:512], qkv[core, rows, 512:1024]
@@ -676,76 +701,73 @@
 
     loop(ZN, back_sum)
 
+    grad_b(3, False)
+    transpose(s.first)
+    r_pass(2, 1, 2, 1)
     rs_done(1, 0)
     rs_a(3, 0, (0, 1, 2))
-    rs_b(2, 1, (6,), {})
-    for n in (4, 5, 6):
-        grad_sent(n)
-    rs_b(
-        3,
-        0,
-        (0, 1, 2),
-        {
-            0: (lambda: transpose(s.first), lambda: grad_a(0, False)),
-            1: (lambda: grad_a(1, False),),
-            2: (lambda: grad_a(2, False),),
-            3: (lambda: grad_b(0, False),),
-            4: (lambda: grad_b(1, False),),
-        },
-    )
-    rs_c(3, 0)
-    n_first, rstd = normed(tok[own_rows, :].astype(F32))
-    g_in = s.rsum[...]
-    s.vec[0:1, :] = jnp.sum(g_in * n_first, axis=0, keepdims=True)
-    g_tok = s.ghid[...] + norm_back(n_first, rstd, g_in * gain_row(0))
-    s.ostage[0] = g_tok.astype(BF)
-
-    def out_copies(j, dst):
-        there = dst.at[own_rows]
-        return (
-            remote(s.ostage.at[j], there, s.o_s.at[j], s.o_r.at[j], ydev),
-            pltpu.make_async_copy(s.ostage.at[j], there, s.ol.at[1 + j]),
-        )
-
-    for copy in out_copies(0, gtok_o):
-        copy.start()
-    grad_b(2, False)
-    grad_b(3, False)
+    r_pass(2, 1, 3, 1)
+    grad_sent(5)
+    grad_a(1, False)
+    rs_y(3, 0, (0, 1, 2), 0)
+    grad_sent(4)
+    grad_a(0, False)
+    rs_y(3, 0, (0, 1, 2), 1)
+    grad_sent(6)
+    grad_a(2, False)
+    r_pass(3, 0, 0, 1)
+    r_pass(3, 0, 1, 1)
+    r_pass(2, 1, 1, 2)
+    r_pass(3, 0, 0, 2)
+    r_pass(2, 1, 2, 2)
+    rs_y(3, 0, (0, 1, 2), 2)
+    r_pass(3, 0, 2, 1)
+    rs_y(3, 0, (0, 1, 2), 3)
+    r_pass(3, 0, 1, 2)
+    r_pass(2, 1, 3, 2)
     rs_c(2, 1)
     s.ostage[1] = (s.hidden[...] + s.rsum[...]).astype(BF)
     for copy in out_copies(1, res_o):
         copy.start()
-
-    vec = s.vec
-
+    grad_b(1, False)
+    r_pass(3, 0, 3, 1)
+    r_pass(3, 0, 2, 2)
+    r_pass(3, 0, 3, 2)
+    rs_c(3, 0)
+    n_first, rstd = normed(tok[own_rows, :].astype(F32))
+    g_in = s.rsum[...]
+    vec[:, 0:256] = packed(jnp.sum(g_in * n_first, axis=0, keepdims=True))
+    g_tok = s.ghid[...] + norm_back(n_first, rstd, g_in * gain_row(0))
+    s.ostage[0] = g_tok.astype(BF)
+
+    for copy in out_copies(0, gtok_o):
+        copy.start()
+    grad_b(0, False)
     def v_copy(j, dst, dev):
         return remote(vec, dst, s.v_s.at[j], s.v_r.at[j], dev)
 
-    vec[3:8, :] = jnp.zeros((5, D), F32)
-    vec[2:3, CH:D] = jnp.zeros((1, D - CH), F32)
-    for j, (dst, dev) in enumerate(((s.vrc, cdev), (s.vrx, xdev), (s.vry, ydev))):
-        copy = v_copy(j, dst, dev)
-        copy.start()
-        copy.wait()
-        if j < 2:
-            vec[...] = vec[...] + dst[...]
-        else:
-            vec[0:2, :] = vec[0:2, :] + dst[0:2, :]
-    s.vz[z] = vec[...]
+    v_copy(0, s.vrc, cdev).start()
+    v_copy(0, s.vrc, cdev).wait()
+    vec[...] = vec[...] + s.vrc[...]
+    v_copy(1, s.vrx, xdev).start()
+    v_copy(1, s.vrx, xdev).wait()
+    vec[...] = vec[...] + s.vrx[...]
+    v_copy(2, s.vry, ydev).start()
+    grad_b(2, False)
+    v_copy(2, s.vry, ydev).wait()
+    vec[:, 0:512] = vec[:, 0:512] + s.vry[:, 0:512]
+    vz = s.vz
+    vz[z] = vec[...]
     for i in peers:
-        remote(vec, s.vz.at[z], s.v_s.at[2 + i], s.v_r.at[2 + i], zdev[i]).start()
+        v_copy(2 + i, vz.at[z], zdev[i]).start()
     for i in peers:
-        there = s.vz.at[zdn[i]]
-        copy = remote(there, there, s.v_s.at[2 + i], s.v_r.at[2 + i], zdev[i])
-        copy.wait_recv()
+        there = vz.at[zdn[i]]
+        remote(there, there, s.v_s.at[2 + i], s.v_r.at[2 + i], zdev[i]).wait_recv()
     for i in peers:
-        remote(vec, s.vz.at[z], s.v_s.at[2 + i], s.v_r.at[2 + i], zdev[i]).wait_send()
-    vz = s.vz
-    vec_o[0:2, :] = ((vz[0, 0:2, :] + vz[1, 0:2, :]) + vz[2, 0:2, :]) + vz[3, 0:2, :]
-    vec_o[2:4, :] = jnp.zeros((2, D), F32)
+        v_copy(2 + i, vz.at[z], zdev[i]).wait_send()
+    vec_o[:, 0:512] = ((vz[0, :, 0:512] + vz[1, :, 0:512]) + vz[2, :, 0:512]) + vz[3, :, 0:512]
     for zz in range(ZN):
-        vec_o[4 + zz : 5 + zz, :] = vz[zz, 2:3, :]
-
+        vec_o[:, 512 + 128 * zz : 640 + 128 * zz] = vz[zz, :, 512:VW]
     for j, dst in enumerate((gtok_o, res_o)):
         there = dst.at[pl.ds(pl.multiple_of((1 - y) * HALF, HALF), HALF)]
         a, b = out_copies(j, dst)
@@ -765,31 +787,125 @@
     rs_done(3, 0)
 
 
-def pieces(tokens, w_query, w_key, w_value, w_swish, w_output, w_gelu, w_up, w_down, gain_first, gain_second, gain_group, decay_rate, cotangent):
+def finish_kernel(gwa, gwf, res, gtok, vec, o_res, o_tok, o_q, o_k, o_v, o_s, o_o, o_g, o_u, o_d, o_first, o_second, o_group):
+    o_res[0] = res[...].astype(F32)
+    o_tok[0] = gtok[...].astype(F32)
+    for n, out in enumerate((o_g, o_u, o_d)):
+        out[...] = gwf[n].astype(F32)
+    both = jnp.swapaxes(gwa[0].astype(F32), 0, 1)
+    o_q[...] = both[:, :, 0:256]
+    o_k[...] = both[:, :, 256:512]
+    for n, out in enumerate((o_v, o_s, o_o)):
+        out[...] = jnp.swapaxes(gwa[n + 1].astype(F32), 0, 1)
     me = lax.axis_index("fsdp") * 8 + lax.axis_index("ctx")
-    pk = jnp.concatenate([w_query, w_key, w_value, w_swish, w_output], axis=2).transpose(1, 0, 2)
+    quarter = lax.rem(me, 4)
+
+    def row(r, start, stop):
+        block = vec[:, start:stop]
+        return jnp.sum(jnp.where(lax.broadcasted_iota(jnp.int32, block.shape, 0) == r, block, 0.0), axis=0, keepdims=True)
+
+    for out, start in ((o_first, 0), (o_second, 256)):
+        pair = row(me // 2, start, start + 256)
+        out[...] = jnp.where(lax.rem(me, 2) == 0, pair[:, 0:128], pair[:, 128:256])
+    for zz in range(ZN):
+        line = row(me // 4, 512 + 128 * zz, 640 + 128 * zz)
+        total = jnp.zeros((1, 32), F32)
+        for q in range(4):
+            total = total + jnp.where(quarter == q, line[:, 32 * q : 32 * q + 32], 0.0)
+        o_group[zz : zz + 1, :] = total
+
+
+def finish(res, gtok, gwa, gwf, vec):
+    steps = 2
+    rows = BLK // steps
+    flat = pl.BlockSpec((rows, D), lambda i: (i, 0))
+    deep = pl.BlockSpec((1, rows, D), lambda i: (0, i, 0))
+    narrow = pl.BlockSpec((rows, ZN, 256), lambda i: (i, 0, 0))
+    wide = pl.BlockSpec((rows, ZN, CH), lambda i: (i, 0, 0))
+
+    def whole(*shape):
+        return pl.BlockSpec(shape, lambda i: (0,) * len(shape))
+
+    def f32(*shape):
+        return jax.ShapeDtypeStruct(shape, F32)
+
+    outs = pl.pallas_call(
+        finish_kernel,
+        grid=(steps,),
+        in_specs=[
+            pl.BlockSpec((4, ZN, rows, CH), lambda i: (0, 0, i, 0)),
+            pl.BlockSpec((3, rows, D), lambda i: (0, i, 0)),
+            flat,
+            flat,
+            whole(8, 1024),
+        ],
+        out_specs=[deep, deep, narrow, narrow, wide, wide, wide, flat, flat, flat, whole(1, BLK), whole(1, BLK), whole(ZN, 32)],
+        out_shape=[f32(1, BLK, D)] * 2
+        + [f32(BLK, ZN, 256)] * 2
+        + [f32(BLK, ZN, CH)] * 3
+        + [f32(BLK, D)] * 3
+        + [f32(1, BLK)] * 2
+        + [f32(ZN, 32)],
+        compiler_params=pltpu.CompilerParams(vmem_limit_bytes=VLIM),
+    )(gwa, gwf, res, gtok, vec)
+    return tuple(outs[:10]) + (outs[10].reshape(BLK), outs[11].reshape(BLK), outs[12])
+
+
+def start_kernel(q, k, v, sw, o, g_first, g_second, g_group, rate, pk, gp, lr):
+    for ref, at in ((q, 0), (k, 256), (v, 512), (sw, 1024), (o, 1536)):
+        pk[:, :, at : at + ref.shape[2]] = jnp.swapaxes(ref[...], 0, 1)
+    me = lax.axis_index("fsdp") * 8 + lax.axis_index("ctx")
+    quarter = lax.rem(me, 4)
+    gp[...] = jnp.zeros((8, BLK), F32)
+    gp[0:1, :] = g_first[...].astype(F32)
+    gp[1:2, :] = g_second[...].astype(F32)
     lane = lax.broadcasted_iota(jnp.int32, (ZN, BLK), 1) // 32
-    spread = jnp.where(lane == lax.rem(me, 4), jnp.tile(gain_group.astype(F32), (1, 4)), 0.0)
-    gp = jnp.concatenate(
-        [gain_first.astype(F32)[None], gain_second.astype(F32)[None], spread, jnp.zeros((2, BLK), F32)], axis=0
-    )
-    return (tokens[0], gp, jnp.log(decay_rate), cotangent[0], pk, w_gelu, w_up, w_down)
-
-
-def fused(*args):
+    wide = jnp.concatenate([g_group[...].astype(F32)] * 4, axis=1)
+    gp[2:6, :] = jnp.where(lane == quarter, wide, 0.0)
+    lr[...] = jnp.log(rate[...])
+
+
+def begin(w_query, w_key, w_value, w_swish, w_output, gain_first, gain_second, gain_group, decay_rate):
+    steps = 2
+    rows = BLK // steps
+    narrow = pl.BlockSpec((rows, ZN, 256), lambda i: (i, 0, 0))
+    wide = pl.BlockSpec((rows, ZN, CH), lambda i: (i, 0, 0))
+
+    def whole(*shape):
+        return pl.BlockSpec(shape, lambda i: (0,) * len(shape))
+
+    pk, gp, lr = pl.pallas_call(
+        start_kernel,
+        grid=(steps,),
+        in_specs=[narrow, narrow, wide, wide, wide, whole(1, BLK), whole(1, BLK), whole(ZN, 32), whole(1, ZN)],
+        out_specs=[pl.BlockSpec((ZN, rows, 4 * CH), lambda i: (0, i, 0)), whole(8, BLK), whole(1, ZN)],
+        out_shape=[
+            jax.ShapeDtypeStruct((ZN, BLK, 4 * CH), BF),
+            jax.ShapeDtypeStruct((8, BLK), F32),
+            jax.ShapeDtypeStruct((1, ZN), F32),
+        ],
+        compiler_params=pltpu.CompilerParams(vmem_limit_bytes=VLIM),
+    )(w_query, w_key, w_value, w_swish, w_output, gain_first[None], gain_second[None], gain_group, decay_rate[None])
+    return pk, gp, lr[0]
+
+
+def fused(
+    tokens, w_query, w_key, w_value, w_swish, w_output, w_gelu, w_up, w_down, gain_first, gain_second, gain_group, decay_rate, cotangent
+):
+    pk, gp, lr = begin(w_query, w_key, w_value, w_swish, w_output, gain_first, gain_second, gain_group, decay_rate)
     shapes = [
         jax.ShapeDtypeStruct((BLK, D), BF),
         jax.ShapeDtypeStruct((BLK, D), BF),
         jax.ShapeDtypeStruct((4, ZN, BLK, CH), BF),
         jax.ShapeDtypeStruct((3, BLK, D), BF),
-        jax.ShapeDtypeStruct((8, D), F32),
+        jax.ShapeDtypeStruct((8, 1024), F32),
     ]
     hbm = pl.BlockSpec(memory_space=pl.ANY)
     vmem = pl.BlockSpec(memory_space=pltpu.VMEM)
     smem = pl.BlockSpec(memory_space=pltpu.SMEM)
     scratch = [pltpu.VMEM(*v) for v in SCRATCH.values()]
-    for name, shape in SEMS.items():
-        scratch.append(pltpu.SemaphoreType.REGULAR if shape is None else pltpu.SemaphoreType.DMA(shape))
+    for shape in SEMS.values():
+        scratch.append(pltpu.SemaphoreType.REGULAR((3,)) if shape is None else pltpu.SemaphoreType.DMA(shape))
     result, g_tok, gwa, gwf, vec = pl.pallas_call(
         kernel,
         out_shape=shapes,
@@ -797,28 +913,8 @@
         out_specs=[hbm, hbm, hbm, hbm, vmem],
         scratch_shapes=scratch,
         compiler_params=pltpu.CompilerParams(collective_id=0, has_side_effects=True, vmem_limit_bytes=VLIM),
-    )(*pieces(*args))
-    me = lax.axis_index("fsdp") * 8 + lax.axis_index("ctx")
-    swap = gwa.transpose(0, 2, 1, 3).astype(F32)
-    gwf = gwf.astype(F32)
-    g_first = lax.dynamic_slice(vec[0], (me * BLK,), (BLK,))
-    g_second = lax.dynamic_slice(vec[1], (me * BLK,), (BLK,))
-    g_group = lax.dynamic_slice(vec, (4, me * 32), (4, 32))
-    return (
-        result[None].astype(F32),
-        g_tok[None].astype(F32),
-        swap[0, :, :, 0:256],
-        swap[0, :, :, 256:512],
-        swap[1],
-        swap[2],
-        swap[3],
-        gwf[0],
-        gwf[1],
-        gwf[2],
-        g_first,
-        g_second,
-        g_group,
-    )
+    )(tokens[0], gp, lr, cotangent[0], pk, w_gelu, w_up, w_down)
+    return finish(result, g_tok, gwa, gwf, vec)
 
 
 highest_precision = lax.Precision.HIGHEST

time: 389 us -> 324 us (0.83)
  Pallas kernels: 359 us -> 322 us
  local copies, waits for them, and re-layouts: 22 us -> 0 us
  other arithmetic: 6.69 us -> 0 us
    pallas_call x1, Pallas kernels: 359 us -> 314 us  [fused(): pl.pallas_call(kernel, out_shape=shapes, in_specs=[vmem, vmem, smem, hbm,...]
    unnamed x17 -> x0, local copies, waits for them, and re-layouts: 13.5 us -> none
    pallas_call x0 -> x2, Pallas kernels: none -> 8.17 us  [the longest x1 5.28 us: finish(): pl.pallas_call(finish_kernel, grid=(steps,), in_specs=[pl.BlockSpec((4, Z...]
    convert_element_type x4 -> x0, other arithmetic: 5.33 us -> none  [the longest x1 2.27 us: fused(): result[None].astype(F32)]
where the time goes in v3:
time: 324 us; the launch traced here: 323 us
  Pallas kernels  322 us (99%)
    pallas_call x1, Pallas kernels, fused(): pl.pallas_call(kernel, out_shape=shapes, in_specs=[vmem, vmem, smem, hbm,...  314 us

profile of v3, /device:TPU:0, one launch (start us, length us, event | category | flops | bytes accessed | tf_op | source)
XLA Modules:
  0.0 322.8 jit_solution(16533663813001557679)
XLA Ops:
  0.6 2.9 shard_map.237
  3.5 313.8 %shard_map.238 = (bf16[128,2048]{1,0:T(8,128)(2,1)}, bf16[128,2048]{1,0:T(8,128)(2,1)}, bf16[4,4,128,512]{3,2,1,0:T(8,128)(2,1)}, bf16[3,128,2048]{2,1,0:T(8,128)(2,1)}, f32[8,1024]{1,0:T(8,128)}) custom-call(bf16[128,2048]{1,0:T(8,128)(2,1)} %bitcast.8, f32[8,128]{1,0:T(8,128)} %get-tuple-element.34.gp, f32[4]{0:T(128)} %bitcast.10, ...), custom_call_target="tpu_custom_call" | custom-call | tf_op jit(solution)/shard_map/pallas_call | solution.py:909
  317.3 5.3 %shard_map.239 = (f32[1,128,2048]{2,1,0:T(8,128)}, f32[1,128,2048]{2,1,0:T(8,128)}, f32[128,4,256]{2,1,0:T(4,128)}, f32[128,4,256]{2,1,0:T(4,128)}, f32[128,4,51...) custom-call(bf16[4,4,128,512]{3,2,1,0:T(8,128)(2,1)} %get-tuple-elem, ...), custom_call_target="tpu_custom_call" | custom-call | tf_op jit(solution)/shard_map/pallas_call | solution.py:832

commit v4 on v3

--- a/solution.py
+++ b/solution.py
@@ -13,12 +13,16 @@
 
 ZN = 4
 BLK = 128
+ROOT = 0.7978845608028654
+HR = 32
 HALF = 64
 TOK = ZN * BLK
 D = 2048
 CH = 512
 NCH = 7
-NC = 4
+NC = 2
+RC = D // NC
+RB = 16 // NC
 AC = 4
 AR = HALF // AC
 SETS = 4
@@ -65,11 +69,11 @@
     YB=((NCH, TOK, CH), BF),
     dkv_s=((TOK, 768), BF),
     dkv_r=((TOK, 768), BF),
-    tmp=((3, TOK, 256), F32),
-    ysend=((2, NC, ZN, HALF, CH), BF),
-    yrecv=((2, NC, ZN, HALF, CH), BF),
-    zsend=((2, NC, ZN, HALF, CH), BF),
-    zrecv=((2, NC, ZN + 1, HALF, CH), BF),
+    tmp=((5, TOK, 256), F32),
+    ysend=((2, 2, NC, ZN, HR, RC), BF),
+    yrecv=((2, 2, NC, ZN, HR, RC), BF),
+    zsend=((2, 2, NC, ZN, HR, RC), BF),
+    zrecv=((2, 2, NC, ZN + 1, HR, RC), BF),
     hidden=((HALF, D), F32),
     ghid=((HALF, D), F32),
     rsum=((HALF, D), F32),
@@ -89,10 +93,10 @@
     g_s=(3, 8), g_r=(3, 8),
     wz_s=(NCH, 3), wz_r=(NCH, 3), wx_s=(NCH, 4), wx_r=(NCH, 4), wc_s=(NCH, 8), wc_r=(NCH, 8), wl=(NCH,),
     az_s=(4, AC, 2, ZN), az_r=(4, AC, ZN), ay_s=(4, AC, ZN), ay_r=(4, AC, ZN),
-    ry_s=(4, NC), ry_r=(4, NC), rz_s=(4, NC, ZN), rz_r=(4, NC, ZN + 1),
+    ry_s=(4, 2, NC), ry_r=(4, 2, NC), rz_s=(4, 2, NC, ZN), rz_r=(4, 2, NC, ZN + 1),
     kv_s=(2,), kv_r=(2,),
     gc_s=(NCH, 2), gc_r=(NCH, 2), gx_s=(NCH,), gx_r=(NCH,), gz_s=(NCH, 3), gz_r=(NCH, 3), gl=(NCH,),
-    v_s=(6,), v_r=(6,), o_s=(2,), o_r=(2,), ol=(4,),
+    v_s=(6,), v_r=(6,), o_s=(2, 2), o_r=(2, 2), ol=(1,), oo=(2, 2),
     credit=None,
 )
 NAMES = list(SCRATCH) + list(SEMS)
@@ -161,16 +165,14 @@
         w_x(n, 0, x).start()
         w_c(n, 0, c).start()
 
-    def pump_z(n):
-        for i in peers:
-            w_z(n, i).wait_recv()
-            w_x(n, i, x).start()
-            w_c(n, i, c).start()
-
-    def pump_x(n):
-        for j in range(ZN):
-            w_x(n, j, 1 - x).wait_recv()
-            w_c(n, ZN + j, c).start()
+    def pump_z(n, i):
+        w_z(n, i).wait_recv()
+        w_x(n, i, x).start()
+        w_c(n, i, c).start()
+
+    def pump_x(n, j):
+        w_x(n, j, 1 - x).wait_recv()
+        w_c(n, ZN + j, c).start()
 
     def w_fin(n):
         for j in range(8):
@@ -199,16 +201,19 @@
         pl.when((zz <= z) & (z < ZN - 1))(lambda: do(a_z(buf, ia, ch, zz, 0)))
         pl.when((zz >= z) & (z > 0))(lambda: do(a_z(buf, ia, ch, zz, 1)))
 
-    def ag_send(buf, ia, own):
-        def f(ch):
+    def ag_send(buf, ia, own, part):
+        def f(at):
+            ch = at + part * (AC // 2)
             ag_sends(buf, ia, ch, z, lambda copy: copy.start())
             if own:
                 a_y(buf, ia, ch, z, y).start()
 
-        loop(AC, f)
-
-    def ag_forward(buf, ia, d):
-        def f(ch):
+        loop(AC // 2, f)
+
+    def ag_forward(buf, ia, d, part):
+        def f(at):
+            ch = at + part * (AC // 2)
+
             def pass_on(zz):
                 a_z(buf, ia, ch, zz, 0).wait_recv()
                 ag_sends(buf, ia, ch, zz, lambda copy: copy.start())
@@ -217,14 +222,15 @@
             pl.when(z >= d)(lambda: pass_on(z - d))
             pl.when(z + d < ZN)(lambda: pass_on(z + d))
 
-        loop(AC, f)
-
-    def ag_wait(buf, ia, own):
-        def f(ch):
+        loop(AC // 2, f)
+
+    def ag_wait(buf, ia, own, part):
+        def f(at):
+            ch = at + part * (AC // 2)
             for i in range(0 if own else 1, ZN):
                 a_y(buf, ia, ch, zdn[i], 1 - y).wait_recv()
 
-        loop(AC, f)
+        loop(AC // 2, f)
 
     def ag_done(buf, ia, own):
         def f(ch):
@@ -235,79 +241,100 @@
 
         loop(AC, f)
 
-    def product(chunks, j, yy):
+    def group_rows(buf, g):
+        return jnp.concatenate([buf[zz, yy * HALF + g * HR : yy * HALF + g * HR + HR, :] for zz in range(ZN) for yy in range(2)], axis=0)
+
+    def product(chunks, j, yy, g):
         total = None
         for n in chunks:
-            rows = [YB[n, pl.ds(pl.multiple_of(zz * BLK + yy * HALF, HALF), HALF), :] for zz in range(ZN)]
+            rows = []
+            for zz in range(ZN):
+                at = (g * ZN + zz) * HALF + yy * HR if n > 3 else zz * BLK + yy * HALF + g * HR
+                rows.append(YB[n, pl.ds(pl.multiple_of(at, HR), HR), :])
             lhs = jnp.concatenate(rows, axis=0)
-            rhs = W[n, pl.ds(j * 4, 4)].reshape(CH, CH)
+            rhs = W[n, pl.ds(j * RB, RB)].reshape(RC, CH)
             part = nt(lhs, rhs)
             total = part if total is None else total + part
-        return total.reshape(ZN, HALF, CH)
-
-    def r_y(ir, b, j):
-        return remote(s.ysend.at[b, j], s.yrecv.at[b, j], s.ry_s.at[ir, j], s.ry_r.at[ir, j], ydev)
-
-    def r_z(ir, b, j, d, way):
+        return total.reshape(ZN, HR, RC)
+
+    def r_y(ir, b, g, j):
+        return remote(s.ysend.at[b, g, j], s.yrecv.at[b, g, j], s.ry_s.at[ir, g, j], s.ry_r.at[ir, g, j], ydev)
+
+    def r_z(ir, b, g, j, d, way):
         slot = d if way == 0 else jnp.where(d == z - 1, ZN, d)
         return remote(
-            s.zsend.at[b, j, d], s.zrecv.at[b, j, slot], s.rz_s.at[ir, j, d], s.rz_r.at[ir, j, slot], (updev, dndev)[way]
+            s.zsend.at[b, g, j, d],
+            s.zrecv.at[b, g, j, slot],
+            s.rz_s.at[ir, g, j, d],
+            s.rz_r.at[ir, g, j, slot],
+            (updev, dndev)[way],
         )
 
-    def r_arrived(ir, b, j, slot):
-        there = s.zrecv.at[b, j, slot]
-        remote(there, there, s.rz_s.at[ir, j, 0], s.rz_r.at[ir, j, slot], updev).wait_recv()
-
-    def rs_a(ir, b, chunks):
+    def r_arrived(ir, b, g, j, slot):
+        there = s.zrecv.at[b, g, j, slot]
+        remote(there, there, s.rz_s.at[ir, g, j, 0], s.rz_r.at[ir, g, j, slot], updev).wait_recv()
+
+    def rs_a(ir, b, chunks, g):
         def f(j):
-            s.ysend[b, j] = product(chunks, j, 1 - y).astype(BF)
-            r_y(ir, b, j).start()
+            s.ysend[b, g, j] = product(chunks, j, 1 - y, g).astype(BF)
+            r_y(ir, b, g, j).start()
 
         loop(NC, f)
 
-    def r_pass(ir, b, j, level):
+    def r_pass(ir, b, g, j, level):
         def go(dests, way):
             for d in dests:
                 if level > 0:
-                    r_arrived(ir, b, j, d)
-                    s.zsend[b, j, d] = (s.zsend[b, j, d].astype(F32) + s.zrecv[b, j, d].astype(F32)).astype(BF)
-                r_z(ir, b, j, d, way).start()
+                    r_arrived(ir, b, g, j, d)
+                    s.zsend[b, g, j, d] = (s.zsend[b, g, j, d].astype(F32) + s.zrecv[b, g, j, d].astype(F32)).astype(BF)
+                r_z(ir, b, g, j, d, way).start()
 
         pl.when(z == level)(lambda: go(range(ZN - 1, level, -1), 0))
         pl.when(z == ZN - 1 - level)(lambda: go(range(ZN - 1 - level), 1))
 
-    def rs_y(ir, b, chunks, j):
-        own = product(chunks, j, y)
-        r_y(ir, b, j).wait_recv()
-        s.zsend[b, j] = (own + s.yrecv[b, j].astype(F32)).astype(BF)
-        r_pass(ir, b, j, 0)
-
-    def rs_c(ir, b):
+    def rs_y(ir, b, chunks, g, j):
+        own = product(chunks, j, y, g)
+        r_y(ir, b, g, j).wait_recv()
+        s.zsend[b, g, j] = (own + s.yrecv[b, g, j].astype(F32)).astype(BF)
+        r_pass(ir, b, g, j, 0)
+
+    def rs_c(ir, b, g):
+        mine = pl.ds(g * HR, HR)
+
         def f(j):
-            cols = pl.ds(pl.multiple_of(j * CH, CH), CH)
-            s.rsum[:, cols] = s.zsend[b, j, z].astype(F32)
+            cols = pl.ds(pl.multiple_of(j * RC, RC), RC)
+            s.rsum[mine, cols] = s.zsend[b, g, j, z].astype(F32)
 
             def add(slot):
-                r_arrived(ir, b, j, slot)
-                s.rsum[:, cols] = s.rsum[:, cols] + s.zrecv[b, j, slot].astype(F32)
+                r_arrived(ir, b, g, j, slot)
+                s.rsum[mine, cols] = s.rsum[mine, cols] + s.zrecv[b, g, j, slot].astype(F32)
 
             pl.when(z > 0)(lambda: add(z))
             pl.when(z < ZN - 1)(lambda: add(ZN))
 
         loop(NC, f)
-
-    def rs_done(ir, b):
+        return s.rsum[mine, :]
+
+    def rs_done(ir, b, g):
         def f(j):
-            r_y(ir, b, j).wait_send()
+            r_y(ir, b, g, j).wait_send()
             for i in peers:
-                r_z(ir, b, j, zdn[i], 0).wait_send()
+                r_z(ir, b, g, j, zdn[i], 0).wait_send()
 
         loop(NC, f)
 
-    def transpose(buf):
+    def transpose(buf, grouped):
         def f(q):
             cols = pl.ds(pl.multiple_of(q * BLK, BLK), BLK)
-            XT[q] = buf[:, :, cols].reshape(TOK, BLK).T
+            if grouped:
+                parts = []
+                for g in range(2):
+                    for zz in range(ZN):
+                        for yy in range(2):
+                            parts.append(buf[zz, yy * HALF + g * HR : yy * HALF + g * HR + HR, cols])
+                XT[q] = jnp.concatenate(parts, axis=0).T
+            else:
+                XT[q] = buf[:, :, cols].reshape(TOK, BLK).T
 
         loop(16, f)
 
@@ -402,7 +429,8 @@
         keep = gap >= 0
         return jnp.where(keep, jnp.exp(jnp.where(keep, gap, 0).astype(F32) * log_rate), 0.0)
 
-    own_rows = pl.ds(pl.multiple_of(y * HALF, HALF), HALF)
+    def own_rows(g):
+        return pl.ds(pl.multiple_of(y * HALF + g * HR, HR), HR)
 
     gall = s.gall
     gall[me] = gp[...]
@@ -450,34 +478,59 @@
     def all_values():
         return qkv[:, :, 512:1024].reshape(2 * TOK, CH)
 
-    def out_copies(j, dst):
-        there = dst.at[own_rows]
+    def out_copies(j, g, dst):
+        here, there = s.ostage.at[j, pl.ds(g * HR, HR)], dst.at[own_rows(g)]
         return (
-            remote(s.ostage.at[j], there, s.o_s.at[j], s.o_r.at[j], ydev),
-            pltpu.make_async_copy(s.ostage.at[j], there, s.ol.at[1 + j]),
+            remote(here, there, s.o_s.at[j, g], s.o_r.at[j, g], ydev),
+            pltpu.make_async_copy(here, there, s.oo.at[j, g]),
         )
 
+    pump_z(0, 1)
     tokens = tok[...].astype(F32)
     n_first, _ = normed(tokens)
     s.first[z] = (n_first * gain_row(0)).astype(BF)
-    ag_send(s.first, 0, False)
-    ag_forward(s.first, 0, 1)
-    w_own(3)
+    for part in range(2):
+        ag_send(s.first, 0, False, part)
+    ag_forward(s.first, 0, 1, 0)
+    pump_z(0, 2)
+    w_own(6)
     w_own(1)
     w_own(0)
-    pump_z(0)
+    ag_forward(s.first, 0, 1, 1)
+    ag_forward(s.first, 0, 2, 0)
+    ag_forward(s.first, 0, 3, 0)
     w_send(3)
-    ag_forward(s.first, 0, 2)
+    pump_z(0, 3)
     w_send(1)
+    w_own(3)
     w_own(2)
-    pump_x(0)
-    pump_z(3)
+    w_own(4)
+    pump_x(0, 0)
+    pump_x(0, 1)
+    ag_forward(s.first, 0, 2, 1)
+    pump_z(3, 1)
     w_send(2)
-    ag_forward(s.first, 0, 3)
-    ag_wait(s.first, 0, False)
-    pump_z(1)
+    pump_z(3, 2)
+    pump_z(1, 1)
+    pump_z(1, 2)
+    pump_x(3, 0)
+    pump_x(3, 1)
+    pump_z(3, 3)
     cot_local.wait()
-    ag_send(s.cot, 1, False)
+    for part in range(2):
+        ag_send(s.cot, 1, False, part)
+    pump_x(1, 0)
+    pump_x(1, 1)
+    pump_x(0, 2)
+    pump_x(0, 3)
+    pump_z(1, 3)
+    w_send(5)
+    ag_forward(s.first, 0, 3, 1)
+    for part in range(2):
+        ag_wait(s.first, 0, False, part)
+    pump_z(2, 1)
+    w_send(4)
+    pump_z(2, 2)
     w_fin(0)
 
     def project_qk(t):
@@ -486,9 +539,8 @@
         qkv[c, :, pl.ds(pl.multiple_of(t * 256, 256), 256)] = out.astype(BF)
 
     loop(2, project_qk)
-    pump_x(1)
-    w_send(5)
-    pump_z(2)
+    pump_x(1, 2)
+    pump_x(1, 3)
     w_fin(1)
 
     def project_v(t):
@@ -502,8 +554,11 @@
         return remote(blk, blk, s.kv_s.at[0], s.kv_r.at[0], cdev)
 
     kv_copy(c).start()
-    w_own(4)
-    pump_x(3)
+    pump_z(2, 3)
+    ag_forward(s.cot, 1, 1, 0)
+    ag_forward(s.cot, 1, 1, 1)
+    pump_x(2, 0)
+    pump_x(2, 1)
     kv_copy(1 - c).wait_recv()
 
     def retain(h):
@@ -514,9 +569,11 @@
         s.ret[rows, :] = nn(scores.astype(BF), all_values())
 
     loop(2, retain)
-    pump_x(2)
+    pump_x(3, 2)
+    pump_x(3, 3)
     w_send(6)
-    ag_forward(s.cot, 1, 1)
+    pump_x(2, 2)
+    pump_x(2, 3)
     w_fin(2)
 
     def project_s(t):
@@ -532,129 +589,197 @@
 
     loop(ZN, gate)
     w_own(5)
-    w_own(6)
+    pump_z(5, 1)
     w_fin(3)
-    rs_a(0, 0, (3,))
-    w_send(4)
-    rs_y(0, 0, (3,), 0)
-    rs_y(0, 0, (3,), 1)
-    ag_forward(s.cot, 1, 2)
-    pump_z(6)
-    r_pass(0, 0, 0, 1)
-    r_pass(0, 0, 1, 1)
-    rs_y(0, 0, (3,), 2)
-    r_pass(0, 0, 2, 1)
-    r_pass(0, 0, 0, 2)
-    pump_z(4)
-    rs_y(0, 0, (3,), 3)
-    ag_forward(s.cot, 1, 3)
-    r_pass(0, 0, 3, 1)
-    r_pass(0, 0, 1, 2)
-    pump_z(5)
-    r_pass(0, 0, 2, 2)
-    r_pass(0, 0, 3, 2)
-    rs_c(0, 0)
-    hidden = tok[own_rows, :].astype(F32) + s.rsum[...]
-    s.hidden[...] = hidden
+    rs_a(0, 0, (3,), 0)
+    rs_y(0, 0, (3,), 0, 0)
+    rs_a(0, 0, (3,), 1)
+    pump_z(5, 2)
+    pump_z(5, 3)
+    pump_z(4, 1)
+    rs_y(0, 0, (3,), 0, 1)
+    ag_forward(s.cot, 1, 2, 0)
+    rs_y(0, 0, (3,), 1, 0)
+    r_pass(0, 0, 1, 0, 1)
+    rs_y(0, 0, (3,), 1, 1)
+    pump_z(6, 1)
+    ag_forward(s.cot, 1, 2, 1)
+    r_pass(0, 0, 1, 1, 1)
+    pump_z(4, 2)
+    pump_x(5, 0)
+    pump_x(5, 1)
+    ag_forward(s.cot, 1, 3, 0)
+    pump_z(6, 2)
+    pump_z(4, 3)
+    pump_x(6, 0)
+    pump_x(6, 1)
+    r_pass(0, 0, 0, 0, 1)
+    r_pass(0, 0, 1, 0, 2)
+    r_pass(0, 0, 1, 1, 2)
+    pump_x(5, 2)
+    pump_x(5, 3)
+    pump_x(4, 0)
+    pump_x(4, 1)
+    r_pass(0, 0, 0, 1, 1)
+    pump_z(6, 3)
+    r_pass(0, 0, 0, 0, 2)
+    ag_forward(s.cot, 1, 3, 1)
+    hidden = tok[own_rows(1), :].astype(F32) + rs_c(0, 0, 1)
+    s.hidden[32:64, :] = hidden
     n_second, _ = normed(hidden)
-    s.second[z, own_rows, :] = (n_second * gain_row(1)).astype(BF)
-    ag_send(s.second, 2, True)
-    ag_forward(s.second, 2, 1)
-    pump_x(6)
-    ag_wait(s.cot, 1, False)
-    ag_forward(s.second, 2, 2)
-    ag_forward(s.second, 2, 3)
-    pump_x(5)
-    pump_x(4)
-    ag_wait(s.second, 2, True)
-    for n in range(4, NCH):
-        w_fin(n)
-
-    def feed(t):
-        cols = pl.ds(pl.multiple_of(t * 256, 256), 256)
-        sec = s.second[...].reshape(TOK, D)
-        tmp[0] = nn(sec, columns(4, t))
-        tmp[1] = nn(sec, columns(5, t))
-        tmp[2] = nn(s.cot[...].reshape(TOK, D), columns(6, t))
-
-        def act(h):
-            rows = pl.ds(pl.multiple_of(h * HALF, HALF), HALF)
-            a, u, gm = tmp[0, rows, :], tmp[1, rows, :], tmp[2, rows, :]
-            root = 0.7978845608028654
-            th = jnp.tanh(root * (a + 0.044715 * (a * a * a)))
-            half = 0.5 * (1.0 + th)
-            gelu = a * half
-            slope = half + 0.5 * a * (1.0 - th * th) * (root * (1.0 + 0.134145 * (a * a)))
-            YB[6, rows, cols] = (gelu * u).astype(BF)
-            YB[4, rows, cols] = (gm * u * slope).astype(BF)
-            YB[5, rows, cols] = (gm * gelu).astype(BF)
-
-        loop(TOK // HALF, act)
-
-    loop(2, feed)
-    rs_done(0, 0)
-    rs_a(1, 0, (4, 5))
-    rs_y(1, 0, (4, 5), 0)
-    r_pass(1, 0, 0, 1)
-    transpose(s.second)
-    rs_a(2, 1, (6,))
-    rs_y(1, 0, (4, 5), 1)
+    s.second[z, own_rows(1), :] = (n_second * gain_row(1)).astype(BF)
+    ag_send(s.second, 2, True, 1)
+    r_pass(0, 0, 0, 1, 2)
+    ag_forward(s.second, 2, 1, 1)
+    hidden = tok[own_rows(0), :].astype(F32) + rs_c(0, 0, 0)
+    s.hidden[0:32, :] = hidden
+    n_second, _ = normed(hidden)
+    s.second[z, own_rows(0), :] = (n_second * gain_row(1)).astype(BF)
+    ag_send(s.second, 2, True, 0)
+    ag_forward(s.second, 2, 2, 1)
+    pump_x(6, 2)
+    pump_x(6, 3)
+    for part in range(2):
+        ag_wait(s.cot, 1, False, part)
+    ag_forward(s.second, 2, 1, 0)
+    ag_forward(s.second, 2, 3, 1)
+    pump_x(4, 2)
+    pump_x(4, 3)
+    w_fin(4)
+    w_fin(5)
+
+    def feed(g):
+        rows_g = pl.ds(g * 256, 256)
+
+        def tile(t):
+            sec = group_rows(s.second, g)
+            cols = pl.ds(pl.multiple_of(t * 256, 256), 256)
+            tmp[2 * t, rows_g, :] = nn(sec, columns(4, t))
+            tmp[2 * t + 1, rows_g, :] = nn(sec, columns(5, t))
+
+            def act(h):
+                rows = pl.ds(pl.multiple_of(g * 256 + h * HALF, HALF), HALF)
+                a, u = tmp[2 * t, rows, :], tmp[2 * t + 1, rows, :]
+                th = jnp.tanh(ROOT * (a + 0.044715 * (a * a * a)))
+                half = 0.5 * (1.0 + th)
+                gelu = a * half
+                slope = half + 0.5 * a * (1.0 - th * th) * (ROOT * (1.0 + 0.134145 * (a * a)))
+                YB[6, rows, cols] = (gelu * u).astype(BF)
+                tmp[2 * t, rows, :] = u * slope
+                tmp[2 * t + 1, rows, :] = gelu
+
+            loop(4, act)
+
+        loop(2, tile)
+
+    w_fin(6)
+
+    def feed_back(g):
+        rows_g = pl.ds(g * 256, 256)
+
+        def tile(t):
+            cols = pl.ds(pl.multiple_of(t * 256, 256), 256)
+            tmp[4, rows_g, :] = nn(group_rows(s.cot, g), columns(6, t))
+
+            def act(h):
+                rows = pl.ds(pl.multiple_of(g * 256 + h * HALF, HALF), HALF)
+                gm = tmp[4, rows, :]
+                YB[4, rows, cols] = (gm * tmp[2 * t, rows, :]).astype(BF)
+                YB[5, rows, cols] = (gm * tmp[2 * t + 1, rows, :]).astype(BF)
+
+            loop(4, act)
+
+        loop(2, tile)
+
+    ag_forward(s.second, 2, 2, 0)
+    ag_wait(s.second, 2, True, 1)
+    ag_forward(s.second, 2, 3, 0)
+    feed(1)
+    feed_back(1)
+    rs_done(0, 0, 1)
+    rs_a(1, 0, (4, 5), 1)
+    ag_wait(s.second, 2, True, 0)
+    feed(0)
+    transpose(s.second, True)
+    feed_back(0)
+    rs_done(0, 0, 0)
+    rs_a(1, 0, (4, 5), 0)
+    rs_y(1, 0, (4, 5), 1, 0)
+    grad_a(4, True)
+    r_pass(1, 0, 1, 0, 1)
+    rs_a(2, 1, (6,), 1)
+    rs_y(1, 0, (4, 5), 1, 1)
+    rs_y(1, 0, (4, 5), 0, 0)
+    r_pass(1, 0, 1, 1, 1)
+    r_pass(1, 0, 1, 0, 2)
     grad_a(5, True)
-    r_pass(1, 0, 1, 1)
-    rs_y(1, 0, (4, 5), 2)
-    r_pass(1, 0, 2, 1)
-    rs_y(1, 0, (4, 5), 3)
-    r_pass(1, 0, 0, 2)
-    r_pass(1, 0, 1, 2)
-    r_pass(1, 0, 3, 1)
-    r_pass(1, 0, 2, 2)
-    rs_y(2, 1, (6,), 0)
-    r_pass(1, 0, 3, 2)
-    rs_c(1, 0)
-    n_second, rstd = normed(s.hidden[...])
-    g_in = s.rsum[...]
-    vec[:, 256:512] = packed(jnp.sum(g_in * n_second, axis=0, keepdims=True))
-    ghid = s.cot[z, own_rows, :].astype(F32) + norm_back(n_second, rstd, g_in * gain_row(1))
-    s.ghid[...] = ghid
-    s.hlow[z, own_rows, :] = ghid.astype(BF)
-    ag_send(s.hlow, 3, True)
-    r_pass(2, 1, 0, 1)
-    grad_a(4, True)
-    transpose(s.cot)
-    rs_y(2, 1, (6,), 1)
+    r_pass(1, 0, 1, 1, 2)
+    r_pass(1, 0, 0, 0, 1)
+    rs_y(1, 0, (4, 5), 0, 1)
+    g_in = rs_c(1, 0, 1)
+    n_second, rstd = normed(s.hidden[32:64, :])
+    vec[:, 256:512] = vec[:, 256:512] + packed(jnp.sum(g_in * n_second, axis=0, keepdims=True))
+    ghid = s.cot[z, own_rows(1), :].astype(F32) + norm_back(n_second, rstd, g_in * gain_row(1))
+    s.ghid[32:64, :] = ghid
+    s.hlow[z, own_rows(1), :] = ghid.astype(BF)
+    ag_send(s.hlow, 3, True, 1)
+    r_pass(1, 0, 0, 0, 2)
+    r_pass(1, 0, 0, 1, 1)
+    rs_y(2, 1, (6,), 1, 0)
+    transpose(s.cot, True)
+    r_pass(1, 0, 0, 1, 2)
+    ag_forward(s.hlow, 3, 1, 1)
+    g_in = rs_c(1, 0, 0)
+    n_second, rstd = normed(s.hidden[0:32, :])
+    vec[:, 256:512] = vec[:, 256:512] + packed(jnp.sum(g_in * n_second, axis=0, keepdims=True))
+    ghid = s.cot[z, own_rows(0), :].astype(F32) + norm_back(n_second, rstd, g_in * gain_row(1))
+    s.ghid[0:32, :] = ghid
+    s.hlow[z, own_rows(0), :] = ghid.astype(BF)
+    ag_send(s.hlow, 3, True, 0)
+    rs_y(2, 1, (6,), 1, 1)
+    r_pass(2, 1, 1, 0, 1)
     grad_a(6, True)
-    ag_forward(s.hlow, 3, 1)
-    r_pass(2, 1, 1, 1)
-    ag_forward(s.hlow, 3, 2)
+    ag_forward(s.hlow, 3, 2, 1)
+    ag_forward(s.hlow, 3, 1, 0)
+    ag_forward(s.hlow, 3, 3, 1)
+    r_pass(2, 1, 1, 1, 1)
+    ag_forward(s.hlow, 3, 2, 0)
+    grad_b(5, True)
+    ag_forward(s.hlow, 3, 3, 0)
+    rs_a(2, 1, (6,), 0)
+    grad_b(6, True)
+    ag_wait(s.hlow, 3, True, 1)
+    ag_wait(s.hlow, 3, True, 0)
+    r_pass(2, 1, 1, 0, 2)
+    transpose(s.hlow, False)
+    grad_a(3, True)
+    rs_y(2, 1, (6,), 0, 0)
     grad_b(4, True)
-    ag_forward(s.hlow, 3, 3)
-    rs_y(2, 1, (6,), 2)
-    grad_b(5, True)
-    rs_y(2, 1, (6,), 3)
-    grad_b(6, True)
-    ag_wait(s.hlow, 3, True)
-    transpose(s.hlow)
-    grad_a(3, True)
-    def back_gated(t):
-        tmp[t] = nn(s.hlow[...].reshape(TOK, D), columns(3, t))
-
-    loop(2, back_gated)
-
-    def back_gate(h, total):
-        rows = pl.ds(pl.multiple_of(h * BLK, BLK), BLK)
-        n, rstd = normed(s.ret[rows, :])
-        w, g = swish[rows, :], jnp.concatenate([tmp[0, rows, :], tmp[1, rows, :]], axis=1)
-        sig = 1.0 / (1.0 + jnp.exp(-w))
-        silu = w * sig
-        YB[2, rows, :] = (g * (n * gain_g) * (sig * (1.0 + w * (1.0 - sig)))).astype(BF)
-        gs = g * silu
-        s.dr[rows, :] = norm_back(n, rstd, gs * gain_g).astype(BF)
-        return total + jnp.sum(gs * n, axis=0, keepdims=True)
-
-    group = lax.fori_loop(0, ZN, back_gate, jnp.zeros((1, CH), F32))
-    vec[0:4, 512:VW] = jnp.concatenate([group[:, 128 * q : 128 * q + 128] for q in range(4)], axis=0)
-
-    r_pass(2, 1, 0, 2)
+    def back_gated(g):
+        def tile(t):
+            out = nn(group_rows(s.hlow, g), columns(3, t))
+            for q in range(8):
+                tmp[t, q * HALF + g * HR : q * HALF + g * HR + HR, :] = out[q * HR : q * HR + HR]
+
+        loop(2, tile)
+
+        def back_gate(h, total):
+            rows = pl.ds(pl.multiple_of(h * HALF + g * HR, HR), HR)
+            n, rstd = normed(s.ret[rows, :])
+            w, g_out = swish[rows, :], jnp.concatenate([tmp[0, rows, :], tmp[1, rows, :]], axis=1)
+            sig = 1.0 / (1.0 + jnp.exp(-w))
+            silu = w * sig
+            YB[2, rows, :] = (g_out * (n * gain_g) * (sig * (1.0 + w * (1.0 - sig)))).astype(BF)
+            gs = g_out * silu
+            s.dr[rows, :] = norm_back(n, rstd, gs * gain_g).astype(BF)
+            return total + jnp.sum(gs * n, axis=0, keepdims=True)
+
+        group = lax.fori_loop(0, 8, back_gate, jnp.zeros((1, CH), F32))
+        vec[0:4, 512:VW] = vec[0:4, 512:VW] + jnp.concatenate([group[:, 128 * q : 128 * q + 128] for q in range(4)], axis=0)
+
+    back_gated(0)
+    transpose(s.first, False)
+    back_gated(1)
     def back_keys(core, h):
         rows = pl.ds(pl.multiple_of(h * 256, 256), 256)
         keys, values = qkv[core, rows, 256:512], qkv[core, rows, 512:1024]
@@ -682,6 +807,9 @@
     dkv_copy.start()
     loop(2, back_own)
 
+    r_pass(2, 1, 0, 0, 1)
+    grad_b(3, False)
+    r_pass(2, 1, 1, 1, 2)
     def back_query(h):
         rows = pl.ds(pl.multiple_of(h * 256, 256), 256)
         later = position((256, 2 * TOK), 0, False, h * 256)
@@ -701,48 +829,51 @@
 
     loop(ZN, back_sum)
 
-    grad_b(3, False)
-    transpose(s.first)
-    r_pass(2, 1, 2, 1)
-    rs_done(1, 0)
-    rs_a(3, 0, (0, 1, 2))
-    r_pass(2, 1, 3, 1)
+    rs_done(1, 0, 0)
+    rs_a(3, 0, (0, 1, 2), 0)
+    rs_done(1, 0, 1)
+    rs_a(3, 0, (0, 1, 2), 1)
+    rs_y(2, 1, (6,), 0, 1)
     grad_sent(5)
     grad_a(1, False)
-    rs_y(3, 0, (0, 1, 2), 0)
+    r_pass(2, 1, 0, 0, 2)
+    rs_y(3, 0, (0, 1, 2), 0, 0)
+    rs_y(3, 0, (0, 1, 2), 0, 1)
+    r_pass(3, 0, 0, 0, 1)
+    r_pass(2, 1, 0, 1, 1)
+    grad_b(1, False)
+    rs_y(3, 0, (0, 1, 2), 1, 0)
+    r_pass(2, 1, 0, 1, 2)
+    rs_y(3, 0, (0, 1, 2), 1, 1)
+    s.ostage[1, 32:64, :] = (s.hidden[32:64, :] + rs_c(2, 1, 1)).astype(BF)
+    for copy in out_copies(1, 1, res_o):
+        copy.start()
     grad_sent(4)
     grad_a(0, False)
-    rs_y(3, 0, (0, 1, 2), 1)
+    r_pass(3, 0, 0, 1, 1)
     grad_sent(6)
     grad_a(2, False)
-    r_pass(3, 0, 0, 1)
-    r_pass(3, 0, 1, 1)
-    r_pass(2, 1, 1, 2)
-    r_pass(3, 0, 0, 2)
-    r_pass(2, 1, 2, 2)
-    rs_y(3, 0, (0, 1, 2), 2)
-    r_pass(3, 0, 2, 1)
-    rs_y(3, 0, (0, 1, 2), 3)
-    r_pass(3, 0, 1, 2)
-    r_pass(2, 1, 3, 2)
-    rs_c(2, 1)
-    s.ostage[1] = (s.hidden[...] + s.rsum[...]).astype(BF)
-    for copy in out_copies(1, res_o):
+    r_pass(3, 0, 0, 0, 2)
+    r_pass(3, 0, 1, 0, 1)
+    r_pass(3, 0, 1, 1, 1)
+    s.ostage[1, 0:32, :] = (s.hidden[0:32, :] + rs_c(2, 1, 0)).astype(BF)
+    for copy in out_copies(1, 0, res_o):
         copy.start()
-    grad_b(1, False)
-    r_pass(3, 0, 3, 1)
-    r_pass(3, 0, 2, 2)
-    r_pass(3, 0, 3, 2)
-    rs_c(3, 0)
-    n_first, rstd = normed(tok[own_rows, :].astype(F32))
-    g_in = s.rsum[...]
-    vec[:, 0:256] = packed(jnp.sum(g_in * n_first, axis=0, keepdims=True))
-    g_tok = s.ghid[...] + norm_back(n_first, rstd, g_in * gain_row(0))
-    s.ostage[0] = g_tok.astype(BF)
-
-    for copy in out_copies(0, gtok_o):
-        copy.start()
+    r_pass(3, 0, 0, 1, 2)
+    r_pass(3, 0, 1, 0, 2)
+    g_in = rs_c(3, 0, 0)
+    n_first, rstd = normed(tok[own_rows(0), :].astype(F32))
+    vec[:, 0:256] = vec[:, 0:256] + packed(jnp.sum(g_in * n_first, axis=0, keepdims=True))
+    g_tok = s.ghid[0:32, :] + norm_back(n_first, rstd, g_in * gain_row(0))
+    s.ostage[0, 0:32, :] = g_tok.astype(BF)
     grad_b(0, False)
+    r_pass(3, 0, 1, 1, 2)
+    grad_b(2, False)
+    g_in = rs_c(3, 0, 1)
+    n_first, rstd = normed(tok[own_rows(1), :].astype(F32))
+    vec[:, 0:256] = vec[:, 0:256] + packed(jnp.sum(g_in * n_first, axis=0, keepdims=True))
+    g_tok = s.ghid[32:64, :] + norm_back(n_first, rstd, g_in * gain_row(0))
+    s.ostage[0, 32:64, :] = g_tok.astype(BF)
     def v_copy(j, dst, dev):
         return remote(vec, dst, s.v_s.at[j], s.v_r.at[j], dev)
 
@@ -753,7 +884,10 @@
     v_copy(1, s.vrx, xdev).wait()
     vec[...] = vec[...] + s.vrx[...]
     v_copy(2, s.vry, ydev).start()
-    grad_b(2, False)
+    for copy in out_copies(0, 0, gtok_o):
+        copy.start()
+    for copy in out_copies(0, 1, gtok_o):
+        copy.start()
     v_copy(2, s.vry, ydev).wait()
     vec[:, 0:512] = vec[:, 0:512] + s.vry[:, 0:512]
     vz = s.vz
@@ -769,11 +903,12 @@
     for zz in range(ZN):
         vec_o[:, 512 + 128 * zz : 640 + 128 * zz] = vz[zz, :, 512:VW]
     for j, dst in enumerate((gtok_o, res_o)):
-        there = dst.at[pl.ds(pl.multiple_of((1 - y) * HALF, HALF), HALF)]
-        a, b = out_copies(j, dst)
-        a.wait_send()
-        b.wait()
-        remote(s.ostage.at[j], there, s.o_s.at[j], s.o_r.at[j], ydev).wait_recv()
+        for g in range(2):
+            there = dst.at[pl.ds(pl.multiple_of((1 - y) * HALF + g * HR, HR), HR)]
+            a, b = out_copies(j, g, dst)
+            a.wait_send()
+            b.wait()
+            remote(there, there, s.o_s.at[j, g], s.o_r.at[j, g], ydev).wait_recv()
     for n in range(4):
         grad_sent(n)
     for n in range(NCH):
@@ -783,8 +918,9 @@
     dkv_copy.wait_send()
     for ia, (buf, own) in enumerate(((s.first, False), (s.cot, False), (s.second, True), (s.hlow, True))):
         ag_done(buf, ia, own)
-    rs_done(2, 1)
-    rs_done(3, 0)
+    for g in range(2):
+        rs_done(2, 1, g)
+        rs_done(3, 0, g)
 
 
 def finish_kernel(gwa, gwf, res, gtok, vec, o_res, o_tok, o_q, o_k, o_v, o_s, o_o, o_g, o_u, o_d, o_first, o_second, o_group):

time: 324 us -> 308 us (0.951)
  Pallas kernels: 322 us -> 306 us
    pallas_call x1, Pallas kernels: 314 us -> 298 us  [fused(): pl.pallas_call(kernel, out_shape=shapes, in_specs=[vmem, vmem, smem, hbm,...]
where the time goes in v4:
time: 308 us; the launch traced here: 307 us
  Pallas kernels  306 us (99%)
    pallas_call x1, Pallas kernels, fused(): pl.pallas_call(kernel, out_shape=shapes, in_specs=[vmem, vmem, smem, hbm,...  298 us

profile of v4, /device:TPU:0, one launch (start us, length us, event | category | flops | bytes accessed | tf_op | source)
XLA Modules:
  0.0 307.3 jit_solution(3327233168567041928)
XLA Ops:
  0.6 2.9 shard_map.237
  3.5 298.3 %shard_map.238 = (bf16[128,2048]{1,0:T(8,128)(2,1)}, bf16[128,2048]{1,0:T(8,128)(2,1)}, bf16[4,4,128,512]{3,2,1,0:T(8,128)(2,1)}, bf16[3,128,2048]{2,1,0:T(8,128)(2,1)}, f32[8,1024]{1,0:T(8,128)}) custom-call(bf16[128,2048]{1,0:T(8,128)(2,1)} %bitcast.8, f32[8,128]{1,0:T(8,128)} %get-tuple-element.34.gp, f32[4]{0:T(128)} %bitcast.10, ...), custom_call_target="tpu_custom_call" | custom-call | tf_op jit(solution)/shard_map/pallas_call | solution.py:1045
  301.8 5.3 %shard_map.239 = (f32[1,128,2048]{2,1,0:T(8,128)}, f32[1,128,2048]{2,1,0:T(8,128)}, f32[128,4,256]{2,1,0:T(4,128)}, f32[128,4,256]{2,1,0:T(4,128)}, f32[128,4,51...) custom-call(bf16[4,4,128,512]{3,2,1,0:T(8,128)(2,1)} %get-tuple-elem, ...), custom_call_target="tpu_custom_call" | custom-call | tf_op jit(solution)/shard_map/pallas_call | solution.py:968

commit v5 on v4

--- a/solution.py
+++ b/solution.py
@@ -485,52 +485,57 @@
             pltpu.make_async_copy(here, there, s.oo.at[j, g]),
         )
 
-    pump_z(0, 1)
+    w_own(4)
     tokens = tok[...].astype(F32)
     n_first, _ = normed(tokens)
     s.first[z] = (n_first * gain_row(0)).astype(BF)
     for part in range(2):
         ag_send(s.first, 0, False, part)
+    w_own(1)
+    w_own(6)
+    w_own(5)
+    w_own(2)
+    pump_z(0, 1)
     ag_forward(s.first, 0, 1, 0)
-    pump_z(0, 2)
-    w_own(6)
-    w_own(1)
+    w_send(1)
     w_own(0)
     ag_forward(s.first, 0, 1, 1)
     ag_forward(s.first, 0, 2, 0)
+    pump_z(1, 1)
+    pump_z(0, 2)
+    pump_x(0, 0)
+    pump_x(0, 1)
+    w_send(2)
+    pump_z(0, 3)
+    ag_forward(s.first, 0, 2, 1)
+    pump_x(0, 2)
+    pump_x(0, 3)
+    w_own(3)
     ag_forward(s.first, 0, 3, 0)
     w_send(3)
-    pump_z(0, 3)
-    w_send(1)
-    w_own(3)
-    w_own(2)
-    w_own(4)
-    pump_x(0, 0)
-    pump_x(0, 1)
-    ag_forward(s.first, 0, 2, 1)
-    pump_z(3, 1)
-    w_send(2)
-    pump_z(3, 2)
-    pump_z(1, 1)
+    pump_z(2, 1)
+    pump_z(2, 2)
+    pump_x(1, 0)
+    pump_x(1, 1)
+    pump_x(2, 0)
+    pump_x(2, 1)
     pump_z(1, 2)
-    pump_x(3, 0)
-    pump_x(3, 1)
-    pump_z(3, 3)
+    pump_z(1, 3)
     cot_local.wait()
     for part in range(2):
         ag_send(s.cot, 1, False, part)
-    pump_x(1, 0)
-    pump_x(1, 1)
-    pump_x(0, 2)
-    pump_x(0, 3)
-    pump_z(1, 3)
-    w_send(5)
     ag_forward(s.first, 0, 3, 1)
+    pump_z(2, 3)
+    pump_z(3, 1)
+    pump_z(3, 2)
+    pump_x(1, 2)
+    pump_x(1, 3)
+    w_send(6)
+    ag_forward(s.cot, 1, 1, 0)
     for part in range(2):
         ag_wait(s.first, 0, False, part)
-    pump_z(2, 1)
-    w_send(4)
-    pump_z(2, 2)
+    pump_x(2, 2)
+    pump_x(2, 3)
     w_fin(0)
 
     def project_qk(t):
@@ -539,8 +544,6 @@
         qkv[c, :, pl.ds(pl.multiple_of(t * 256, 256), 256)] = out.astype(BF)
 
     loop(2, project_qk)
-    pump_x(1, 2)
-    pump_x(1, 3)
     w_fin(1)
 
     def project_v(t):
@@ -554,11 +557,14 @@
         return remote(blk, blk, s.kv_s.at[0], s.kv_r.at[0], cdev)
 
     kv_copy(c).start()
-    pump_z(2, 3)
-    ag_forward(s.cot, 1, 1, 0)
-    ag_forward(s.cot, 1, 1, 1)
-    pump_x(2, 0)
-    pump_x(2, 1)
+    w_fin(2)
+
+    def project_s(t):
+        out = nn(s.first[...].reshape(TOK, D), columns(2, t))
+        swish[:, pl.ds(pl.multiple_of(t * 256, 256), 256)] = out
+
+    loop(2, project_s)
+    pump_z(3, 3)
     kv_copy(1 - c).wait_recv()
 
     def retain(h):
@@ -569,18 +575,13 @@
         s.ret[rows, :] = nn(scores.astype(BF), all_values())
 
     loop(2, retain)
+    ag_forward(s.cot, 1, 1, 1)
+    w_send(4)
+    pump_x(3, 0)
+    pump_x(3, 1)
     pump_x(3, 2)
     pump_x(3, 3)
-    w_send(6)
-    pump_x(2, 2)
-    pump_x(2, 3)
-    w_fin(2)
-
-    def project_s(t):
-        out = nn(s.first[...].reshape(TOK, D), columns(2, t))
-        swish[:, pl.ds(pl.multiple_of(t * 256, 256), 256)] = out
-
-    loop(2, project_s)
+    w_send(5)
     def gate(h):
         rows = pl.ds(pl.multiple_of(h * BLK, BLK), BLK)
         n, _ = normed(s.ret[rows, :])
@@ -588,63 +589,62 @@
         YB[3, rows, :] = (n * gain_g * (w / (1.0 + jnp.exp(-w)))).astype(BF)
 
     loop(ZN, gate)
-    w_own(5)
-    pump_z(5, 1)
+    pump_z(6, 1)
     w_fin(3)
     rs_a(0, 0, (3,), 0)
+    rs_a(0, 0, (3,), 1)
+    ag_forward(s.cot, 1, 2, 0)
+    pump_z(6, 2)
+    pump_z(6, 3)
+    pump_x(6, 0)
+    pump_x(6, 1)
     rs_y(0, 0, (3,), 0, 0)
-    rs_a(0, 0, (3,), 1)
+    ag_forward(s.cot, 1, 2, 1)
+    rs_y(0, 0, (3,), 0, 1)
+    r_pass(0, 0, 0, 0, 1)
+    r_pass(0, 0, 0, 1, 1)
+    pump_z(4, 1)
+    pump_z(4, 2)
+    rs_y(0, 0, (3,), 1, 0)
+    rs_y(0, 0, (3,), 1, 1)
+    ag_forward(s.cot, 1, 3, 0)
+    r_pass(0, 0, 1, 0, 1)
+    pump_z(4, 3)
+    ag_forward(s.cot, 1, 3, 1)
+    r_pass(0, 0, 0, 0, 2)
+    r_pass(0, 0, 0, 1, 2)
+    r_pass(0, 0, 1, 1, 1)
+    pump_z(5, 1)
+    hidden = tok[own_rows(0), :].astype(F32) + rs_c(0, 0, 0)
+    s.hidden[0:32, :] = hidden
+    n_second, _ = normed(hidden)
+    s.second[z, own_rows(0), :] = (n_second * gain_row(1)).astype(BF)
+    ag_send(s.second, 2, True, 0)
     pump_z(5, 2)
+    r_pass(0, 0, 1, 0, 2)
     pump_z(5, 3)
-    pump_z(4, 1)
-    rs_y(0, 0, (3,), 0, 1)
-    ag_forward(s.cot, 1, 2, 0)
-    rs_y(0, 0, (3,), 1, 0)
-    r_pass(0, 0, 1, 0, 1)
-    rs_y(0, 0, (3,), 1, 1)
-    pump_z(6, 1)
-    ag_forward(s.cot, 1, 2, 1)
-    r_pass(0, 0, 1, 1, 1)
-    pump_z(4, 2)
+    r_pass(0, 0, 1, 1, 2)
     pump_x(5, 0)
     pump_x(5, 1)
-    ag_forward(s.cot, 1, 3, 0)
-    pump_z(6, 2)
-    pump_z(4, 3)
-    pump_x(6, 0)
-    pump_x(6, 1)
-    r_pass(0, 0, 0, 0, 1)
-    r_pass(0, 0, 1, 0, 2)
-    r_pass(0, 0, 1, 1, 2)
-    pump_x(5, 2)
-    pump_x(5, 3)
     pump_x(4, 0)
     pump_x(4, 1)
-    r_pass(0, 0, 0, 1, 1)
-    pump_z(6, 3)
-    r_pass(0, 0, 0, 0, 2)
-    ag_forward(s.cot, 1, 3, 1)
+    pump_x(4, 2)
+    pump_x(4, 3)
+    for part in range(2):
+        ag_wait(s.cot, 1, False, part)
+    ag_forward(s.second, 2, 1, 0)
     hidden = tok[own_rows(1), :].astype(F32) + rs_c(0, 0, 1)
     s.hidden[32:64, :] = hidden
     n_second, _ = normed(hidden)
     s.second[z, own_rows(1), :] = (n_second * gain_row(1)).astype(BF)
     ag_send(s.second, 2, True, 1)
-    r_pass(0, 0, 0, 1, 2)
+    ag_forward(s.second, 2, 2, 0)
     ag_forward(s.second, 2, 1, 1)
-    hidden = tok[own_rows(0), :].astype(F32) + rs_c(0, 0, 0)
-    s.hidden[0:32, :] = hidden
-    n_second, _ = normed(hidden)
-    s.second[z, own_rows(0), :] = (n_second * gain_row(1)).astype(BF)
-    ag_send(s.second, 2, True, 0)
-    ag_forward(s.second, 2, 2, 1)
+    ag_forward(s.second, 2, 3, 0)
+    pump_x(5, 2)
+    pump_x(5, 3)
     pump_x(6, 2)
     pump_x(6, 3)
-    for part in range(2):
-        ag_wait(s.cot, 1, False, part)
-    ag_forward(s.second, 2, 1, 0)
-    ag_forward(s.second, 2, 3, 1)
-    pump_x(4, 2)
-    pump_x(4, 3)
     w_fin(4)
     w_fin(5)
 
@@ -672,6 +672,7 @@
 
         loop(2, tile)
 
+    ag_forward(s.second, 2, 2, 1)
     w_fin(6)
 
     def feed_back(g):
@@ -691,31 +692,43 @@
 
         loop(2, tile)
 
-    ag_forward(s.second, 2, 2, 0)
-    ag_wait(s.second, 2, True, 1)
-    ag_forward(s.second, 2, 3, 0)
-    feed(1)
-    feed_back(1)
-    rs_done(0, 0, 1)
-    rs_a(1, 0, (4, 5), 1)
     ag_wait(s.second, 2, True, 0)
+    ag_forward(s.second, 2, 3, 1)
     feed(0)
-    transpose(s.second, True)
     feed_back(0)
     rs_done(0, 0, 0)
     rs_a(1, 0, (4, 5), 0)
+    ag_wait(s.second, 2, True, 1)
+    feed(1)
+    transpose(s.second, True)
+    feed_back(1)
+    grad_a(4, True)
+    rs_y(1, 0, (4, 5), 0, 0)
+    rs_done(0, 0, 1)
+    rs_a(1, 0, (4, 5), 1)
+    rs_y(1, 0, (4, 5), 0, 1)
+    r_pass(1, 0, 0, 0, 1)
+    rs_a(2, 1, (6,), 1)
+    grad_a(5, True)
+    r_pass(1, 0, 0, 0, 2)
     rs_y(1, 0, (4, 5), 1, 0)
-    grad_a(4, True)
+    r_pass(1, 0, 0, 1, 1)
+    r_pass(1, 0, 0, 1, 2)
     r_pass(1, 0, 1, 0, 1)
-    rs_a(2, 1, (6,), 1)
     rs_y(1, 0, (4, 5), 1, 1)
-    rs_y(1, 0, (4, 5), 0, 0)
+    g_in = rs_c(1, 0, 0)
+    n_second, rstd = normed(s.hidden[0:32, :])
+    vec[:, 256:512] = vec[:, 256:512] + packed(jnp.sum(g_in * n_second, axis=0, keepdims=True))
+    ghid = s.cot[z, own_rows(0), :].astype(F32) + norm_back(n_second, rstd, g_in * gain_row(1))
+    s.ghid[0:32, :] = ghid
+    s.hlow[z, own_rows(0), :] = ghid.astype(BF)
+    ag_send(s.hlow, 3, True, 0)
+    transpose(s.cot, True)
+    r_pass(1, 0, 1, 0, 2)
     r_pass(1, 0, 1, 1, 1)
-    r_pass(1, 0, 1, 0, 2)
-    grad_a(5, True)
+    rs_y(2, 1, (6,), 1, 0)
     r_pass(1, 0, 1, 1, 2)
-    r_pass(1, 0, 0, 0, 1)
-    rs_y(1, 0, (4, 5), 0, 1)
+    ag_forward(s.hlow, 3, 1, 0)
     g_in = rs_c(1, 0, 1)
     n_second, rstd = normed(s.hidden[32:64, :])
     vec[:, 256:512] = vec[:, 256:512] + packed(jnp.sum(g_in * n_second, axis=0, keepdims=True))
@@ -723,38 +736,19 @@
     s.ghid[32:64, :] = ghid
     s.hlow[z, own_rows(1), :] = ghid.astype(BF)
     ag_send(s.hlow, 3, True, 1)
-    r_pass(1, 0, 0, 0, 2)
-    r_pass(1, 0, 0, 1, 1)
-    rs_y(2, 1, (6,), 1, 0)
-    transpose(s.cot, True)
-    r_pass(1, 0, 0, 1, 2)
+    r_pass(2, 1, 1, 0, 1)
+    rs_y(2, 1, (6,), 1, 1)
+    grad_a(6, True)
+    ag_forward(s.hlow, 3, 2, 0)
     ag_forward(s.hlow, 3, 1, 1)
-    g_in = rs_c(1, 0, 0)
-    n_second, rstd = normed(s.hidden[0:32, :])
-    vec[:, 256:512] = vec[:, 256:512] + packed(jnp.sum(g_in * n_second, axis=0, keepdims=True))
-    ghid = s.cot[z, own_rows(0), :].astype(F32) + norm_back(n_second, rstd, g_in * gain_row(1))
-    s.ghid[0:32, :] = ghid
-    s.hlow[z, own_rows(0), :] = ghid.astype(BF)
-    ag_send(s.hlow, 3, True, 0)
-    rs_y(2, 1, (6,), 1, 1)
-    r_pass(2, 1, 1, 0, 1)
-    grad_a(6, True)
+    r_pass(2, 1, 1, 1, 1)
     ag_forward(s.hlow, 3, 2, 1)
-    ag_forward(s.hlow, 3, 1, 0)
-    ag_forward(s.hlow, 3, 3, 1)
-    r_pass(2, 1, 1, 1, 1)
-    ag_forward(s.hlow, 3, 2, 0)
     grad_b(5, True)
     ag_forward(s.hlow, 3, 3, 0)
+    grad_b(6, True)
+    ag_forward(s.hlow, 3, 3, 1)
+    ag_wait(s.hlow, 3, True, 0)
     rs_a(2, 1, (6,), 0)
-    grad_b(6, True)
-    ag_wait(s.hlow, 3, True, 1)
-    ag_wait(s.hlow, 3, True, 0)
-    r_pass(2, 1, 1, 0, 2)
-    transpose(s.hlow, False)
-    grad_a(3, True)
-    rs_y(2, 1, (6,), 0, 0)
-    grad_b(4, True)
     def back_gated(g):
         def tile(t):
             out = nn(group_rows(s.hlow, g), columns(3, t))
@@ -778,8 +772,13 @@
         vec[0:4, 512:VW] = vec[0:4, 512:VW] + jnp.concatenate([group[:, 128 * q : 128 * q + 128] for q in range(4)], axis=0)
 
     back_gated(0)
+    grad_b(4, True)
+    ag_wait(s.hlow, 3, True, 1)
+    transpose(s.hlow, False)
+    grad_a(3, True)
+    rs_y(2, 1, (6,), 0, 0)
+    back_gated(1)
     transpose(s.first, False)
-    back_gated(1)
     def back_keys(core, h):
         rows = pl.ds(pl.multiple_of(h * 256, 256), 256)
         keys, values = qkv[core, rows, 256:512], qkv[core, rows, 512:1024]
@@ -808,8 +807,6 @@
     loop(2, back_own)
 
     r_pass(2, 1, 0, 0, 1)
-    grad_b(3, False)
-    r_pass(2, 1, 1, 1, 2)
     def back_query(h):
         rows = pl.ds(pl.multiple_of(h * 256, 256), 256)
         later = position((256, 2 * TOK), 0, False, h * 256)
@@ -831,69 +828,72 @@
 
     rs_done(1, 0, 0)
     rs_a(3, 0, (0, 1, 2), 0)
+    grad_b(3, False)
+    grad_sent(6)
+    grad_a(2, False)
+    grad_sent(5)
+    grad_a(1, False)
+    rs_y(3, 0, (0, 1, 2), 0, 0)
+    r_pass(3, 0, 0, 0, 1)
+    rs_y(3, 0, (0, 1, 2), 0, 1)
+    r_pass(3, 0, 0, 1, 1)
+    r_pass(2, 1, 0, 0, 2)
     rs_done(1, 0, 1)
     rs_a(3, 0, (0, 1, 2), 1)
-    rs_y(2, 1, (6,), 0, 1)
-    grad_sent(5)
-    grad_a(1, False)
-    r_pass(2, 1, 0, 0, 2)
-    rs_y(3, 0, (0, 1, 2), 0, 0)
-    rs_y(3, 0, (0, 1, 2), 0, 1)
-    r_pass(3, 0, 0, 0, 1)
-    r_pass(2, 1, 0, 1, 1)
-    grad_b(1, False)
+    r_pass(2, 1, 1, 0, 2)
+    grad_b(2, False)
+    r_pass(2, 1, 1, 1, 2)
     rs_y(3, 0, (0, 1, 2), 1, 0)
-    r_pass(2, 1, 0, 1, 2)
-    rs_y(3, 0, (0, 1, 2), 1, 1)
-    s.ostage[1, 32:64, :] = (s.hidden[32:64, :] + rs_c(2, 1, 1)).astype(BF)
-    for copy in out_copies(1, 1, res_o):
-        copy.start()
+    r_pass(3, 0, 1, 0, 1)
     grad_sent(4)
     grad_a(0, False)
-    r_pass(3, 0, 0, 1, 1)
-    grad_sent(6)
-    grad_a(2, False)
+    rs_y(3, 0, (0, 1, 2), 1, 1)
+    rs_y(2, 1, (6,), 0, 1)
     r_pass(3, 0, 0, 0, 2)
-    r_pass(3, 0, 1, 0, 1)
     r_pass(3, 0, 1, 1, 1)
-    s.ostage[1, 0:32, :] = (s.hidden[0:32, :] + rs_c(2, 1, 0)).astype(BF)
-    for copy in out_copies(1, 0, res_o):
-        copy.start()
     r_pass(3, 0, 0, 1, 2)
-    r_pass(3, 0, 1, 0, 2)
     g_in = rs_c(3, 0, 0)
     n_first, rstd = normed(tok[own_rows(0), :].astype(F32))
     vec[:, 0:256] = vec[:, 0:256] + packed(jnp.sum(g_in * n_first, axis=0, keepdims=True))
     g_tok = s.ghid[0:32, :] + norm_back(n_first, rstd, g_in * gain_row(0))
     s.ostage[0, 0:32, :] = g_tok.astype(BF)
-    grad_b(0, False)
+    r_pass(2, 1, 0, 1, 1)
+    r_pass(3, 0, 1, 0, 2)
     r_pass(3, 0, 1, 1, 2)
-    grad_b(2, False)
+    s.ostage[1, 32:64, :] = (s.hidden[32:64, :] + rs_c(2, 1, 1)).astype(BF)
+    for copy in out_copies(1, 1, res_o):
+        copy.start()
+    grad_b(1, False)
+    r_pass(2, 1, 0, 1, 2)
     g_in = rs_c(3, 0, 1)
     n_first, rstd = normed(tok[own_rows(1), :].astype(F32))
     vec[:, 0:256] = vec[:, 0:256] + packed(jnp.sum(g_in * n_first, axis=0, keepdims=True))
     g_tok = s.ghid[32:64, :] + norm_back(n_first, rstd, g_in * gain_row(0))
     s.ostage[0, 32:64, :] = g_tok.astype(BF)
+    grad_b(0, False)
+    for copy in out_copies(0, 0, gtok_o):
+        copy.start()
     def v_copy(j, dst, dev):
         return remote(vec, dst, s.v_s.at[j], s.v_r.at[j], dev)
 
     v_copy(0, s.vrc, cdev).start()
+    for copy in out_copies(0, 1, gtok_o):
+        copy.start()
     v_copy(0, s.vrc, cdev).wait()
     vec[...] = vec[...] + s.vrc[...]
     v_copy(1, s.vrx, xdev).start()
     v_copy(1, s.vrx, xdev).wait()
     vec[...] = vec[...] + s.vrx[...]
     v_copy(2, s.vry, ydev).start()
-    for copy in out_copies(0, 0, gtok_o):
-        copy.start()
-    for copy in out_copies(0, 1, gtok_o):
-        copy.start()
     v_copy(2, s.vry, ydev).wait()
     vec[:, 0:512] = vec[:, 0:512] + s.vry[:, 0:512]
     vz = s.vz
     vz[z] = vec[...]
     for i in peers:
         v_copy(2 + i, vz.at[z], zdev[i]).start()
+    s.ostage[1, 0:32, :] = (s.hidden[0:32, :] + rs_c(2, 1, 0)).astype(BF)
+    for copy in out_copies(1, 0, res_o):
+        copy.start()
     for i in peers:
         there = vz.at[zdn[i]]
         remote(there, there, s.v_s.at[2 + i], s.v_r.at[2 + i], zdev[i]).wait_recv()

time: 308 us -> 307 us (level)
  no operation moved by 1% of the time
where the time goes in v5:
time: 307 us
  Pallas kernels  306 us (100%)
    pallas_call x1, Pallas kernels, fused(): pl.pallas_call(kernel, out_shape=shapes, in_specs=[vmem, vmem, smem, hbm,...  298 us

profile of v5, /device:TPU:0, one launch (start us, length us, event | category | flops | bytes accessed | tf_op | source)
XLA Modules:
  0.0 306.6 jit_solution(1548316886357166764)
XLA Ops:
  0.6 2.9 shard_map.237
  3.5 297.6 %shard_map.238 = (bf16[128,2048]{1,0:T(8,128)(2,1)}, bf16[128,2048]{1,0:T(8,128)(2,1)}, bf16[4,4,128,512]{3,2,1,0:T(8,128)(2,1)}, bf16[3,128,2048]{2,1,0:T(8,128)(2,1)}, f32[8,1024]{1,0:T(8,128)}) custom-call(bf16[128,2048]{1,0:T(8,128)(2,1)} %bitcast.8, f32[8,128]{1,0:T(8,128)} %get-tuple-element.34.gp, f32[4]{0:T(128)} %bitcast.10, ...), custom_call_target="tpu_custom_call" | custom-call | tf_op jit(solution)/shard_map/pallas_call | solution.py:1045
  301.2 5.3 %shard_map.239 = (f32[1,128,2048]{2,1,0:T(8,128)}, f32[1,128,2048]{2,1,0:T(8,128)}, f32[128,4,256]{2,1,0:T(4,128)}, f32[128,4,256]{2,1,0:T(4,128)}, f32[128,4,51...) custom-call(bf16[4,4,128,512]{3,2,1,0:T(8,128)(2,1)} %get-tuple-elem, ...), custom_call_target="tpu_custom_call" | custom-call | tf_op jit(solution)/shard_map/pallas_call | solution.py:968

commit v6 on v5

--- a/solution.py
+++ b/solution.py
@@ -445,6 +445,8 @@
         w_local(n, z).start()
     cot_local = pltpu.make_async_copy(cot_in, s.cot.at[z], s.ol.at[0])
     cot_local.start()
+    s.rsum[...], _ = normed(tok[pl.ds(pl.multiple_of(y * HALF, HALF), HALF), :].astype(F32))
+    s.ghid[...], _ = normed(tok[pl.ds(pl.multiple_of((1 - y) * HALF, HALF), HALF), :].astype(F32))
     for i in peers:
         g_gain(0, i, zdev[i], place(x, zdn[i], c)).wait_recv()
     for i in range(ZN):
@@ -466,7 +468,6 @@
         g_gain(2, i, cdev, place(xx, zdn[i % ZN], c)).wait_send()
     vec = s.vec
     vec[...] = jnp.zeros((8, VW), F32)
-    gain_g = group_gain()
     tmp, qkv, swish = s.tmp, s.qkv, s.swish
 
     def columns(n, t):
@@ -486,11 +487,11 @@
         )
 
     w_own(4)
-    tokens = tok[...].astype(F32)
-    n_first, _ = normed(tokens)
-    s.first[z] = (n_first * gain_row(0)).astype(BF)
+    gain_1 = gain_row(0)
+    s.first[z, pl.ds(pl.multiple_of(y * HALF, HALF), HALF), :] = (s.rsum[...] * gain_1).astype(BF)
     for part in range(2):
         ag_send(s.first, 0, False, part)
+    s.first[z, pl.ds(pl.multiple_of((1 - y) * HALF, HALF), HALF), :] = (s.ghid[...] * gain_1).astype(BF)
     w_own(1)
     w_own(6)
     w_own(5)
@@ -582,6 +583,8 @@
     pump_x(3, 2)
     pump_x(3, 3)
     w_send(5)
+    gain_g = group_gain()
+
     def gate(h):
         rows = pl.ds(pl.multiple_of(h * BLK, BLK), BLK)
         n, _ = normed(s.ret[rows, :])

time: 307 us -> 307 us (level)
  no operation moved by 1% of the time
where the time goes in v6:
time: 307 us; the launch traced here: 306 us
  Pallas kernels  306 us (100%)
    pallas_call x1, Pallas kernels, fused(): pl.pallas_call(kernel, out_shape=shapes, in_specs=[vmem, vmem, smem, hbm,...  297 us

profile of v6, /device:TPU:0, one launch (start us, length us, event | category | flops | bytes accessed | tf_op | source)
XLA Modules:
  0.0 306.5 jit_solution(9060280761563289284)
XLA Ops:
  0.6 2.9 shard_map.237
  3.5 297.4 %shard_map.238 = (bf16[128,2048]{1,0:T(8,128)(2,1)}, bf16[128,2048]{1,0:T(8,128)(2,1)}, bf16[4,4,128,512]{3,2,1,0:T(8,128)(2,1)}, bf16[3,128,2048]{2,1,0:T(8,128)(2,1)}, f32[8,1024]{1,0:T(8,128)}) custom-call(bf16[128,2048]{1,0:T(8,128)(2,1)} %bitcast.8, f32[8,128]{1,0:T(8,128)} %get-tuple-element.34.gp, f32[4]{0:T(128)} %bitcast.10, ...), custom_call_target="tpu_custom_call" | custom-call | tf_op jit(solution)/shard_map/pallas_call | solution.py:1048
  301.0 5.3 %shard_map.239 = (f32[1,128,2048]{2,1,0:T(8,128)}, f32[1,128,2048]{2,1,0:T(8,128)}, f32[128,4,256]{2,1,0:T(4,128)}, f32[128,4,256]{2,1,0:T(4,128)}, f32[128,4,51...) custom-call(bf16[4,4,128,512]{3,2,1,0:T(8,128)(2,1)} %get-tuple-elem, ...), custom_call_target="tpu_custom_call" | custom-call | tf_op jit(solution)/shard_map/pallas_call | solution.py:971
